TPU v7x, 32 devices: a whole 2x2x4 slice. The times are simulated.
32 devices in a mesh: leaf: 32 (over z, y, x, core).
Axes of the slice: x: 2, y: 2, z: 4, core: 2. Of those that a mesh axis runs over, the one named last changes fastest.
Arguments:
- points: bfloat16 [64, 131072], P(None, 'leaf'), may hold values from -3 to 3
- charges: bfloat16 [16, 131072], P(None, 'leaf'), may hold values from -6 to 6
- leaf_order: int32 [131072], P('leaf'), may hold values from 0 to 4095, as said below
- near_owner: int32 [512, 8], P('leaf'), may hold values from 0 to 31, all different within a row; in each aligned block of 16 rows (0 to 15, 16 to 31, ...) at most 6 rows name the same one
- near_slot: int32 [512, 8], P('leaf'), may hold values from 0 to 15
- far_list: int32 [512, 16], P('leaf'), may hold values from 0 to 30
- far_count: int32 [512], P('leaf'), may hold values from 1 to 16
- leaf_interp: bfloat16 [512, 256, 128], P('leaf'), may hold values from -0.375 to 0.375
- leaf_skel: int32 [512, 128], P('leaf'), may hold values from 0 to 255, as said below
- inner_interp: bfloat16 [480, 256, 128], P('leaf'), may hold values from -0.375 to 0.375
- inner_skel: int32 [480, 128], P('leaf'), may hold values from 0 to 255, as said below
- top_interp: bfloat16 [30, 256, 128], replicated, may hold values from -0.375 to 0.375
- top_skel: int32 [30, 128], replicated, may hold values from 0 to 255, as said below
Outputs:
- potential: float32 [16, 131072], P(None, 'leaf')
Inputs may be any that keep to these rules, and one draw needn't show every extreme that they name: `leaf_order`: each device's 4096 entries are a permutation of its point numbers. `near_owner`: a row names 8 different devices; over the rows of one device, no device is named more than 6 times. `leaf_skel`: the entries of a row are different. `inner_skel`: the entries of a row are different. `top_skel`: the entries of a row are different.
All inputs are finite; a program needn't handle non-finite values.
Results may differ from a plain program's by a relative error of at most 0.008.
Values may be sent and summed in bfloat16 or wider, within the bound.
No kernel may reach another device: no remote copies, remote signals or barrier semaphores. Data moves between devices by JAX's collectives and lax.ppermute only.
A program may use at most 128 MiB of HBM per device.

v0:
```python
import functools

import jax
import jax.numpy as jnp
from jax import lax
from jax.experimental import pallas as pl
from jax.experimental.pallas import tpu as pltpu
from jax.sharding import PartitionSpec as P

TARGET_BITS = (1, 3)
FAR_UNROLL = 8
NEAR_STEPS = (8, 4, 2)
DUMMY = 1 << 30
PHASE_BIT = 24
CODE = (1 << PHASE_BIT) - 1
VMEM_LIMIT = 24 * 1024 * 1024
FIRST_LIMIT = 58 * 1024 * 1024
PHASES = 3
bf16 = jnp.bfloat16
f32 = jnp.float32

VMEM = pl.BlockSpec(memory_space=pltpu.VMEM)
SMEM = pl.BlockSpec(memory_space=pltpu.SMEM)
ANY = pl.BlockSpec(memory_space=pl.ANY)
HBM = pl.BlockSpec(memory_space=pltpu.HBM)


def params(limit=VMEM_LIMIT):
    return pltpu.CompilerParams(vmem_limit_bytes=limit)


def cost():
    return pl.CostEstimate(flops=1, bytes_accessed=1, transcendentals=0)


def dot(a, b):
    return lax.dot_general(a, b, (((1,), (0,)), ((), ())), preferred_element_type=f32)


def dot_nt(a, b):
    return lax.dot_general(a, b, (((1,), (1,)), ((), ())), preferred_element_type=f32)


def split3(value):
    hi = value.astype(bf16).astype(f32)
    rest = value - hi
    mid = rest.astype(bf16).astype(f32)
    return hi, mid, rest - mid


def norm_row(coords):
    wide = coords.astype(f32)
    return jnp.sum(wide * wide, axis=0, keepdims=True) * 0.125


def extra_rows(norms, first):
    hi, mid, lo = split3(-norms)
    row = lax.broadcasted_iota(jnp.int32, (16, norms.shape[1]), 0)
    one_at = 3 - first
    out = jnp.where((row >= one_at) & (row < one_at + 3), 1.0, 0.0)
    out = jnp.where(row == first, hi, out)
    out = jnp.where(row == first + 1, mid, out)
    return jnp.where(row == first + 2, lo, out)


def source_matrix(coords, norms):
    width = coords.shape[1]
    extra = extra_rows(norms, 0).astype(bf16)
    return jnp.concatenate([coords, extra, jnp.zeros((48, width), bf16)], axis=0)


def target_matrix(coords, norms):
    width = coords.shape[1]
    extra = extra_rows(norms, 3)
    wide = jnp.concatenate(
        [coords.astype(f32) * 0.25, extra, jnp.zeros((48, width), f32)], axis=0
    )
    return jnp.transpose(wide).astype(bf16)


def placed(loads, place):
    zero = jnp.zeros_like(loads)
    return jnp.concatenate(
        [jnp.where(place == k, loads, zero) for k in range(8)], axis=0
    )


def onehot(picks, size):
    row = lax.broadcasted_iota(jnp.int32, (size, picks.shape[1]), 0)
    return jnp.where(row == picks, 1.0, 0.0).astype(bf16)


def combine(left, right, picks, interp):
    both = jnp.concatenate([left, right], axis=1)
    coords = dot(both[:64], onehot(picks, 256)).astype(bf16)
    load = dot(both[64:], interp).astype(bf16)
    return jnp.concatenate([coords, load], axis=0)


def first_kernel(
    order, points_in, charges_in, owner_in, slot_in,
    leaf_interp_in, leaf_skel_in, inner_interp_in, inner_skel_in, top_interp, top_skel,
    src_out, tgt_out, cols_out, loads_out, rows_out, norms_out, mine_out, interps_out, skels_out,
    points, charges, owner, slot, unsorted, buffer0, buffer1, src, tgt, cols, loads, rows, norms,
    joined, root, leaf_interp, leaf_skel, inner_interp, inner_skel, sems,
):
    count = points.shape[1]
    chunks = 4
    width = count // chunks
    begun = []

    def begin(a, b):
        copy = pltpu.make_async_copy(a, b, sems.at[len(begun)])
        copy.start()
        begun.append(copy)
        return copy

    parts = [begin(charges_in, charges)]
    for c in range(chunks):
        at = pl.ds(c * width, width)
        parts.append(begin(points_in.at[:, at], points.at[:, at]))
    near_lists = [begin(owner_in, owner), begin(slot_in, slot)]
    needed = [
        begin(leaf_skel_in, leaf_skel),
        begin(leaf_interp_in, leaf_interp),
        begin(inner_skel_in, inner_skel),
        begin(inner_interp_in, inner_interp),
    ]
    rest = []
    path = path_rows()
    for k in range(interps_out.shape[0]):
        rest.append(begin(top_interp.at[path[k]], interps_out.at[k]))
        rest.append(begin(top_skel.at[pl.ds(path[k], 1)], skels_out.at[k]))

    parts[0].wait()
    for c in range(count // 128):
        at = slice(c * 128, (c + 1) * 128)
        if c * 128 % width == 0:
            parts[1 + c * 128 // width].wait()
        block = jnp.concatenate(
            [
                points[:, at].astype(f32),
                charges[:, at].astype(f32),
                jnp.zeros((48, 128), f32),
            ],
            axis=0,
        )
        unsorted[at, :] = jnp.transpose(block)

    leaves = src.shape[0]
    first_node = 2 * leaves
    lane = lax.broadcasted_iota(jnp.int32, (256, 128), 1)

    def finish(node, both):
        joined[node] = both
        cols[first_node + node] = source_matrix(both[:64], norm_row(both[:64]))
        loads[first_node + node] = both[64:]

    def copy_rows(pair, buffer):
        base = pl.multiple_of(pair * 512, 512)
        for u in range(512):
            buffer[u : u + 1, :] = unsorted[pl.ds(order[base + u], 1), :]

    def process(pair, buffer):
        even = buffer[:256]
        odd = buffer[256:]
        both = jnp.where(lane < 64, even, pltpu.roll(odd, 64, 1))
        tgt[pl.ds(pl.multiple_of(pair * 256, 256), 256), :] = (both * 0.25).astype(bf16)
        for k, mine in enumerate((even, odd)):
            i = 2 * pair + k
            both = jnp.transpose(mine)[:80].astype(bf16)
            src[i] = both
            coords, load = both[:64], both[64:]
            norm = norm_row(coords)
            norms[i] = norm
            rows[i] = target_matrix(coords, norm)
            matrix = source_matrix(coords, norm)
            for half in range(2):
                cols[2 * i + half] = matrix[:, half * 128 : half * 128 + 128]
                loads[2 * i + half] = load[:, half * 128 : half * 128 + 128]
            picked = dot(coords, onehot(leaf_skel[pl.ds(i, 1), :], 256)).astype(bf16)
            value = dot(load, leaf_interp[i]).astype(bf16)
            finish(i, jnp.concatenate([picked, value], axis=0))

    for copy in needed:
        copy.wait()

    def two_pairs(i, carry):
        copy_rows(2 * i, buffer0)
        process(jnp.maximum(2 * i - 1, 0), buffer1)
        copy_rows(2 * i + 1, buffer1)
        process(2 * i, buffer0)
        return carry

    lax.fori_loop(0, leaves // 4, two_pairs, 0)
    process(leaves // 2 - 1, buffer1)
    for copy in near_lists:
        copy.wait()
    near = jnp.concatenate([owner[...].astype(f32), slot[...].astype(f32)], axis=0)
    blank = jnp.zeros((near.shape[0], 128 - near.shape[1]), f32)
    tgt[count // 2 :, :] = jnp.concatenate([near, blank], axis=1).astype(bf16)
    rest += [begin(src, src_out), begin(tgt, tgt_out), begin(src, mine_out.at[pl.ds(0, leaves)])]
    rest += [begin(rows, rows_out), begin(norms, norms_out)]
    tiles = pl.ds(0, 3 * leaves)
    rest += [begin(cols.at[tiles], cols_out.at[tiles])]
    first, half = 0, leaves // 2
    number, row = leaves, 0
    while half > 0:
        for j in range(half):
            left = joined[first + 2 * j]
            right = joined[first + 2 * j + 1]
            finish(number, combine(left, right, inner_skel[row : row + 1, :], inner_interp[row]))
            number, row = number + 1, row + 1
        first = first + 2 * half
        half = half // 2
    node = joined[2 * leaves - 2]
    root[...] = jnp.concatenate([node, jnp.zeros_like(node)], axis=1)
    last = cols.shape[0] - 1
    cols[last] = jnp.zeros((128, 128), bf16)
    loads[last] = jnp.zeros((16, 128), bf16)
    inner_tiles = pl.ds(3 * leaves, leaves)
    rest += [begin(root, mine_out.at[leaves]), begin(loads, loads_out)]
    rest += [begin(cols.at[inner_tiles], cols_out.at[inner_tiles])]
    for copy in rest:
        copy.wait()


def path_rows():
    devices = lax.axis_size("leaf")
    device = lax.axis_index("leaf")
    bits = devices.bit_length() - 1
    return [devices - (devices >> (h - 1)) + (device >> h) for h in range(1, bits)]


def first_part(points, charges, order, owner, slot, *tables):
    count = points.shape[1]
    leaves = count // 256
    tiles = 4 * leaves
    steps = len(path_rows())
    leaf_interp, leaf_skel, inner_interp, inner_skel = tables[:4]
    src = (leaves, 80, 256)
    tgt = (count // 2 + 2 * owner.shape[0], 128)
    cols = (tiles, 128, 128)
    loads = (tiles, 16, 128)
    rows = (leaves, 256, 128)
    norms = (leaves, 1, 256)
    shapes = [
        (src, bf16),
        (tgt, bf16),
        (cols, bf16),
        (loads, bf16),
        (rows, bf16),
        (norms, f32),
        ((leaves + 1, 80, 256), bf16),
        ((steps, 256, 128), bf16),
        ((steps, 1, 128), jnp.int32),
    ]
    held = [
        (points.shape, bf16),
        (charges.shape, bf16),
        (owner.shape, jnp.int32),
        (slot.shape, jnp.int32),
        ((count, 128), f32),
        ((512, 128), f32),
        ((512, 128), f32),
    ]
    held += shapes[:6]
    held += [((2 * leaves - 1, 80, 128), bf16), ((80, 256), bf16)]
    held += [(table.shape, table.dtype) for table in tables[:4]]
    return pl.pallas_call(
        first_kernel,
        out_shape=tuple(jax.ShapeDtypeStruct(*shape) for shape in shapes),
        in_specs=[SMEM] + [ANY] * 10,
        out_specs=(ANY,) * 9,
        scratch_shapes=[pltpu.VMEM(*shape) for shape in held]
        + [pltpu.SemaphoreType.DMA((20 + 2 * steps,))],
        compiler_params=params(FIRST_LIMIT),
        cost_estimate=cost(),
        name="order_and_subtree",
    )(order, points, charges, owner, slot, *tables)


def far_kernel(*refs, first_leaf, n_leaves, n_ids):
    codes = refs[:n_ids]
    far_list, far_count, cols_in, loads_in, rows_in, acc = refs[n_ids : 6 + n_ids]
    lists = refs[6 + n_ids : -5]
    cols, loads, rows, tiles, sems = refs[-5:]
    leaves = rows.shape[0]
    width = far_list.shape[1]
    first_node = 2 * leaves
    empty = cols.shape[0] - 1
    mine = pl.ds(first_leaf, n_leaves)
    my_tiles = pl.ds(2 * first_leaf, 2 * n_leaves)
    nodes = pl.ds(first_node, cols.shape[0] - first_node)
    copies = [
        pltpu.make_async_copy(rows_in.at[mine], rows.at[mine], sems.at[0]),
        pltpu.make_async_copy(cols_in.at[my_tiles], cols.at[my_tiles], sems.at[1]),
        pltpu.make_async_copy(loads_in, loads, sems.at[2]),
        pltpu.make_async_copy(cols_in.at[nodes], cols.at[nodes], sems.at[3]),
    ]
    for copy in copies:
        copy.start()

    def list_leaf(k, count):
        i = first_leaf + k
        tiles[count] = (i << 16) | ((2 * i) << 8) | (2 * i + 1)
        count = count + 1
        used = far_count[i]
        for k in range(0, width, 2):
            first = far_list[i, k] + first_node
            second = jnp.where(k + 1 < used, far_list[i, k + 1] + first_node, empty)
            tiles[count] = (i << 16) | (first << 8) | second
            count = count + (k < used).astype(jnp.int32)
        return count

    count = lax.fori_loop(0, n_leaves, list_leaf, 0)
    for u in range(FAR_UNROLL):
        tiles[count + u] = (empty << 8) | empty

    def step(g, carry):
        values, weights = [], []
        for u in range(FAR_UNROLL):
            packed = tiles[g * FAR_UNROLL + u]
            leaf = packed >> 16
            first = (packed >> 8) & 255
            second = packed & 255
            matrix = jnp.concatenate([cols[first], cols[second]], axis=1)
            load = jnp.concatenate([loads[first], loads[second]], axis=1)
            values.append(jnp.exp(dot(rows[leaf], matrix)).astype(bf16))
            weights.append(placed(load, leaf & 7))
        acc[...] += dot_nt(jnp.concatenate(values, axis=1), jnp.concatenate(weights, axis=1))
        return carry

    acc[...] = jnp.zeros_like(acc)
    for k in range(n_ids):
        list_pairs(codes[k], lists[PHASES * k : PHASES * k + PHASES])
    for copy in copies:
        copy.wait()
    lax.fori_loop(0, lax.div(count + FAR_UNROLL - 1, FAR_UNROLL), step, 0)


def list_pairs(codes, tables):
    per_leaf, leaves = codes.shape
    for g in range(leaves // 8):
        counts = [jnp.int32(0)] * len(tables)
        for j in range(8):
            for u in range(per_leaf):
                value = codes[u, g * 8 + j]
                for p, table in enumerate(tables):
                    if table is None:
                        continue
                    table[g, 1 + counts[p]] = value & CODE
                    counts[p] = counts[p] + ((value >> (PHASE_BIT + p)) & 1)
        for p, table in enumerate(tables):
            if table is None:
                continue
            table[g, 1 + counts[p]] = DUMMY
            table[g, 0] = (counts[p] + 1) & ~1


def pair_table(leaves):
    return jax.ShapeDtypeStruct((leaves // 8, 128), jnp.int32)


def self_and_far(codes, far_list, far_count, cols, loads, rows, call, calls):
    leaves = rows.shape[0]
    width = far_list.shape[1]
    n_leaves = leaves // calls
    out = pl.pallas_call(
        functools.partial(
            far_kernel, first_leaf=call * n_leaves, n_leaves=n_leaves, n_ids=len(codes)
        ),
        out_shape=(jax.ShapeDtypeStruct((256, 128), f32),) + (pair_table(leaves),) * (PHASES * len(codes)),
        in_specs=[SMEM] * (2 + len(codes)) + [ANY] * 3,
        out_specs=(VMEM,) + (SMEM,) * (PHASES * len(codes)),
        scratch_shapes=[
            pltpu.VMEM(cols.shape, bf16),
            pltpu.VMEM(loads.shape, bf16),
            pltpu.VMEM(rows.shape, bf16),
            pltpu.SMEM((n_leaves * (1 + width // 2) + 1 + FAR_UNROLL,), jnp.int32),
            pltpu.SemaphoreType.DMA((4,)),
        ],
        compiler_params=params(FIRST_LIMIT),
        cost_estimate=cost(),
        name=f"self_and_far{call}",
    )(*codes, far_list, far_count, cols, loads, rows)
    return out[0], [out[1 + PHASES * k : 1 + PHASES * k + PHASES] for k in range(len(codes))]


def near_kernel(*refs, n_sources, n_targets, n_lists, phase):
    refs = list(refs)

    def take(n):
        taken = refs[:n]
        del refs[:n]
        return taken

    makes = phase < PHASES - 1
    (codes,) = take(1) if makes else (None,)
    lists = take(n_lists)
    target_parts = take(n_targets)
    source_parts = take(n_sources)
    before = take(phase > 0)
    outs = take(n_targets) if not makes else []
    (acc,) = take(1) if makes else (None,)
    tables = take(PHASES - 1 - phase) if makes else []
    sources, targets, sems, table, flat, steps = take(6)
    if not makes:
        (acc,) = refs
    leaves = source_parts[0].shape[0]
    size = leaves * 128
    copies = []

    def begin(part, place):
        copies.append(pltpu.make_async_copy(part, place, sems.at[len(copies)]))
        copies[-1].start()

    done = 0
    for part in before:
        done = part.shape[0]
        begin(part, acc.at[pl.ds(0, done)])
    for k, part in enumerate(target_parts):
        begin(part.at[pl.ds(0, size)], targets.at[pl.ds(k * size, size)])
    for k, part in enumerate(source_parts):
        begin(part.at[pl.ds(0, leaves)], sources.at[pl.ds(k * leaves, leaves)])
    if done < acc.shape[0]:
        acc[done:] = jnp.zeros((acc.shape[0] - done,) + acc.shape[1:], f32)
    if makes:
        if phase > 0:
            list_pairs(codes, [None] * phase + [table] + tables)
            lists = lists + [table]
        else:
            list_pairs(codes, [None] + tables)

    counts = [jnp.int32(0)] * len(NEAR_STEPS)
    base = jnp.int32(0)
    for number, pairs in enumerate(lists):
        for row in range(pairs.shape[0]):
            group = number * pairs.shape[0] + row
            used = pairs[row, 0]

            def copy_pair(i, at, pairs=pairs, row=row, group=group):
                flat[at + i] = pairs[row, 1 + i] | (group << 19)
                return at

            lax.fori_loop(0, used, copy_pair, base)
            start = base
            for k, size in enumerate(NEAR_STEPS):
                if k == 0:
                    whole = lax.div(used, size)

                    def note(i, count, start=start, size=size):
                        steps[0, count + i] = start + i * size
                        return count

                    lax.fori_loop(0, whole, note, counts[0])
                    counts[0] = counts[0] + whole
                    start = start + whole * size
                else:
                    steps[k, counts[k]] = start
                    has = jnp.where((used & size) > 0, 1, 0)
                    counts[k] = counts[k] + has
                    start = start + has * size
            base = base + used

    for copy in copies:
        copy.wait()

    for k, size in enumerate(NEAR_STEPS):

        def step(i, carry, k=k, size=size):
            start = steps[k, i]
            values, weights = [], []
            group = (flat[start] >> 19) & 31
            for u in range(size):
                packed = flat[start + u]
                target = (packed >> 16) & 7
                source = packed & 65535
                place = jnp.where(packed < DUMMY, target, 8)
                odd = target & 1
                both = sources[source]
                coords = both[:64]
                zero = jnp.zeros_like(coords)
                matrix = jnp.concatenate(
                    [jnp.where(odd == 0, coords, zero), jnp.where(odd == 1, coords, zero)],
                    axis=0,
                )
                at = pl.multiple_of(group * 1024 + (target >> 1) * 256, 256)
                value = dot(targets[pl.ds(at, 256), :], matrix) - norm_row(coords)
                values.append(jnp.exp(value).astype(bf16))
                weights.append(placed(both[64:], place))
            acc[group] += dot_nt(jnp.concatenate(values, axis=1), jnp.concatenate(weights, axis=1))
            return carry

        lax.fori_loop(0, counts[k], step, 0)

    each = acc.shape[0] // n_targets
    for k, out in enumerate(outs):
        out[...] = acc[k * each : (k + 1) * each].astype(bf16)


def near(phase, lists, targets, sources, codes=None, before=None):
    n_sources, n_targets = len(sources), len(targets)
    leaves = min(source.shape[0] for source in sources)
    sums = jax.ShapeDtypeStruct((n_targets * leaves // 8, 256, 128), f32)
    part = jax.ShapeDtypeStruct((leaves // 8, 256, 128), bf16)
    makes = phase < PHASES - 1
    args = ([codes] if makes else []) + list(lists) + list(targets) + list(sources)
    args += [] if before is None else [before]
    n_smem = len(lists) + makes
    n_tables = PHASES - 1 - phase
    if makes:
        out_shape = (sums,) + (pair_table(leaves),) * n_tables
        out_specs = (VMEM,) + (SMEM,) * n_tables
    else:
        out_shape, out_specs = (part,) * n_targets, (VMEM,) * n_targets
    scratch = [
        pltpu.VMEM((n_sources * leaves, 80, 256), bf16),
        pltpu.VMEM((n_targets * leaves * 128, 128), bf16),
        pltpu.SemaphoreType.DMA((n_sources + n_targets + 1,)),
        pltpu.SMEM(pair_table(leaves).shape, jnp.int32),
        pltpu.SMEM((n_targets * leaves * 8,), jnp.int32),
        pltpu.SMEM((len(NEAR_STEPS), n_targets * leaves), jnp.int32),
    ]
    if not makes:
        scratch.append(pltpu.VMEM(sums.shape, f32))
    return pl.pallas_call(
        functools.partial(
            near_kernel, n_sources=n_sources, n_targets=n_targets, n_lists=len(lists), phase=phase
        ),
        out_shape=out_shape,
        in_specs=[SMEM] * n_smem + [ANY] * (len(args) - n_smem),
        out_specs=out_specs,
        scratch_shapes=scratch,
        compiler_params=params(),
        cost_estimate=cost(),
        name=f"near{phase}",
    )(*args)


def ordered(first, second, test):
    return jnp.where(test, first, second), jnp.where(test, second, first)


def climb_kernel(me, own, other, skels, interps, parent, *, height, row):
    sibling = other[0, :, :128] if len(other.shape) == 3 else other[...]
    left, right = ordered(own[0, :, :128] if len(own.shape) == 3 else own[...], sibling, ((me[0] >> height) & 1) == 0)
    parent[...] = combine(left, right, skels[row], interps[row])


def last_block(value):
    if value.ndim == 2:
        return VMEM
    blocks = value.shape[0]
    return pl.BlockSpec((1,) + value.shape[1:], lambda i: (blocks - 1, 0, 0))


def climb(me, own, other, skels, interps, height, row):
    return pl.pallas_call(
        functools.partial(climb_kernel, height=height, row=row),
        grid=(1,),
        out_shape=jax.ShapeDtypeStruct((80, 128), bf16),
        in_specs=[SMEM, last_block(own), last_block(other), VMEM, VMEM],
        out_specs=VMEM,
        compiler_params=params(),
        cost_estimate=cost(),
        name=f"climb{height}",
    )(me, own, other, skels, interps)


def top_kernel(*refs):
    parts, (rows, acc, cols, loads) = refs[:-4], refs[-4:]
    for t, part in enumerate(parts):
        node = part[0, :, :128] if len(part.shape) == 3 else part[...]
        cols[:, t * 128 : (t + 1) * 128] = source_matrix(node[:64], norm_row(node[:64]))
        loads[:, t * 128 : (t + 1) * 128] = jnp.concatenate([node[64:]] * 8, axis=0)
    lane = lax.broadcasted_iota(jnp.int32, (256, 128), 1) >> 4

    def two_leaves(i, carry):
        both = rows[pl.ds(2 * i, 2)].reshape(512, 128)
        value = jnp.exp(dot(both, cols[...])).astype(bf16)
        result = dot_nt(value, loads[...])
        group = lax.div(i, 4)
        place = (2 * i) & 7
        acc[group] += jnp.where(lane == place, result[:256], 0.0) + jnp.where(
            lane == place + 1, result[256:], 0.0
        )
        return carry

    acc[...] = jnp.zeros_like(acc)
    lax.fori_loop(0, rows.shape[0] // 2, two_leaves, 0, unroll=2)


def top(parts, rows):
    levels = len(parts)
    return pl.pallas_call(
        top_kernel,
        out_shape=jax.ShapeDtypeStruct((rows.shape[0] // 8, 256, 128), f32),
        grid=(1,),
        in_specs=[last_block(part) for part in parts] + [VMEM],
        out_specs=VMEM,
        scratch_shapes=[
            pltpu.VMEM((128, levels * 128), bf16),
            pltpu.VMEM((128, levels * 128), bf16),
        ],
        compiler_params=params(),
        cost_estimate=cost(),
        name="top",
    )(*parts, rows)


def last_kernel(*refs, n_far):
    fars = refs[:n_far]
    above, norms = refs[n_far : n_far + 2]
    received, out = refs[n_far + 2 : -1], refs[-1]
    groups = above.shape[0]
    for group in range(groups):
        local = above[group]
        for far in fars[group * n_far // groups : (group + 1) * n_far // groups]:
            local = local + far[...]
        local = jnp.transpose(local)
        total = received[0][group].astype(f32)
        for part in received[1:]:
            total = total + part[group].astype(f32)
        total = jnp.transpose(total)
        for j in range(8):
            leaf = group * 8 + j
            rows = slice(16 * j, 16 * j + 16)
            out[:, leaf * 256 : (leaf + 1) * 256] = local[rows] + total[rows] * jnp.exp(-norms[leaf])


def last(fars, above, norms, received):
    return pl.pallas_call(
        functools.partial(last_kernel, n_far=len(fars)),
        out_shape=jax.ShapeDtypeStruct((16, norms.shape[0] * 256), f32),
        in_specs=[VMEM] * (2 + len(fars) + len(received)),
        out_specs=VMEM,
        compiler_params=params(),
        cost_estimate=cost(),
        name="last_sum",
    )(*fars, above, norms, *received)


def spread(number, bits):
    return sum(((number >> k) & 1) << b for k, b in enumerate(bits))


def compress(number, bits):
    return sum(((number >> b) & 1) << k for k, b in enumerate(bits))


def swap(value, mask):
    pairs = [(d, d ^ mask) for d in range(lax.axis_size("leaf"))]
    return lax.ppermute(value, "leaf", pairs)


def after(value, *others):
    return lax.optimization_barrier((value,) + others)[0]


def shards(
    points,
    charges,
    leaf_order,
    near_owner,
    near_slot,
    far_list,
    far_count,
    leaf_interp,
    leaf_skel,
    inner_interp,
    inner_skel,
    top_interp,
    top_skel,
):
    device_count = lax.axis_size("leaf")
    bits = device_count.bit_length() - 1
    source_bits = tuple(b for b in range(bits) if b not in TARGET_BITS)
    outer_bits = source_bits[1:]
    device = lax.axis_index("leaf")
    leaves = near_owner.shape[0]
    me = device.reshape(1).astype(jnp.int32)
    mates = range(1, 2 ** len(TARGET_BITS))
    early_bits = outer_bits[:-1]
    late = 2 ** outer_bits[-1]

    def codes_of(owner, slot, first):
        other = owner ^ device
        target_mask = sum(2**b for b in TARGET_BITS)
        place = compress(other, source_bits) * leaves + slot
        here = jnp.where((other & target_mask) == 0, 1, 0)
        near_half = leaves << (len(source_bits) - 1)
        is_late = place >= near_half
        place = place & (near_half - 1)
        is_last = is_late & (place >= 2 * leaves)
        piece = place // leaves
        is_first = ~is_late & (first == 0) & ((piece < 2) | (piece % 2 == 0))
        phase = jnp.where(is_last, 2, jnp.where(is_first, 0, 1))
        first_place = place - (piece - jnp.where(piece < 2, piece, piece // 2 + 1)) * leaves
        place = jnp.where(
            is_last,
            place - 2 * leaves,
            jnp.where(is_late, near_half + place, jnp.where(is_first, first_place, place)),
        )
        target = lax.broadcasted_iota(jnp.int32, owner.shape, 1) & 7
        return (here << (phase + PHASE_BIT)) | (target << 16) | place

    def payload_codes(payload, first):
        near = payload[-2 * near_owner.shape[1] :, :leaves].astype(jnp.int32)
        return codes_of(near[: near_owner.shape[1]], near[near_owner.shape[1] :], first)

    owner, slot = near_owner.T, near_slot.T
    src, tgt, cols, loads, rows, norms, mine, interps, skels = first_part(
        points, charges, leaf_order, owner, slot,
        leaf_interp, leaf_skel, inner_interp, inner_skel, top_interp, top_skel,
    )
    pieces = {0: src, late: swap(src, late)}
    for b in reversed(early_bits):
        pieces[2**b] = swap(src, 2**b)
    beside = swap(tgt, 2 ** TARGET_BITS[0])
    far_away = swap(tgt, 2 ** TARGET_BITS[1])
    pieces[1] = swap(mine, 1)

    def far(call, codes, token):
        return self_and_far(
            codes, after(far_list, token), far_count, cols, loads, rows, call, 2
        )

    far0, lists0 = far(0, [codes_of(owner, slot, 0)], norms)
    node = climb(me, after(mine, far0, beside), pieces[1], skels, interps, 0, 0)
    siblings = [pieces[1], swap(node, 2)]
    far1, lists1 = far(1, [payload_codes(after(beside, far0), 0)], node)
    last_targets = swap(after(far_away, far1), 2 ** TARGET_BITS[0])
    for n, b in enumerate(early_bits):
        for low in range(2**n):
            place = spread(low, early_bits[:n])
            if low:
                pieces[place | 2**b] = swap(pieces[place], 2**b)
    wanted = [spread(k, source_bits) for k in range(2 ** (len(source_bits) - 1))]
    targets = [tgt, beside, far_away, last_targets]
    lists = lists0 + lists1
    sums, far_tables1, far_tables2 = near(
        0,
        [tables[0] for tables in lists],
        targets[:2],
        [pieces[k] for k in wanted if k == 1 or not k & 1],
        codes=payload_codes(after(far_away, far1), 1),
    )
    node = climb(me, node, after(siblings[1], sums), skels, interps, 1, 1)
    for k in wanted[2::2]:
        pieces[k | 1] = swap(after(pieces[k], node), 1)
    pieces[late] = after(pieces[late], node)
    for n, b in enumerate(early_bits):
        for low in range(2**n):
            place = spread(low, early_bits[:n]) | late
            pieces[place | 2**b] = swap(pieces[place], 2**b)
    pieces[late | 1] = swap(pieces[late], 1)
    siblings.append(swap(node, 4))
    sums, last_table = near(
        1,
        [tables[1] for tables in lists] + [far_tables1],
        targets,
        [pieces[k] for k in wanted + [late, late | 1]],
        codes=payload_codes(after(last_targets, node), 1),
        before=sums,
    )
    node = climb(me, node, after(siblings[2], sums), skels, interps, 2, 2)
    siblings.append(swap(node, 8))
    for k in wanted[2::2]:
        pieces[k | late | 1] = swap(after(pieces[k | late], node), 1)
    parts = near(
        2,
        [tables[2] for tables in lists] + [far_tables2, last_table],
        targets,
        [pieces[k | late] for k in wanted[2:]],
        before=sums,
    )
    for height in range(3, bits - 1):
        node = climb(me, node, after(siblings[height], parts[0]), skels, interps, height, height)
        siblings.append(swap(node, 2 ** (height + 1)))
    received = [parts[0]] + [swap(after(parts[k], node), spread(k, TARGET_BITS)) for k in mates]
    above = top(siblings, after(rows, parts[0]))
    return last((far0, far1), above, norms, received)


def solution(mesh):
    in_specs = (
        P(None, "leaf"),
        P(None, "leaf"),
        P("leaf"),
        P("leaf", None),
        P("leaf", None),
        P("leaf", None),
        P("leaf"),
        P("leaf", None, None),
        P("leaf", None),
        P("leaf", None, None),
        P("leaf", None),
        P(),
        P(),
    )
    out_specs = P(None, "leaf")
    return jax.shard_map(shards, mesh=mesh, in_specs=in_specs, out_specs=out_specs, check_vma=False)
```

profile of v0, /device:TPU:0, one launch (start us, length us, event | category | flops | bytes accessed | tf_op | source)
XLA Modules:
  0.0 91.7 jit_solution(2846764410047728999)
XLA Ops:
  0.0 10.4 %order_and_subtree.1 = (bf16[16,80,256]{2,1,0:T(8,128)(2,1)}, bf16[2064,128]{1,0:T(8,128)(2,1)}, bf16[64,128,128]{2,1,0:T(8,128)(2,1)}, bf16[64,16,128]{2,1,0:T(...) custom-call(s32[4096]{0:T(1024)} %order.1, ...), custom_call_target="tpu_custom_call" | custom-call | flops 1 | bytes 1 | tf_op jit(solution)/shard_map/order_and_subtree/pallas_call | solution.py:270
  10.5 3.0 %collective-permute-start = (bf16[2064,128]{1,0:T(8,128)(2,1)}, bf16[2064,128]{1,0:T(8,128)(2,1)S(1)}, u32[]{:S(2)}, u32[]{:S(2)}) collective-permute-start(bf16[2064,128]{1,0:T(8,128)(2,1)} %get-tuple-element.53.refs_3_.refs_4_), channel_id=1, source_target_pairs={{0,2},{1,3},{2,0},{3,1},{4,6},{5,7},{6,4},{7,5},{8,10},{9,11},{10,... | collective-permute-start | bytes 1585160 | tf_op jit(solution)/shard_map/ppermute | solution.py:654
  13.5 1.6 %collective-permute-start.3 = (bf16[2064,128]{1,0:T(8,128)(2,1)}, bf16[2064,128]{1,0:T(8,128)(2,1)S(1)}, u32[]{:S(2)}, u32[]{:S(2)}) collective-permute-start(bf16[2064,128]{1,0:T(8,128)(2,1)} %get-tuple-element.53.refs_3_.refs_4_), channel_id=1, source_target_pairs={{0,8},{1,9},{2,10},{3,11},{4,12},{5,13},{6,14},{7,15},{8,0},{9,1},... | collective-permute-start | bytes 1585160 | tf_op jit(solution)/shard_map/ppermute | solution.py:654
  15.1 1.5 %collective-permute-start.4 = (bf16[16,80,256]{2,1,0:T(8,128)(2,1)}, bf16[16,80,256]{2,1,0:T(8,128)(2,1)S(1)}, u32[]{:S(2)}, u32[]{:S(2)}) collective-permute-start(bf16[16,80,256]{2,1,0:T(8,128)(2,1)} %get-tuple-element.64.refs_5_.refs_8_), channel_id=1, source_target_pairs={{0,4},{1,5},{2,6},{3,7},{4,0},{5,1},{6,2},{7,3},{8,12},{9,13},{10,... | collective-permute-start | bytes 1966088 | tf_op jit(solution)/shard_map/ppermute | solution.py:654
  16.6 2.6 %collective-permute-start.8 = (bf16[16,80,256]{2,1,0:T(8,128)(2,1)}, bf16[16,80,256]{2,1,0:T(8,128)(2,1)}, u32[]{:S(2)}, u32[]{:S(2)}) collective-permute-start(bf16[16,80,256]{2,1,0:T(8,128)(2,1)} %get-tuple-element.64.refs_5_.refs_8_), channel_id=1, source_target_pairs={{0,16},{1,17},{2,18},{3,19},{4,20},{5,21},{6,22},{7,23},{8,24},{9,... | collective-permute-start | bytes 1966088 | tf_op jit(solution)/shard_map/ppermute | solution.py:654
  19.2 0.6 fusion.6.refs_0_
  19.8 8.8 %self_and_far0.1 = (f32[256,128]{1,0:T(8,128)}, s32[2,128]{1,0:T(2,128)}, s32[2,128]{1,0:T(2,128)}, s32[2,128]{1,0:T(2,128)}) custom-call(s32[8,16]{1,0:T(8,128)} %fusion.6.refs_0_, s32[16,16]{1,0:T(8,128)} %refs_1_.1, s32[16]{0:T(128)} %refs_2_.3, bf16[64,128,128]{2,1,0:T(8,128)(2,1)} %get-tuple-element.49.refs_3_, ...), custom_call_target="tpu_custom_call" | custom-call | flops 1 | bytes 1 | tf_op jit(solution)/shard_map/self_and_far0/pallas_call | solution.py:369
  28.7 0.6 fusion.13.refs_0_
  29.3 0.1 climb0.1.own
  29.5 8.2 %self_and_far1.1 = (f32[256,128]{1,0:T(8,128)}, s32[2,128]{1,0:T(2,128)}, s32[2,128]{1,0:T(2,128)}, s32[2,128]{1,0:T(2,128)}) custom-call(s32[8,16]{1,0:T(8,128)} %fusion.13.refs_0_, s32[16,16]{1,0:T(8,128)} %refs_1_.1, s32[16]{0:T(128)} %refs_2_.3, bf16[64,128,128]{2,1,0:T(8,128)(2,1)} %get-tuple-element.49.refs_3_, ...), custom_call_target="tpu_custom_call" | custom-call | flops 1 | bytes 1 | tf_op jit(solution)/shard_map/self_and_far1/pallas_call | solution.py:369
  37.8 0.1 collective-permute-start.6
  37.9 2.0 %collective-permute-start.2 = (bf16[80,128]{1,0:T(8,128)(2,1)S(1)}, bf16[80,128]{1,0:T(8,128)(2,1)S(1)}, u32[]{:S(2)}, u32[]{:S(2)}) collective-permute-start(bf16[80,128]{1,0:T(8,128)(2,1)S(1)} %climb0.1.own), channel_id=1, source_target_pairs={{0,2},{1,3},{2,0},{3,1},{4,6},{5,7},{6,4},{7,5},{8,10},{9,11},{10,... | collective-permute-start | bytes 61448 | tf_op jit(solution)/shard_map/ppermute | solution.py:654
  39.9 0.7 copy-done.14
  40.6 5.7 %near0.1 = (f32[4,256,128]{2,1,0:T(8,128)S(1)}, s32[2,128]{1,0:T(2,128)S(1)}, s32[2,128]{1,0:T(2,128)S(1)}) custom-call(s32[8,16]{1,0:T(8,128)S(1)} %fusion.15.refs_0_, s32[2,128]{1,0:T(2,128)S(1)} %copy-done.13, s32[2,128]{1,0:T(2,128)S(1)} %copy-done.14, bf16[2064,128]{1,0:T(8,128)(2,1)S(1)} %copy-done.1, ...), custom_call_target="tpu_custom_call" | custom-call | flops 1 | bytes 1 | tf_op jit(solution)/shard_map/near0/pallas_call | solution.py:527
  46.3 4.0 %collective-permute-done.2.other.refs_1_ = bf16[80,128]{1,0:T(8,128)(2,1)S(1)} collective-permute-done((bf16[80,128]{1,0:T(8,128)(2,1)S(1)}, bf16[80,128]{1,0:T(8,128)(2,1)S(1)}, u32[]{:S(2)}, u32[]{:S(2)}) %collective-permute-start.2) | collective-permute-done | bytes 20512 | tf_op jit(solution)/shard_map/ppermute | solution.py:654
  50.2 0.1 climb1.1.own
  50.5 0.5 collective-permute-start.7
  51.0 2.5 %collective-permute-start.11 = (bf16[16,80,256]{2,1,0:T(8,128)(2,1)}, bf16[16,80,256]{2,1,0:T(8,128)(2,1)S(1)}, u32[]{:S(2)}, u32[]{:S(2)}) collective-permute-start(bf16[16,80,256]{2,1,0:T(8,128)(2,1)} %collective-permute-done.8.refs_12_), channel_id=1, source_target_pairs={{0,4},{1,5},{2,6},{3,7},{4,0},{5,1},{6,2},{7,3},{8,12},{9,13},{10,... | collective-permute-start | bytes 1966088 | tf_op jit(solution)/shard_map/ppermute | solution.py:654
  53.6 12.2 %near1.1 = (f32[8,256,128]{2,1,0:T(8,128)S(1)}, s32[2,128]{1,0:T(2,128)S(1)}) custom-call(s32[8,16]{1,0:T(8,128)S(1)} %fusion.17.refs_0_, s32[2,128]{1,0:T(2,128)S(1)} %copy-done.11, s32[2,128]{1,0:T(2,128)S(1)} %copy-done.12, s32[2,128]{1,0:T(2,128)S(1)} %get-tuple-element.70.refs_3_, bf16[2064,128]{1,0:T(8,128)(2,1)S(1)} %copy-done.1, ...), custom_call_target="tpu_custom_call" | custom-call | flops 1 | bytes 1 | tf_op jit(solution)/shard_map/near1/pallas_call | solution.py:527
  65.8 3.3 %collective-permute-done.5.other.refs_2_ = bf16[80,128]{1,0:T(8,128)(2,1)S(1)} collective-permute-done((bf16[80,128]{1,0:T(8,128)(2,1)S(1)}, bf16[80,128]{1,0:T(8,128)(2,1)S(1)}, u32[]{:S(2)}, u32[]{:S(2)}) %collective-permute-start.5) | collective-permute-done | bytes 20512 | tf_op jit(solution)/shard_map/ppermute | solution.py:654
  69.1 0.1 climb2.1.own
  69.3 0.1 collective-permute-start.12
  69.4 0.1 collective-permute-start.10
  69.4 2.0 %collective-permute-done.12.refs_9_ = bf16[16,80,256]{2,1,0:T(8,128)(2,1)S(1)} collective-permute-done((bf16[16,80,256]{2,1,0:T(8,128)(2,1)S(1)}, bf16[16,80,256]{2,1,0:T(8,128)(2,1)S(1)}, u32[]{:S(2)}, u32[]{:S(2)}) %collective-permute-start.12) | collective-permute-done | bytes 655392 | tf_op jit(solution)/shard_map/ppermute | solution.py:654
  71.5 6.8 %near2.1 = (bf16[2,256,128]{2,1,0:T(8,128)(2,1)S(1)}, bf16[2,256,128]{2,1,0:T(8,128)(2,1)S(1)}, bf16[2,256,128]{2,1,0:T(8,128)(2,1)S(1)}, bf16[2,256,128]{2,1,0:T(8,128)(2,1)S(1)}) custom-call(s32[2,128]{1,0:T(2,128)S(1)} %copy-done.9, s32[2,128]{1,0:T(2,128)S(1)} %copy-done.10, s32[2,128]{1,0:T(2,128)S(1)} %get-tuple-element.77.refs_2_, ...), custom_call_target="tpu_custom_call" | custom-call | flops 1 | bytes 1 | tf_op jit(solution)/shard_map/near2/pallas_call | solution.py:527
  78.3 0.1 climb3.1
  78.6 1.6 %collective-permute-start.15 = (bf16[2,256,128]{2,1,0:T(8,128)(2,1)S(1)}, bf16[2,256,128]{2,1,0:T(8,128)(2,1)S(1)}, u32[]{:S(2)}, u32[]{:S(2)}) collective-permute-start(bf16[2,256,128]{2,1,0:T(8,128)(2,1)S(1)} %get-tuple-element.86), channel_id=1, source_target_pairs={{0,8},{1,9},{2,10},{3,11},{4,12},{5,13},{6,14},{7,15},{8,0},{9,1},... | collective-permute-start | bytes 393224 | tf_op jit(solution)/shard_map/ppermute | solution.py:654
  80.2 1.9 %collective-permute-start.14 = (bf16[2,256,128]{2,1,0:T(8,128)(2,1)S(1)}, bf16[2,256,128]{2,1,0:T(8,128)(2,1)S(1)}, u32[]{:S(2)}, u32[]{:S(2)}) collective-permute-start(bf16[2,256,128]{2,1,0:T(8,128)(2,1)S(1)} %get-tuple-element.84), channel_id=1, source_target_pairs={{0,2},{1,3},{2,0},{3,1},{4,6},{5,7},{6,4},{7,5},{8,10},{9,11},{10,... | collective-permute-start | bytes 393224 | tf_op jit(solution)/shard_map/ppermute | solution.py:654
  82.0 0.6 collective-permute-start.13
  82.7 4.2 %collective-permute-done.13.refs_4_ = bf16[80,128]{1,0:T(8,128)(2,1)S(1)} collective-permute-done((bf16[80,128]{1,0:T(8,128)(2,1)S(1)}, bf16[80,128]{1,0:T(8,128)(2,1)S(1)}, u32[]{:S(2)}, u32[]{:S(2)}) %collective-permute-start.13) | collective-permute-done | bytes 20512 | tf_op jit(solution)/shard_map/ppermute | solution.py:654
  86.8 3.9 %top.1.refs_2_ = f32[2,256,128]{2,1,0:T(8,128)S(1)} custom-call(bf16[17,80,256]{2,1,0:T(8,128)(2,1)S(1)} %collective-permute-done.1.other.refs_6_.refs_9_.refs_0_, bf16[80,128]{1,0:T(8,128)(2,1)S(1)} %collective-permute-done.2.other.refs_1_, bf16[80,128]{1,0:T(8,128)(2,1)S(1)} %collective-permute-done.5.other.refs_2_, ...), custom_call_target="tpu_custom_call" | custom-call | flops 1 | bytes 1 | tf_op jit(solution)/shard_map/top/pallas_call | solution.py:596
  90.8 0.9 last_sum.1
  (56 shorter events, 0.3 us)
Async XLA Ops:
  0.0 19.2 %copy-start.15 = (s32[16,8]{0,1:T(8,128)S(1)}, s32[16,8]{0,1:T(8,128)}, u32[]{:S(2)}) copy-start(s32[16,8]{0,1:T(8,128)} %param.17) | copy-start | bytes 1540
  0.0 19.2 %copy-start.16 = (s32[16,8]{0,1:T(8,128)S(1)}, s32[16,8]{0,1:T(8,128)}, u32[]{:S(2)}) copy-start(s32[16,8]{0,1:T(8,128)} %param.16) | copy-start | bytes 1540
  10.5 18.8 %copy-start.2 = (bf16[4,256,128]{2,1,0:T(8,128)(2,1)S(1)}, bf16[4,256,128]{2,1,0:T(8,128)(2,1)}, u32[]{:S(2)}) copy-start(bf16[4,256,128]{2,1,0:T(8,128)(2,1)} %get-tuple-element.58.interps) | copy-start | bytes 786436
  10.5 18.8 %copy-start.4 = (bf16[17,80,256]{2,1,0:T(8,128)(2,1)S(1)}, bf16[17,80,256]{2,1,0:T(8,128)(2,1)}, u32[]{:S(2)}) copy-start(bf16[17,80,256]{2,1,0:T(8,128)(2,1)} %get-tuple-element.56.own) | copy-start | bytes 2088964
  10.5 18.8 %copy-start.7 = (s32[4,1,128]{2,1,0:T(1,128)S(1)}, s32[4,1,128]{2,1,0:T(1,128)}, u32[]{:S(2)}) copy-start(s32[4,1,128]{2,1,0:T(1,128)} %get-tuple-element.57.skels) | copy-start | bytes 6148
  10.5 18.1 %collective-permute-start = (bf16[2064,128]{1,0:T(8,128)(2,1)}, bf16[2064,128]{1,0:T(8,128)(2,1)S(1)}, u32[]{:S(2)}, u32[]{:S(2)}) collective-permute-start(bf16[2064,128]{1,0:T(8,128)(2,1)} %get-tuple-element.53.refs_3_.refs_4_), channel_id=1, source_target_pairs={{0,2},{1,3},{2,0},{3,1},{4,6},{5,7},{6,4},{7,5},{8,10},{9,11},{10,... | collective-permute-start | bytes 1585160 | tf_op jit(solution)/shard_map/ppermute | solution.py:654
  13.5 24.3 %collective-permute-start.3 = (bf16[2064,128]{1,0:T(8,128)(2,1)}, bf16[2064,128]{1,0:T(8,128)(2,1)S(1)}, u32[]{:S(2)}, u32[]{:S(2)}) collective-permute-start(bf16[2064,128]{1,0:T(8,128)(2,1)} %get-tuple-element.53.refs_3_.refs_4_), channel_id=1, source_target_pairs={{0,8},{1,9},{2,10},{3,11},{4,12},{5,13},{6,14},{7,15},{8,0},{9,1},... | collective-permute-start | bytes 1585160 | tf_op jit(solution)/shard_map/ppermute | solution.py:654
  15.1 24.8 %collective-permute-start.4 = (bf16[16,80,256]{2,1,0:T(8,128)(2,1)}, bf16[16,80,256]{2,1,0:T(8,128)(2,1)S(1)}, u32[]{:S(2)}, u32[]{:S(2)}) collective-permute-start(bf16[16,80,256]{2,1,0:T(8,128)(2,1)} %get-tuple-element.64.refs_5_.refs_8_), channel_id=1, source_target_pairs={{0,4},{1,5},{2,6},{3,7},{4,0},{5,1},{6,2},{7,3},{8,12},{9,13},{10,... | collective-permute-start | bytes 1966088 | tf_op jit(solution)/shard_map/ppermute | solution.py:654
  16.6 33.8 %collective-permute-start.8 = (bf16[16,80,256]{2,1,0:T(8,128)(2,1)}, bf16[16,80,256]{2,1,0:T(8,128)(2,1)}, u32[]{:S(2)}, u32[]{:S(2)}) collective-permute-start(bf16[16,80,256]{2,1,0:T(8,128)(2,1)} %get-tuple-element.64.refs_5_.refs_8_), channel_id=1, source_target_pairs={{0,16},{1,17},{2,18},{3,19},{4,20},{5,21},{6,22},{7,23},{8,24},{9,... | collective-permute-start | bytes 1966088 | tf_op jit(solution)/shard_map/ppermute | solution.py:654
  19.2 10.1 %collective-permute-start.1 = (bf16[17,80,256]{2,1,0:T(8,128)(2,1)}, bf16[17,80,256]{2,1,0:T(8,128)(2,1)S(1)}, u32[]{:S(2)}, u32[]{:S(2)}) collective-permute-start(bf16[17,80,256]{2,1,0:T(8,128)(2,1)} %get-tuple-element.56.own), channel_id=1, source_target_pairs={{0,1},{1,0},{2,3},{3,2},{4,5},{5,4},{6,7},{7,6},{8,9},{9,8},{10,11... | collective-permute-start | bytes 2088968 | tf_op jit(solution)/shard_map/ppermute | solution.py:654
  29.5 10.4 %copy-start.1 = (bf16[2064,128]{1,0:T(8,128)(2,1)S(1)}, bf16[2064,128]{1,0:T(8,128)(2,1)}, u32[]{:S(2)}) copy-start(bf16[2064,128]{1,0:T(8,128)(2,1)} %get-tuple-element.53.refs_3_.refs_4_) | copy-start | bytes 1585156
  29.5 10.4 %copy-start.3 = (bf16[16,80,256]{2,1,0:T(8,128)(2,1)S(1)}, bf16[16,80,256]{2,1,0:T(8,128)(2,1)}, u32[]{:S(2)}) copy-start(bf16[16,80,256]{2,1,0:T(8,128)(2,1)} %get-tuple-element.64.refs_5_.refs_8_) | copy-start | bytes 1966084
  37.7 15.9 %copy-start.11 = (s32[2,128]{1,0:T(2,128)S(1)}, s32[2,128]{1,0:T(2,128)}, u32[]{:S(2)}) copy-start(s32[2,128]{1,0:T(2,128)} %get-tuple-element.68.refs_1_) | copy-start | bytes 3076
  37.7 15.9 %copy-start.12 = (s32[2,128]{1,0:T(2,128)S(1)}, s32[2,128]{1,0:T(2,128)}, u32[]{:S(2)}) copy-start(s32[2,128]{1,0:T(2,128)} %get-tuple-element.69.refs_2_) | copy-start | bytes 3076
  37.8 15.8 %collective-permute-start.6 = (bf16[2064,128]{1,0:T(8,128)(2,1)S(1)}, bf16[2064,128]{1,0:T(8,128)(2,1)S(1)}, u32[]{:S(2)}, u32[]{:S(2)}) collective-permute-start(bf16[2064,128]{1,0:T(8,128)(2,1)S(1)} %collective-permute-done.3.refs_6_), channel_id=1, source_target_pairs={{0,2},{1,3},{2,0},{3,1},{4,6},{5,7},{6,4},{7,5},{8,10},{9,11},{10,... | collective-permute-start | bytes 1585160 | tf_op jit(solution)/shard_map/ppermute | solution.py:654
  37.9 12.4 %collective-permute-start.2 = (bf16[80,128]{1,0:T(8,128)(2,1)S(1)}, bf16[80,128]{1,0:T(8,128)(2,1)S(1)}, u32[]{:S(2)}, u32[]{:S(2)}) collective-permute-start(bf16[80,128]{1,0:T(8,128)(2,1)S(1)} %climb0.1.own), channel_id=1, source_target_pairs={{0,2},{1,3},{2,0},{3,1},{4,6},{5,7},{6,4},{7,5},{8,10},{9,11},{10,... | collective-permute-start | bytes 61448 | tf_op jit(solution)/shard_map/ppermute | solution.py:654
  50.4 3.2 %collective-permute-start.9 = (bf16[16,80,256]{2,1,0:T(8,128)(2,1)}, bf16[16,80,256]{2,1,0:T(8,128)(2,1)S(1)}, u32[]{:S(2)}, u32[]{:S(2)}) collective-permute-start(bf16[16,80,256]{2,1,0:T(8,128)(2,1)} %collective-permute-done.8.refs_12_), channel_id=1, source_target_pairs={{0,1},{1,0},{2,3},{3,2},{4,5},{5,4},{6,7},{7,6},{8,9},{9,8},{10,11... | collective-permute-start | bytes 1966088 | tf_op jit(solution)/shard_map/ppermute | solution.py:654
  50.5 3.1 %collective-permute-start.7 = (bf16[16,80,256]{2,1,0:T(8,128)(2,1)S(1)}, bf16[16,80,256]{2,1,0:T(8,128)(2,1)S(1)}, u32[]{:S(2)}, u32[]{:S(2)}) collective-permute-start(bf16[16,80,256]{2,1,0:T(8,128)(2,1)S(1)} %collective-permute-done.4.refs_7_.refs_10_), channel_id=1, source_target_pairs={{0,1},{1,0},{2,3},{3,2},{4,5},{5,4},{6,7},{7,6},{8,9},{9,8},{10,11... | collective-permute-start | bytes 1966088 | tf_op jit(solution)/shard_map/ppermute | solution.py:654
  51.0 18.3 %collective-permute-start.11 = (bf16[16,80,256]{2,1,0:T(8,128)(2,1)}, bf16[16,80,256]{2,1,0:T(8,128)(2,1)S(1)}, u32[]{:S(2)}, u32[]{:S(2)}) collective-permute-start(bf16[16,80,256]{2,1,0:T(8,128)(2,1)} %collective-permute-done.8.refs_12_), channel_id=1, source_target_pairs={{0,4},{1,5},{2,6},{3,7},{4,0},{5,1},{6,2},{7,3},{8,12},{9,13},{10,... | collective-permute-start | bytes 1966088 | tf_op jit(solution)/shard_map/ppermute | solution.py:654
  53.5 15.6 %collective-permute-start.5 = (bf16[80,128]{1,0:T(8,128)(2,1)S(1)}, bf16[80,128]{1,0:T(8,128)(2,1)S(1)}, u32[]{:S(2)}, u32[]{:S(2)}) collective-permute-start(bf16[80,128]{1,0:T(8,128)(2,1)S(1)} %climb1.1.own), channel_id=1, source_target_pairs={{0,4},{1,5},{2,6},{3,7},{4,0},{5,1},{6,2},{7,3},{8,12},{9,13},{10,... | collective-permute-start | bytes 61448 | tf_op jit(solution)/shard_map/ppermute | solution.py:654
  53.6 17.8 %copy-start.9 = (s32[2,128]{1,0:T(2,128)S(1)}, s32[2,128]{1,0:T(2,128)}, u32[]{:S(2)}) copy-start(s32[2,128]{1,0:T(2,128)} %get-tuple-element.75.refs_0_) | copy-start | bytes 3076
  53.6 17.8 %copy-start.10 = (s32[2,128]{1,0:T(2,128)S(1)}, s32[2,128]{1,0:T(2,128)}, u32[]{:S(2)}) copy-start(s32[2,128]{1,0:T(2,128)} %get-tuple-element.76.refs_1_) | copy-start | bytes 3076
  69.3 2.2 %collective-permute-start.12 = (bf16[16,80,256]{2,1,0:T(8,128)(2,1)S(1)}, bf16[16,80,256]{2,1,0:T(8,128)(2,1)S(1)}, u32[]{:S(2)}, u32[]{:S(2)}) collective-permute-start(bf16[16,80,256]{2,1,0:T(8,128)(2,1)S(1)} %collective-permute-done.11.refs_8_), channel_id=1, source_target_pairs={{0,1},{1,0},{2,3},{3,2},{4,5},{5,4},{6,7},{7,6},{8,9},{9,8},{10,11... | collective-permute-start | bytes 1966088 | tf_op jit(solution)/shard_map/ppermute | solution.py:654
  69.4 8.9 %collective-permute-start.10 = (bf16[80,128]{1,0:T(8,128)(2,1)S(1)}, bf16[80,128]{1,0:T(8,128)(2,1)S(1)}, u32[]{:S(2)}, u32[]{:S(2)}) collective-permute-start(bf16[80,128]{1,0:T(8,128)(2,1)S(1)} %climb2.1.own), channel_id=1, source_target_pairs={{0,8},{1,9},{2,10},{3,11},{4,12},{5,13},{6,14},{7,15},{8,0},{9,1},... | collective-permute-start | bytes 61448 | tf_op jit(solution)/shard_map/ppermute | solution.py:654
  71.5 15.4 %copy-start = (bf16[16,256,128]{2,1,0:T(8,128)(2,1)S(1)}, bf16[16,256,128]{2,1,0:T(8,128)(2,1)}, u32[]{:S(2)}) copy-start(bf16[16,256,128]{2,1,0:T(8,128)(2,1)} %get-tuple-element.82.refs_5_) | copy-start | bytes 3145732
  78.3 12.5 %copy-start.5 = (f32[256,128]{1,0:T(8,128)S(1)}, f32[256,128]{1,0:T(8,128)}, u32[]{:S(2)}) copy-start(f32[256,128]{1,0:T(8,128)} %get-tuple-element.52.refs_0_) | copy-start | bytes 393220
  78.3 12.5 %copy-start.6 = (f32[256,128]{1,0:T(8,128)S(1)}, f32[256,128]{1,0:T(8,128)}, u32[]{:S(2)}) copy-start(f32[256,128]{1,0:T(8,128)} %get-tuple-element.60.refs_1_) | copy-start | bytes 393220
  78.3 12.5 %copy-start.8 = (f32[16,1,256]{2,1,0:T(1,128)S(1)}, f32[16,1,256]{2,1,0:T(1,128)}, u32[]{:S(2)}) copy-start(f32[16,1,256]{2,1,0:T(1,128)} %get-tuple-element.47.refs_3_) | copy-start | bytes 49156
  78.5 12.2 %collective-permute-start.16 = (bf16[2,256,128]{2,1,0:T(8,128)(2,1)S(1)}, bf16[2,256,128]{2,1,0:T(8,128)(2,1)S(1)}, u32[]{:S(2)}, u32[]{:S(2)}) collective-permute-start(bf16[2,256,128]{2,1,0:T(8,128)(2,1)S(1)} %get-tuple-element.88), channel_id=1, source_target_pairs={{0,10},{1,11},{2,8},{3,9},{4,14},{5,15},{6,12},{7,13},{8,2},{9,3},... | collective-permute-start | bytes 393224 | tf_op jit(solution)/shard_map/ppermute | solution.py:654
  78.6 12.2 %collective-permute-start.15 = (bf16[2,256,128]{2,1,0:T(8,128)(2,1)S(1)}, bf16[2,256,128]{2,1,0:T(8,128)(2,1)S(1)}, u32[]{:S(2)}, u32[]{:S(2)}) collective-permute-start(bf16[2,256,128]{2,1,0:T(8,128)(2,1)S(1)} %get-tuple-element.86), channel_id=1, source_target_pairs={{0,8},{1,9},{2,10},{3,11},{4,12},{5,13},{6,14},{7,15},{8,0},{9,1},... | collective-permute-start | bytes 393224 | tf_op jit(solution)/shard_map/ppermute | solution.py:654
  80.2 10.6 %collective-permute-start.14 = (bf16[2,256,128]{2,1,0:T(8,128)(2,1)S(1)}, bf16[2,256,128]{2,1,0:T(8,128)(2,1)S(1)}, u32[]{:S(2)}, u32[]{:S(2)}) collective-permute-start(bf16[2,256,128]{2,1,0:T(8,128)(2,1)S(1)} %get-tuple-element.84), channel_id=1, source_target_pairs={{0,2},{1,3},{2,0},{3,1},{4,6},{5,7},{6,4},{7,5},{8,10},{9,11},{10,... | collective-permute-start | bytes 393224 | tf_op jit(solution)/shard_map/ppermute | solution.py:654
  82.0 4.8 %collective-permute-start.13 = (bf16[80,128]{1,0:T(8,128)(2,1)S(1)}, bf16[80,128]{1,0:T(8,128)(2,1)S(1)}, u32[]{:S(2)}, u32[]{:S(2)}) collective-permute-start(bf16[80,128]{1,0:T(8,128)(2,1)S(1)} %climb3.1), channel_id=1, source_target_pairs={{0,16},{1,17},{2,18},{3,19},{4,20},{5,21},{6,22},{7,23},{8,24},{9,... | collective-permute-start | bytes 61448 | tf_op jit(solution)/shard_map/ppermute | solution.py:654
  (2 other events, 11.1 us)
where the time goes:
time: 92.4 us; the launch traced here: 91.7 us
  Pallas kernels  57.5 us (62%)
  starting transfers between devices  18.2 us (20%)
  waiting for transfers between devices  13.5 us (15%)
  other arithmetic  1.31 us (1%)
    pallas_call x3, Pallas kernels, near(): pl.pallas_call(functools.partial(near_kernel, n_sources=n_sources, n_targ...  24.7 us
    ppermute x17, starting transfers between devices, swap(): return lax.ppermute(value, 'leaf', pairs)  18.2 us
    pallas_call x2, Pallas kernels, self_and_far(): pl.pallas_call(functools.partial(far_kernel, first_leaf=call * n_leaves,...  17 us
    ppermute x17, waiting for transfers between devices, swap(): return lax.ppermute(value, 'leaf', pairs)  13.5 us
    pallas_call x1, Pallas kernels, first_part(): pl.pallas_call(first_kernel, out_shape=tuple((jax.ShapeDtypeStruct(*shape...  10.4 us
    pallas_call x1, Pallas kernels, top(): pl.pallas_call(top_kernel, out_shape=jax.ShapeDtypeStruct((rows.shape[0]...  3.88 us
  transfers between devices with their start and end apart: 17, of which 4 were waited for; matrix products, arithmetic and copies ran while one was open for 1% of the time, Pallas kernels for 50%

commit v1 on v0

--- a/solution.py
+++ b/solution.py
@@ -76,6 +76,22 @@
         [coords.astype(f32) * 0.25, extra, jnp.zeros((48, width), f32)], axis=0
     )
     return jnp.transpose(wide).astype(bf16)
+
+
+def tiles_sum(count, exponent, weight):
+    total = None
+    value = None
+    ahead = exponent(0)
+    for u in range(count):
+        now = ahead
+        if u + 1 < count:
+            ahead = exponent(u + 1)
+        if value is not None:
+            part = dot_nt(value, weight(u - 1))
+            total = part if total is None else total + part
+        value = jnp.exp(now).astype(bf16)
+    part = dot_nt(value, weight(count - 1))
+    return part if total is None else total + part
 
 
 def placed(loads, place):
@@ -229,7 +245,16 @@
     devices = lax.axis_size("leaf")
     device = lax.axis_index("leaf")
     bits = devices.bit_length() - 1
-    return [devices - (devices >> (h - 1)) + (device >> h) for h in range(1, bits)]
+
+    def row_at(height, node):
+        return devices - (devices >> (height - 1)) + node
+
+    path = [row_at(1, device >> 1), row_at(2, device >> 2)]
+    for height in range(2, bits - 1, 2):
+        up = device >> (height + 1)
+        path += [row_at(height + 1, up), row_at(height + 1, up ^ 1)]
+        path.append(row_at(min(height + 2, bits - 1), up >> 1))
+    return path
 
 
 def first_part(points, charges, order, owner, slot, *tables):
@@ -318,17 +343,19 @@
         tiles[count + u] = (empty << 8) | empty
 
     def step(g, carry):
-        values, weights = [], []
-        for u in range(FAR_UNROLL):
+        def entry(u):
             packed = tiles[g * FAR_UNROLL + u]
-            leaf = packed >> 16
-            first = (packed >> 8) & 255
-            second = packed & 255
-            matrix = jnp.concatenate([cols[first], cols[second]], axis=1)
-            load = jnp.concatenate([loads[first], loads[second]], axis=1)
-            values.append(jnp.exp(dot(rows[leaf], matrix)).astype(bf16))
-            weights.append(placed(load, leaf & 7))
-        acc[...] += dot_nt(jnp.concatenate(values, axis=1), jnp.concatenate(weights, axis=1))
+            return packed >> 16, (packed >> 8) & 255, packed & 255
+
+        def exponent(u):
+            leaf, first, second = entry(u)
+            return dot(rows[leaf], jnp.concatenate([cols[first], cols[second]], axis=1))
+
+        def weight(u):
+            leaf, first, second = entry(u)
+            return placed(jnp.concatenate([loads[first], loads[second]], axis=1), leaf & 7)
+
+        acc[...] += tiles_sum(FAR_UNROLL, exponent, weight)
         return carry
 
     acc[...] = jnp.zeros_like(acc)
@@ -426,12 +453,8 @@
     if done < acc.shape[0]:
         acc[done:] = jnp.zeros((acc.shape[0] - done,) + acc.shape[1:], f32)
     if makes:
-        if phase > 0:
-            list_pairs(codes, [None] * phase + [table] + tables)
-            lists = lists + [table]
-        else:
-            list_pairs(codes, [None] + tables)
-
+        list_pairs(codes, [None] * phase + [table] + tables)
+        lists = lists + [table]
     counts = [jnp.int32(0)] * len(NEAR_STEPS)
     base = jnp.int32(0)
     for number, pairs in enumerate(lists):
@@ -470,26 +493,27 @@
 
         def step(i, carry, k=k, size=size):
             start = steps[k, i]
-            values, weights = [], []
             group = (flat[start] >> 19) & 31
-            for u in range(size):
+
+            def exponent(u):
                 packed = flat[start + u]
                 target = (packed >> 16) & 7
-                source = packed & 65535
-                place = jnp.where(packed < DUMMY, target, 8)
+                coords = sources[packed & 65535, :64, :]
                 odd = target & 1
-                both = sources[source]
-                coords = both[:64]
                 zero = jnp.zeros_like(coords)
                 matrix = jnp.concatenate(
                     [jnp.where(odd == 0, coords, zero), jnp.where(odd == 1, coords, zero)],
                     axis=0,
                 )
                 at = pl.multiple_of(group * 1024 + (target >> 1) * 256, 256)
-                value = dot(targets[pl.ds(at, 256), :], matrix) - norm_row(coords)
-                values.append(jnp.exp(value).astype(bf16))
-                weights.append(placed(both[64:], place))
-            acc[group] += dot_nt(jnp.concatenate(values, axis=1), jnp.concatenate(weights, axis=1))
+                return dot(targets[pl.ds(at, 256), :], matrix) - norm_row(coords)
+
+            def weight(u):
+                packed = flat[start + u]
+                place = jnp.where(packed < DUMMY, (packed >> 16) & 7, 8)
+                return placed(sources[packed & 65535, 64:, :], place)
+
+            acc[group] += tiles_sum(size, exponent, weight)
             return carry
 
         lax.fori_loop(0, counts[k], step, 0)
@@ -568,6 +592,31 @@
     )(me, own, other, skels, interps)
 
 
+def climb_two_kernel(me, own, one, two, three, skels, interps, sibling, parent, *, height, row):
+    node = me[0] >> height
+    is_left = (node & 1) == 0
+    left, right = ordered(own[...], one[...], is_left)
+    mine = combine(left, right, skels[row], interps[row])
+    left, right = ordered(two[...], three[...], is_left)
+    other = combine(left, right, skels[row + 1], interps[row + 1])
+    sibling[...] = other
+    left, right = ordered(mine, other, (node & 2) == 0)
+    parent[...] = combine(left, right, skels[row + 2], interps[row + 2])
+
+
+def climb_two(me, own, others, skels, interps, height, row):
+    node = jax.ShapeDtypeStruct((80, 128), bf16)
+    return pl.pallas_call(
+        functools.partial(climb_two_kernel, height=height, row=row),
+        out_shape=(node, node),
+        in_specs=[SMEM] + [VMEM] * 6,
+        out_specs=(VMEM, VMEM),
+        compiler_params=params(),
+        cost_estimate=cost(),
+        name=f"climb{height}",
+    )(me, own, *others, skels, interps)
+
+
 def top_kernel(*refs):
     parts, (rows, acc, cols, loads) = refs[:-4], refs[-4:]
     for t, part in enumerate(parts):
@@ -576,10 +625,16 @@
         loads[:, t * 128 : (t + 1) * 128] = jnp.concatenate([node[64:]] * 8, axis=0)
     lane = lax.broadcasted_iota(jnp.int32, (256, 128), 1) >> 4
 
+    levels = len(parts)
+    spans = [slice(c * 128, min(c + 2, levels) * 128) for c in range(0, levels, 2)]
+
     def two_leaves(i, carry):
         both = rows[pl.ds(2 * i, 2)].reshape(512, 128)
-        value = jnp.exp(dot(both, cols[...])).astype(bf16)
-        result = dot_nt(value, loads[...])
+        result = tiles_sum(
+            len(spans),
+            lambda u: dot(both, cols[:, spans[u]]),
+            lambda u: loads[:, spans[u]],
+        )
         group = lax.div(i, 4)
         place = (2 * i) & 7
         acc[group] += jnp.where(lane == place, result[:256], 0.0) + jnp.where(
@@ -742,9 +797,9 @@
     sums, far_tables1, far_tables2 = near(
         0,
         [tables[0] for tables in lists],
-        targets[:2],
+        targets[:3],
         [pieces[k] for k in wanted if k == 1 or not k & 1],
-        codes=payload_codes(after(far_away, far1), 1),
+        codes=payload_codes(after(far_away, far1), 0),
     )
     node = climb(me, node, after(siblings[1], sums), skels, interps, 1, 1)
     for k in wanted[2::2]:
@@ -755,7 +810,8 @@
             place = spread(low, early_bits[:n]) | late
             pieces[place | 2**b] = swap(pieces[place], 2**b)
     pieces[late | 1] = swap(pieces[late], 1)
-    siblings.append(swap(node, 4))
+    height, row = 2, 2
+    others = [swap(node, k * 2**height) for k in (1, 2, 3)]
     sums, last_table = near(
         1,
         [tables[1] for tables in lists] + [far_tables1],
@@ -764,21 +820,28 @@
         codes=payload_codes(after(last_targets, node), 1),
         before=sums,
     )
-    node = climb(me, node, after(siblings[2], sums), skels, interps, 2, 2)
-    siblings.append(swap(node, 8))
+    others[0] = after(others[0], sums)
+    while height + 1 < bits:
+        if height > 2:
+            others = [swap(node, k * 2**height) for k in (1, 2, 3)]
+        sibling, node = climb_two(me, node, others, skels, interps, height, row)
+        siblings += [others[0], sibling]
+        height, row = height + 2, row + 3
+    if height < bits:
+        siblings.append(swap(node, 2**height))
     for k in wanted[2::2]:
         pieces[k | late | 1] = swap(after(pieces[k | late], node), 1)
     parts = near(
         2,
-        [tables[2] for tables in lists] + [far_tables2, last_table],
+        [tables[2] for tables in lists] + [far_tables2, after(last_table, node)],
         targets,
         [pieces[k | late] for k in wanted[2:]],
         before=sums,
     )
-    for height in range(3, bits - 1):
-        node = climb(me, node, after(siblings[height], parts[0]), skels, interps, height, height)
-        siblings.append(swap(node, 2 ** (height + 1)))
-    received = [parts[0]] + [swap(after(parts[k], node), spread(k, TARGET_BITS)) for k in mates]
+    siblings[-1] = after(siblings[-1], parts[0])
+    received = [parts[0]] + [
+        swap(after(parts[k], siblings[-1]), spread(k, TARGET_BITS)) for k in mates
+    ]
     above = top(siblings, after(rows, parts[0]))
     return last((far0, far1), above, norms, received)
 

time: 92.4 us -> 88.7 us (0.960)
  waiting for transfers between devices: 13.5 us -> 7.23 us
  Pallas kernels: 57.5 us -> 59 us
    ppermute x17 -> x18, waiting for transfers between devices: 13.5 us -> 7.23 us  [swap(): return lax.ppermute(value, 'leaf', pairs)]
    pallas_call x1, Pallas kernels: 10.4 us -> 12.5 us  [first_part(): pl.pallas_call(first_kernel, out_shape=tuple((jax.ShapeDtypeStruct(*shape...]
    pallas_call x2, Pallas kernels: 17 us -> 15.5 us  [self_and_far(): pl.pallas_call(functools.partial(far_kernel, first_leaf=call * n_leaves,...]
    ppermute x17 -> x18, starting transfers between devices: 18.2 us -> 19.1 us  [swap(): return lax.ppermute(value, 'leaf', pairs)]
  transfers between devices with their start and end apart: 17 -> 18, of which waited for: 4 -> 6; matrix products, arithmetic and copies ran while one was open for 1% -> 2% of each run, Pallas kernels for 50% -> 52%
where the time goes in v1:
time: 88.7 us; the launch traced here: 87.8 us
  Pallas kernels  59 us (67%)
  starting transfers between devices  19.1 us (22%)
  waiting for transfers between devices  7.23 us (8%)
  other arithmetic  1.33 us (1%)
    pallas_call x3, Pallas kernels, near(): pl.pallas_call(functools.partial(near_kernel, n_sources=n_sources, n_targ...  25.1 us
    ppermute x18, starting transfers between devices, swap(): return lax.ppermute(value, 'leaf', pairs)  19.1 us
    pallas_call x2, Pallas kernels, self_and_far(): pl.pallas_call(functools.partial(far_kernel, first_leaf=call * n_leaves,...  15.5 us
    pallas_call x1, Pallas kernels, first_part(): pl.pallas_call(first_kernel, out_shape=tuple((jax.ShapeDtypeStruct(*shape...  12.5 us
    ppermute x18, waiting for transfers between devices, swap(): return lax.ppermute(value, 'leaf', pairs)  7.23 us
    pallas_call x1, Pallas kernels, top(): pl.pallas_call(top_kernel, out_shape=jax.ShapeDtypeStruct((rows.shape[0]...  4.4 us
  transfers between devices with their start and end apart: 18, of which 6 were waited for; matrix products, arithmetic and copies ran while one was open for 2% of the time, Pallas kernels for 52%

profile of v1, /device:TPU:0, one launch (start us, length us, event | category | flops | bytes accessed | tf_op | source)
XLA Modules:
  0.0 87.8 jit_solution(10066965086917424427)
XLA Ops:
  0.0 12.5 %order_and_subtree.1 = (bf16[16,80,256]{2,1,0:T(8,128)(2,1)}, bf16[2064,128]{1,0:T(8,128)(2,1)}, bf16[64,128,128]{2,1,0:T(8,128)(2,1)}, bf16[64,16,128]{2,1,0:T(...) custom-call(s32[4096]{0:T(1024)} %order.1, ...), custom_call_target="tpu_custom_call" | custom-call | flops 1 | bytes 1 | tf_op jit(solution)/shard_map/order_and_subtree/pallas_call | solution.py:295
  12.5 3.0 %collective-permute-start = (bf16[2064,128]{1,0:T(8,128)(2,1)}, bf16[2064,128]{1,0:T(8,128)(2,1)S(1)}, u32[]{:S(2)}, u32[]{:S(2)}) collective-permute-start(bf16[2064,128]{1,0:T(8,128)(2,1)} %get-tuple-element.56.refs_3_.refs_4_), channel_id=1, source_target_pairs={{0,2},{1,3},{2,0},{3,1},{4,6},{5,7},{6,4},{7,5},{8,10},{9,11},{10,... | collective-permute-start | bytes 1585160 | tf_op jit(solution)/shard_map/ppermute | solution.py:709
  15.5 1.6 %collective-permute-start.3 = (bf16[2064,128]{1,0:T(8,128)(2,1)}, bf16[2064,128]{1,0:T(8,128)(2,1)S(1)}, u32[]{:S(2)}, u32[]{:S(2)}) collective-permute-start(bf16[2064,128]{1,0:T(8,128)(2,1)} %get-tuple-element.56.refs_3_.refs_4_), channel_id=1, source_target_pairs={{0,8},{1,9},{2,10},{3,11},{4,12},{5,13},{6,14},{7,15},{8,0},{9,1},... | collective-permute-start | bytes 1585160 | tf_op jit(solution)/shard_map/ppermute | solution.py:709
  17.1 1.5 %collective-permute-start.4 = (bf16[16,80,256]{2,1,0:T(8,128)(2,1)}, bf16[16,80,256]{2,1,0:T(8,128)(2,1)S(1)}, u32[]{:S(2)}, u32[]{:S(2)}) collective-permute-start(bf16[16,80,256]{2,1,0:T(8,128)(2,1)} %get-tuple-element.67.refs_6_.refs_8_), channel_id=1, source_target_pairs={{0,4},{1,5},{2,6},{3,7},{4,0},{5,1},{6,2},{7,3},{8,12},{9,13},{10,... | collective-permute-start | bytes 1966088 | tf_op jit(solution)/shard_map/ppermute | solution.py:709
  18.6 2.6 %collective-permute-start.8 = (bf16[16,80,256]{2,1,0:T(8,128)(2,1)}, bf16[16,80,256]{2,1,0:T(8,128)(2,1)}, u32[]{:S(2)}, u32[]{:S(2)}) collective-permute-start(bf16[16,80,256]{2,1,0:T(8,128)(2,1)} %get-tuple-element.67.refs_6_.refs_8_), channel_id=1, source_target_pairs={{0,16},{1,17},{2,18},{3,19},{4,20},{5,21},{6,22},{7,23},{8,24},{9,... | collective-permute-start | bytes 1966088 | tf_op jit(solution)/shard_map/ppermute | solution.py:709
  21.2 0.6 fusion.6.refs_0_
  21.8 7.7 %self_and_far0.1 = (f32[256,128]{1,0:T(8,128)}, s32[2,128]{1,0:T(2,128)}, s32[2,128]{1,0:T(2,128)}, s32[2,128]{1,0:T(2,128)}) custom-call(s32[8,16]{1,0:T(8,128)} %fusion.6.refs_0_, s32[16,16]{1,0:T(8,128)} %refs_1_.1, s32[16]{0:T(128)} %refs_2_.3, bf16[64,128,128]{2,1,0:T(8,128)(2,1)} %get-tuple-element.52.refs_3_, ...), custom_call_target="tpu_custom_call" | custom-call | flops 1 | bytes 1 | tf_op jit(solution)/shard_map/self_and_far0/pallas_call | solution.py:396
  29.6 0.6 fusion.13.refs_0_
  30.2 0.1 climb0.1.own
  30.5 7.8 %self_and_far1.1 = (f32[256,128]{1,0:T(8,128)}, s32[2,128]{1,0:T(2,128)}, s32[2,128]{1,0:T(2,128)}, s32[2,128]{1,0:T(2,128)}) custom-call(s32[8,16]{1,0:T(8,128)} %fusion.13.refs_0_, s32[16,16]{1,0:T(8,128)} %refs_1_.1, s32[16]{0:T(128)} %refs_2_.3, bf16[64,128,128]{2,1,0:T(8,128)(2,1)} %get-tuple-element.52.refs_3_, ...), custom_call_target="tpu_custom_call" | custom-call | flops 1 | bytes 1 | tf_op jit(solution)/shard_map/self_and_far1/pallas_call | solution.py:396
  38.4 0.8 collective-permute-done.3.refs_5_.refs_6_
  39.1 1.2 %collective-permute-start.6 = (bf16[2064,128]{1,0:T(8,128)(2,1)S(1)}, bf16[2064,128]{1,0:T(8,128)(2,1)S(1)}, u32[]{:S(2)}, u32[]{:S(2)}) collective-permute-start(bf16[2064,128]{1,0:T(8,128)(2,1)S(1)} %collective-permute-done.3.refs_5_.refs_6_), channel_id=1, source_target_pairs={{0,2},{1,3},{2,0},{3,1},{4,6},{5,7},{6,4},{7,5},{8,10},{9,11},{10,... | collective-permute-start | bytes 1585160 | tf_op jit(solution)/shard_map/ppermute | solution.py:709
  40.4 0.7 copy-done.14
  41.1 8.2 %near0.1 = (f32[6,256,128]{2,1,0:T(8,128)S(1)}, s32[2,128]{1,0:T(2,128)S(1)}, s32[2,128]{1,0:T(2,128)S(1)}) custom-call(s32[8,16]{1,0:T(8,128)S(1)} %fusion.20.refs_0_, s32[2,128]{1,0:T(2,128)S(1)} %copy-done.13, s32[2,128]{1,0:T(2,128)S(1)} %copy-done.14, bf16[2064,128]{1,0:T(8,128)(2,1)S(1)} %copy-done.1, ...), custom_call_target="tpu_custom_call" | custom-call | flops 1 | bytes 1 | tf_op jit(solution)/shard_map/near0/pallas_call | solution.py:551
  49.3 0.1 climb1.1.own
  49.4 0.1 collective-permute-done.8.refs_12_
  49.6 0.6 collective-permute-start.9
  50.3 1.3 %collective-permute-start.13 = (bf16[16,80,256]{2,1,0:T(8,128)(2,1)}, bf16[16,80,256]{2,1,0:T(8,128)(2,1)S(1)}, u32[]{:S(2)}, u32[]{:S(2)}) collective-permute-start(bf16[16,80,256]{2,1,0:T(8,128)(2,1)} %collective-permute-done.8.refs_12_), channel_id=1, source_target_pairs={{0,4},{1,5},{2,6},{3,7},{4,0},{5,1},{6,2},{7,3},{8,12},{9,13},{10,... | collective-permute-start | bytes 1966088 | tf_op jit(solution)/shard_map/ppermute | solution.py:709
  51.5 0.8 collective-permute-start.5
  52.3 0.8 collective-permute-done.6.refs_7_
  53.2 2.6 %collective-permute-start.11 = (bf16[80,128]{1,0:T(8,128)(2,1)S(1)}, bf16[80,128]{1,0:T(8,128)(2,1)S(1)}, u32[]{:S(2)}, u32[]{:S(2)}) collective-permute-start(bf16[80,128]{1,0:T(8,128)(2,1)S(1)} %climb1.1.own), channel_id=1, source_target_pairs={{0,12},{1,13},{2,14},{3,15},{4,8},{5,9},{6,10},{7,11},{8,4},{9,5},... | collective-permute-start | bytes 61448 | tf_op jit(solution)/shard_map/ppermute | solution.py:709
  55.9 11.6 %near1.1 = (f32[8,256,128]{2,1,0:T(8,128)S(1)}, s32[2,128]{1,0:T(2,128)S(1)}) custom-call(s32[8,16]{1,0:T(8,128)S(1)} %fusion.22.refs_0_, s32[2,128]{1,0:T(2,128)S(1)} %copy-done.11, s32[2,128]{1,0:T(2,128)S(1)} %copy-done.12, s32[2,128]{1,0:T(2,128)S(1)} %get-tuple-element.73.refs_3_, bf16[2064,128]{1,0:T(8,128)(2,1)S(1)} %copy-done.1, ...), custom_call_target="tpu_custom_call" | custom-call | flops 1 | bytes 1 | tf_op jit(solution)/shard_map/near1/pallas_call | solution.py:551
  67.4 1.0 %collective-permute-done.5.one.refs_2_ = bf16[80,128]{1,0:T(8,128)(2,1)S(1)} collective-permute-done((bf16[80,128]{1,0:T(8,128)(2,1)S(1)}, bf16[80,128]{1,0:T(8,128)(2,1)S(1)}, u32[]{:S(2)}, u32[]{:S(2)}) %collective-permute-start.5) | collective-permute-done | bytes 20512 | tf_op jit(solution)/shard_map/ppermute | solution.py:709
  68.5 0.3 climb2.1
  68.9 2.0 %collective-permute-done.14.refs_9_ = bf16[16,80,256]{2,1,0:T(8,128)(2,1)S(1)} collective-permute-done((bf16[16,80,256]{2,1,0:T(8,128)(2,1)S(1)}, bf16[16,80,256]{2,1,0:T(8,128)(2,1)S(1)}, u32[]{:S(2)}, u32[]{:S(2)}) %collective-permute-start.14) | collective-permute-done | bytes 655392 | tf_op jit(solution)/shard_map/ppermute | solution.py:709
  70.9 5.4 %near2.1 = (bf16[2,256,128]{2,1,0:T(8,128)(2,1)S(1)}, bf16[2,256,128]{2,1,0:T(8,128)(2,1)S(1)}, bf16[2,256,128]{2,1,0:T(8,128)(2,1)S(1)}, bf16[2,256,128]{2,1,0:T(8,128)(2,1)S(1)}) custom-call(s32[2,128]{1,0:T(2,128)S(1)} %copy-done.9, s32[2,128]{1,0:T(2,128)S(1)} %copy-done.10, s32[2,128]{1,0:T(2,128)S(1)} %get-tuple-element.82.refs_2_, ...), custom_call_target="tpu_custom_call" | custom-call | flops 1 | bytes 1 | tf_op jit(solution)/shard_map/near2/pallas_call | solution.py:551
  76.4 2.5 %collective-permute-start.17 = (bf16[2,256,128]{2,1,0:T(8,128)(2,1)S(1)}, bf16[2,256,128]{2,1,0:T(8,128)(2,1)S(1)}, u32[]{:S(2)}, u32[]{:S(2)}) collective-permute-start(bf16[2,256,128]{2,1,0:T(8,128)(2,1)S(1)} %get-tuple-element.94), channel_id=1, source_target_pairs={{0,10},{1,11},{2,8},{3,9},{4,14},{5,15},{6,12},{7,13},{8,2},{9,3},... | collective-permute-start | bytes 393224 | tf_op jit(solution)/shard_map/ppermute | solution.py:709
  78.9 0.8 collective-permute-start.16
  79.7 0.3 collective-permute-start.15
  79.9 4.4 %top.1.refs_2_ = f32[2,256,128]{2,1,0:T(8,128)S(1)} custom-call(bf16[17,80,256]{2,1,0:T(8,128)(2,1)S(1)} %collective-permute-done.1.other.refs_7_.refs_9_.refs_0_, bf16[80,128]{1,0:T(8,128)(2,1)S(1)} %collective-permute-done.2.other.refs_1_, bf16[80,128]{1,0:T(8,128)(2,1)S(1)} %collective-permute-done.5.one.refs_2_, ...), custom_call_target="tpu_custom_call" | custom-call | flops 1 | bytes 1 | tf_op jit(solution)/shard_map/top/pallas_call | solution.py:651
  84.4 2.5 %collective-permute-done.16.refs_6_ = bf16[2,256,128]{2,1,0:T(8,128)(2,1)S(1)} collective-permute-done((bf16[2,256,128]{2,1,0:T(8,128)(2,1)S(1)}, bf16[2,256,128]{2,1,0:T(8,128)(2,1)S(1)}, u32[]{:S(2)}, u32[]{:S(2)}) %collective-permute-start.16) | collective-permute-done | bytes 131104 | tf_op jit(solution)/shard_map/ppermute | solution.py:709
  86.8 0.9 %last_sum.1 = f32[16,4096]{1,0:T(8,128)} custom-call(f32[256,128]{1,0:T(8,128)S(1)} %copy-done.5, f32[256,128]{1,0:T(8,128)S(1)} %copy-done.6, f32[2,256,128]{2,1,0:T(8,128)S(1)} %top.1.refs_2_, f32[16,1,256]{2,1,0:T(1,128)S(1)} %copy-done.8, bf16[2,256,128]{2,1,0:T(8,128)(2,1)S(1)} %get-tuple-element.86.refs_4_, ...), custom_call_target="tpu_custom_call" | custom-call | flops 1 | bytes 1 | tf_op jit(solution)/shard_map/last_sum/pallas_call | solution.py:688
  (57 shorter events, 0.5 us)
Async XLA Ops:
  0.0 21.2 %copy-start.15 = (s32[16,8]{0,1:T(8,128)S(1)}, s32[16,8]{0,1:T(8,128)}, u32[]{:S(2)}) copy-start(s32[16,8]{0,1:T(8,128)} %param.17) | copy-start | bytes 1540
  0.0 21.2 %copy-start.16 = (s32[16,8]{0,1:T(8,128)S(1)}, s32[16,8]{0,1:T(8,128)}, u32[]{:S(2)}) copy-start(s32[16,8]{0,1:T(8,128)} %param.16) | copy-start | bytes 1540
  12.5 17.7 %copy-start.2 = (bf16[5,256,128]{2,1,0:T(8,128)(2,1)S(1)}, bf16[5,256,128]{2,1,0:T(8,128)(2,1)}, u32[]{:S(2)}) copy-start(bf16[5,256,128]{2,1,0:T(8,128)(2,1)} %get-tuple-element.61.interps) | copy-start | bytes 983044
  12.5 17.7 %copy-start.4 = (bf16[17,80,256]{2,1,0:T(8,128)(2,1)S(1)}, bf16[17,80,256]{2,1,0:T(8,128)(2,1)}, u32[]{:S(2)}) copy-start(bf16[17,80,256]{2,1,0:T(8,128)(2,1)} %get-tuple-element.59.own) | copy-start | bytes 2088964
  12.5 17.7 %copy-start.7 = (s32[5,1,128]{2,1,0:T(1,128)S(1)}, s32[5,1,128]{2,1,0:T(1,128)}, u32[]{:S(2)}) copy-start(s32[5,1,128]{2,1,0:T(1,128)} %get-tuple-element.60.skels) | copy-start | bytes 7684
  12.5 17.1 %collective-permute-start = (bf16[2064,128]{1,0:T(8,128)(2,1)}, bf16[2064,128]{1,0:T(8,128)(2,1)S(1)}, u32[]{:S(2)}, u32[]{:S(2)}) collective-permute-start(bf16[2064,128]{1,0:T(8,128)(2,1)} %get-tuple-element.56.refs_3_.refs_4_), channel_id=1, source_target_pairs={{0,2},{1,3},{2,0},{3,1},{4,6},{5,7},{6,4},{7,5},{8,10},{9,11},{10,... | collective-permute-start | bytes 1585160 | tf_op jit(solution)/shard_map/ppermute | solution.py:709
  15.5 23.6 %collective-permute-start.3 = (bf16[2064,128]{1,0:T(8,128)(2,1)}, bf16[2064,128]{1,0:T(8,128)(2,1)S(1)}, u32[]{:S(2)}, u32[]{:S(2)}) collective-permute-start(bf16[2064,128]{1,0:T(8,128)(2,1)} %get-tuple-element.56.refs_3_.refs_4_), channel_id=1, source_target_pairs={{0,8},{1,9},{2,10},{3,11},{4,12},{5,13},{6,14},{7,15},{8,0},{9,1},... | collective-permute-start | bytes 1585160 | tf_op jit(solution)/shard_map/ppermute | solution.py:709
  17.1 23.3 %collective-permute-start.4 = (bf16[16,80,256]{2,1,0:T(8,128)(2,1)}, bf16[16,80,256]{2,1,0:T(8,128)(2,1)S(1)}, u32[]{:S(2)}, u32[]{:S(2)}) collective-permute-start(bf16[16,80,256]{2,1,0:T(8,128)(2,1)} %get-tuple-element.67.refs_6_.refs_8_), channel_id=1, source_target_pairs={{0,4},{1,5},{2,6},{3,7},{4,0},{5,1},{6,2},{7,3},{8,12},{9,13},{10,... | collective-permute-start | bytes 1966088 | tf_op jit(solution)/shard_map/ppermute | solution.py:709
  18.6 31.0 %collective-permute-start.8 = (bf16[16,80,256]{2,1,0:T(8,128)(2,1)}, bf16[16,80,256]{2,1,0:T(8,128)(2,1)}, u32[]{:S(2)}, u32[]{:S(2)}) collective-permute-start(bf16[16,80,256]{2,1,0:T(8,128)(2,1)} %get-tuple-element.67.refs_6_.refs_8_), channel_id=1, source_target_pairs={{0,16},{1,17},{2,18},{3,19},{4,20},{5,21},{6,22},{7,23},{8,24},{9,... | collective-permute-start | bytes 1966088 | tf_op jit(solution)/shard_map/ppermute | solution.py:709
  21.2 9.0 %collective-permute-start.1 = (bf16[17,80,256]{2,1,0:T(8,128)(2,1)}, bf16[17,80,256]{2,1,0:T(8,128)(2,1)S(1)}, u32[]{:S(2)}, u32[]{:S(2)}) collective-permute-start(bf16[17,80,256]{2,1,0:T(8,128)(2,1)} %get-tuple-element.59.own), channel_id=1, source_target_pairs={{0,1},{1,0},{2,3},{3,2},{4,5},{5,4},{6,7},{7,6},{8,9},{9,8},{10,11... | collective-permute-start | bytes 2088968 | tf_op jit(solution)/shard_map/ppermute | solution.py:709
  30.4 10.0 %copy-start.1 = (bf16[2064,128]{1,0:T(8,128)(2,1)S(1)}, bf16[2064,128]{1,0:T(8,128)(2,1)}, u32[]{:S(2)}) copy-start(bf16[2064,128]{1,0:T(8,128)(2,1)} %get-tuple-element.56.refs_3_.refs_4_) | copy-start | bytes 1585156
  30.4 10.0 %copy-start.3 = (bf16[16,80,256]{2,1,0:T(8,128)(2,1)S(1)}, bf16[16,80,256]{2,1,0:T(8,128)(2,1)}, u32[]{:S(2)}) copy-start(bf16[16,80,256]{2,1,0:T(8,128)(2,1)} %get-tuple-element.67.refs_6_.refs_8_) | copy-start | bytes 1966084
  30.4 18.8 %collective-permute-start.2 = (bf16[80,128]{1,0:T(8,128)(2,1)S(1)}, bf16[80,128]{1,0:T(8,128)(2,1)S(1)}, u32[]{:S(2)}, u32[]{:S(2)}) collective-permute-start(bf16[80,128]{1,0:T(8,128)(2,1)S(1)} %climb0.1.own), channel_id=1, source_target_pairs={{0,2},{1,3},{2,0},{3,1},{4,6},{5,7},{6,4},{7,5},{8,10},{9,11},{10,... | collective-permute-start | bytes 61448 | tf_op jit(solution)/shard_map/ppermute | solution.py:709
  38.3 17.5 %copy-start.11 = (s32[2,128]{1,0:T(2,128)S(1)}, s32[2,128]{1,0:T(2,128)}, u32[]{:S(2)}) copy-start(s32[2,128]{1,0:T(2,128)} %get-tuple-element.71.refs_1_) | copy-start | bytes 3076
  38.3 17.5 %copy-start.12 = (s32[2,128]{1,0:T(2,128)S(1)}, s32[2,128]{1,0:T(2,128)}, u32[]{:S(2)}) copy-start(s32[2,128]{1,0:T(2,128)} %get-tuple-element.72.refs_2_) | copy-start | bytes 3076
  39.1 13.9 %collective-permute-start.6 = (bf16[2064,128]{1,0:T(8,128)(2,1)S(1)}, bf16[2064,128]{1,0:T(8,128)(2,1)S(1)}, u32[]{:S(2)}, u32[]{:S(2)}) collective-permute-start(bf16[2064,128]{1,0:T(8,128)(2,1)S(1)} %collective-permute-done.3.refs_5_.refs_6_), channel_id=1, source_target_pairs={{0,2},{1,3},{2,0},{3,1},{4,6},{5,7},{6,4},{7,5},{8,10},{9,11},{10,... | collective-permute-start | bytes 1585160 | tf_op jit(solution)/shard_map/ppermute | solution.py:709
  49.6 3.6 %collective-permute-start.9 = (bf16[16,80,256]{2,1,0:T(8,128)(2,1)}, bf16[16,80,256]{2,1,0:T(8,128)(2,1)S(1)}, u32[]{:S(2)}, u32[]{:S(2)}) collective-permute-start(bf16[16,80,256]{2,1,0:T(8,128)(2,1)} %collective-permute-done.8.refs_12_), channel_id=1, source_target_pairs={{0,1},{1,0},{2,3},{3,2},{4,5},{5,4},{6,7},{7,6},{8,9},{9,8},{10,11... | collective-permute-start | bytes 1966088 | tf_op jit(solution)/shard_map/ppermute | solution.py:709
  50.2 5.6 %collective-permute-start.7 = (bf16[16,80,256]{2,1,0:T(8,128)(2,1)S(1)}, bf16[16,80,256]{2,1,0:T(8,128)(2,1)S(1)}, u32[]{:S(2)}, u32[]{:S(2)}) collective-permute-start(bf16[16,80,256]{2,1,0:T(8,128)(2,1)S(1)} %collective-permute-done.4.refs_8_.refs_10_), channel_id=1, source_target_pairs={{0,1},{1,0},{2,3},{3,2},{4,5},{5,4},{6,7},{7,6},{8,9},{9,8},{10,11... | collective-permute-start | bytes 1966088 | tf_op jit(solution)/shard_map/ppermute | solution.py:709
  50.3 18.5 %collective-permute-start.13 = (bf16[16,80,256]{2,1,0:T(8,128)(2,1)}, bf16[16,80,256]{2,1,0:T(8,128)(2,1)S(1)}, u32[]{:S(2)}, u32[]{:S(2)}) collective-permute-start(bf16[16,80,256]{2,1,0:T(8,128)(2,1)} %collective-permute-done.8.refs_12_), channel_id=1, source_target_pairs={{0,4},{1,5},{2,6},{3,7},{4,0},{5,1},{6,2},{7,3},{8,12},{9,13},{10,... | collective-permute-start | bytes 1966088 | tf_op jit(solution)/shard_map/ppermute | solution.py:709
  51.5 16.9 %collective-permute-start.5 = (bf16[80,128]{1,0:T(8,128)(2,1)S(1)}, bf16[80,128]{1,0:T(8,128)(2,1)S(1)}, u32[]{:S(2)}, u32[]{:S(2)}) collective-permute-start(bf16[80,128]{1,0:T(8,128)(2,1)S(1)} %climb1.1.own), channel_id=1, source_target_pairs={{0,4},{1,5},{2,6},{3,7},{4,0},{5,1},{6,2},{7,3},{8,12},{9,13},{10,... | collective-permute-start | bytes 61448 | tf_op jit(solution)/shard_map/ppermute | solution.py:709
  53.1 15.4 %collective-permute-start.10 = (bf16[80,128]{1,0:T(8,128)(2,1)S(1)}, bf16[80,128]{1,0:T(8,128)(2,1)S(1)}, u32[]{:S(2)}, u32[]{:S(2)}) collective-permute-start(bf16[80,128]{1,0:T(8,128)(2,1)S(1)} %climb1.1.own), channel_id=1, source_target_pairs={{0,8},{1,9},{2,10},{3,11},{4,12},{5,13},{6,14},{7,15},{8,0},{9,1},... | collective-permute-start | bytes 61448 | tf_op jit(solution)/shard_map/ppermute | solution.py:709
  53.2 15.3 %collective-permute-start.11 = (bf16[80,128]{1,0:T(8,128)(2,1)S(1)}, bf16[80,128]{1,0:T(8,128)(2,1)S(1)}, u32[]{:S(2)}, u32[]{:S(2)}) collective-permute-start(bf16[80,128]{1,0:T(8,128)(2,1)S(1)} %climb1.1.own), channel_id=1, source_target_pairs={{0,12},{1,13},{2,14},{3,15},{4,8},{5,9},{6,10},{7,11},{8,4},{9,5},... | collective-permute-start | bytes 61448 | tf_op jit(solution)/shard_map/ppermute | solution.py:709
  55.9 15.1 %copy-start.9 = (s32[2,128]{1,0:T(2,128)S(1)}, s32[2,128]{1,0:T(2,128)}, u32[]{:S(2)}) copy-start(s32[2,128]{1,0:T(2,128)} %get-tuple-element.80.refs_0_) | copy-start | bytes 3076
  55.9 15.1 %copy-start.10 = (s32[2,128]{1,0:T(2,128)S(1)}, s32[2,128]{1,0:T(2,128)}, u32[]{:S(2)}) copy-start(s32[2,128]{1,0:T(2,128)} %get-tuple-element.81.refs_1_) | copy-start | bytes 3076
  68.8 2.2 %collective-permute-start.14 = (bf16[16,80,256]{2,1,0:T(8,128)(2,1)S(1)}, bf16[16,80,256]{2,1,0:T(8,128)(2,1)S(1)}, u32[]{:S(2)}, u32[]{:S(2)}) collective-permute-start(bf16[16,80,256]{2,1,0:T(8,128)(2,1)S(1)} %collective-permute-done.13.refs_8_), channel_id=1, source_target_pairs={{0,1},{1,0},{2,3},{3,2},{4,5},{5,4},{6,7},{7,6},{8,9},{9,8},{10,11... | collective-permute-start | bytes 1966088 | tf_op jit(solution)/shard_map/ppermute | solution.py:709
  68.8 7.5 %collective-permute-start.12 = (bf16[80,128]{1,0:T(8,128)(2,1)S(1)}, bf16[80,128]{1,0:T(8,128)(2,1)S(1)}, u32[]{:S(2)}, u32[]{:S(2)}) collective-permute-start(bf16[80,128]{1,0:T(8,128)(2,1)S(1)} %get-tuple-element.79), channel_id=1, source_target_pairs={{0,16},{1,17},{2,18},{3,19},{4,20},{5,21},{6,22},{7,23},{8,24},{9,... | collective-permute-start | bytes 61448 | tf_op jit(solution)/shard_map/ppermute | solution.py:709
  76.3 10.5 %copy-start.5 = (f32[256,128]{1,0:T(8,128)S(1)}, f32[256,128]{1,0:T(8,128)}, u32[]{:S(2)}) copy-start(f32[256,128]{1,0:T(8,128)} %get-tuple-element.55.refs_0_) | copy-start | bytes 393220
  76.3 10.5 %copy-start.6 = (f32[256,128]{1,0:T(8,128)S(1)}, f32[256,128]{1,0:T(8,128)}, u32[]{:S(2)}) copy-start(f32[256,128]{1,0:T(8,128)} %get-tuple-element.63.refs_1_) | copy-start | bytes 393220
  76.4 10.5 %copy-start.8 = (f32[16,1,256]{2,1,0:T(1,128)S(1)}, f32[16,1,256]{2,1,0:T(1,128)}, u32[]{:S(2)}) copy-start(f32[16,1,256]{2,1,0:T(1,128)} %get-tuple-element.50.refs_3_) | copy-start | bytes 49156
  76.4 8.0 %collective-permute-start.17 = (bf16[2,256,128]{2,1,0:T(8,128)(2,1)S(1)}, bf16[2,256,128]{2,1,0:T(8,128)(2,1)S(1)}, u32[]{:S(2)}, u32[]{:S(2)}) collective-permute-start(bf16[2,256,128]{2,1,0:T(8,128)(2,1)S(1)} %get-tuple-element.94), channel_id=1, source_target_pairs={{0,10},{1,11},{2,8},{3,9},{4,14},{5,15},{6,12},{7,13},{8,2},{9,3},... | collective-permute-start | bytes 393224 | tf_op jit(solution)/shard_map/ppermute | solution.py:709
  78.9 8.0 %collective-permute-start.16 = (bf16[2,256,128]{2,1,0:T(8,128)(2,1)S(1)}, bf16[2,256,128]{2,1,0:T(8,128)(2,1)S(1)}, u32[]{:S(2)}, u32[]{:S(2)}) collective-permute-start(bf16[2,256,128]{2,1,0:T(8,128)(2,1)S(1)} %get-tuple-element.92), channel_id=1, source_target_pairs={{0,8},{1,9},{2,10},{3,11},{4,12},{5,13},{6,14},{7,15},{8,0},{9,1},... | collective-permute-start | bytes 393224 | tf_op jit(solution)/shard_map/ppermute | solution.py:709
  79.7 7.2 %collective-permute-start.15 = (bf16[2,256,128]{2,1,0:T(8,128)(2,1)S(1)}, bf16[2,256,128]{2,1,0:T(8,128)(2,1)S(1)}, u32[]{:S(2)}, u32[]{:S(2)}) collective-permute-start(bf16[2,256,128]{2,1,0:T(8,128)(2,1)S(1)} %get-tuple-element.90), channel_id=1, source_target_pairs={{0,2},{1,3},{2,0},{3,1},{4,6},{5,7},{6,4},{7,5},{8,10},{9,11},{10,... | collective-permute-start | bytes 393224 | tf_op jit(solution)/shard_map/ppermute | solution.py:709
  (3 other events, 19.6 us)

commit v2 on v1

--- a/solution.py
+++ b/solution.py
@@ -118,7 +118,7 @@
     leaf_interp_in, leaf_skel_in, inner_interp_in, inner_skel_in, top_interp, top_skel,
     src_out, tgt_out, cols_out, loads_out, rows_out, norms_out, mine_out, interps_out, skels_out,
     points, charges, owner, slot, unsorted, buffer0, buffer1, src, tgt, cols, loads, rows, norms,
-    joined, root, leaf_interp, leaf_skel, inner_interp, inner_skel, sems,
+    joined, root, interps, skels, leaf_interp, leaf_skel, inner_interp, inner_skel, sems,
 ):
     count = points.shape[1]
     chunks = 4
@@ -144,9 +144,10 @@
     ]
     rest = []
     path = path_rows()
+    on_path = []
     for k in range(interps_out.shape[0]):
-        rest.append(begin(top_interp.at[path[k]], interps_out.at[k]))
-        rest.append(begin(top_skel.at[pl.ds(path[k], 1)], skels_out.at[k]))
+        on_path.append(begin(top_interp.at[path[k]], interps.at[k]))
+        on_path.append(begin(top_skel.at[pl.ds(path[k], 1)], skels.at[k]))
 
     parts[0].wait()
     for c in range(count // 128):
@@ -210,8 +211,9 @@
 
     lax.fori_loop(0, leaves // 4, two_pairs, 0)
     process(leaves // 2 - 1, buffer1)
-    for copy in near_lists:
+    for copy in near_lists + on_path:
         copy.wait()
+    rest += [begin(interps, interps_out), begin(skels, skels_out)]
     near = jnp.concatenate([owner[...].astype(f32), slot[...].astype(f32)], axis=0)
     blank = jnp.zeros((near.shape[0], 128 - near.shape[1]), f32)
     tgt[count // 2 :, :] = jnp.concatenate([near, blank], axis=1).astype(bf16)
@@ -291,6 +293,7 @@
     ]
     held += shapes[:6]
     held += [((2 * leaves - 1, 80, 128), bf16), ((80, 256), bf16)]
+    held += shapes[7:]
     held += [(table.shape, table.dtype) for table in tables[:4]]
     return pl.pallas_call(
         first_kernel,
@@ -298,7 +301,7 @@
         in_specs=[SMEM] + [ANY] * 10,
         out_specs=(ANY,) * 9,
         scratch_shapes=[pltpu.VMEM(*shape) for shape in held]
-        + [pltpu.SemaphoreType.DMA((20 + 2 * steps,))],
+        + [pltpu.SemaphoreType.DMA((24 + 2 * steps,))],
         compiler_params=params(FIRST_LIMIT),
         cost_estimate=cost(),
         name="order_and_subtree",
@@ -343,19 +346,17 @@
         tiles[count + u] = (empty << 8) | empty
 
     def step(g, carry):
-        def entry(u):
+        values, weights = [], []
+        for u in range(FAR_UNROLL):
             packed = tiles[g * FAR_UNROLL + u]
-            return packed >> 16, (packed >> 8) & 255, packed & 255
-
-        def exponent(u):
-            leaf, first, second = entry(u)
-            return dot(rows[leaf], jnp.concatenate([cols[first], cols[second]], axis=1))
-
-        def weight(u):
-            leaf, first, second = entry(u)
-            return placed(jnp.concatenate([loads[first], loads[second]], axis=1), leaf & 7)
-
-        acc[...] += tiles_sum(FAR_UNROLL, exponent, weight)
+            leaf = packed >> 16
+            first = (packed >> 8) & 255
+            second = packed & 255
+            matrix = jnp.concatenate([cols[first], cols[second]], axis=1)
+            load = jnp.concatenate([loads[first], loads[second]], axis=1)
+            values.append(jnp.exp(dot(rows[leaf], matrix)).astype(bf16))
+            weights.append(placed(load, leaf & 7))
+        acc[...] += dot_nt(jnp.concatenate(values, axis=1), jnp.concatenate(weights, axis=1))
         return carry
 
     acc[...] = jnp.zeros_like(acc)
@@ -625,16 +626,10 @@
         loads[:, t * 128 : (t + 1) * 128] = jnp.concatenate([node[64:]] * 8, axis=0)
     lane = lax.broadcasted_iota(jnp.int32, (256, 128), 1) >> 4
 
-    levels = len(parts)
-    spans = [slice(c * 128, min(c + 2, levels) * 128) for c in range(0, levels, 2)]
-
     def two_leaves(i, carry):
         both = rows[pl.ds(2 * i, 2)].reshape(512, 128)
-        result = tiles_sum(
-            len(spans),
-            lambda u: dot(both, cols[:, spans[u]]),
-            lambda u: loads[:, spans[u]],
-        )
+        value = jnp.exp(dot(both, cols[...])).astype(bf16)
+        result = dot_nt(value, loads[...])
         group = lax.div(i, 4)
         place = (2 * i) & 7
         acc[group] += jnp.where(lane == place, result[:256], 0.0) + jnp.where(

time: 88.7 us -> 87.8 us (0.990)
  Pallas kernels: 59 us -> 53.7 us
  starting transfers between devices: 19.1 us -> 21.8 us
  waiting for transfers between devices: 7.23 us -> 8.41 us
    ppermute x18, starting transfers between devices: 19.1 us -> 21.8 us  [swap(): return lax.ppermute(value, 'leaf', pairs)]
    pallas_call x3, Pallas kernels: 25.1 us -> 22.9 us  [near(): pl.pallas_call(functools.partial(near_kernel, n_sources=n_sources, n_targ...]
    pallas_call x1, Pallas kernels: 12.5 us -> 10.6 us  [first_part(): pl.pallas_call(first_kernel, out_shape=tuple((jax.ShapeDtypeStruct(*shape...]
    ppermute x18, waiting for transfers between devices: 7.23 us -> 8.41 us  [swap(): return lax.ppermute(value, 'leaf', pairs)]
  transfers between devices with their start and end apart: 18 -> 18, of which waited for: 6 -> 6; matrix products, arithmetic and copies ran while one was open for 2% -> 2% of each run, Pallas kernels for 52% -> 49%
where the time goes in v2:
time: 87.8 us; the launch traced here: 86.3 us
  Pallas kernels  53.7 us (61%)
  starting transfers between devices  21.8 us (25%)
  waiting for transfers between devices  8.41 us (10%)
  other arithmetic  1.33 us (2%)
    pallas_call x3, Pallas kernels, near(): pl.pallas_call(functools.partial(near_kernel, n_sources=n_sources, n_targ...  22.9 us
    ppermute x18, starting transfers between devices, swap(): return lax.ppermute(value, 'leaf', pairs)  21.8 us
    pallas_call x2, Pallas kernels, self_and_far(): pl.pallas_call(functools.partial(far_kernel, first_leaf=call * n_leaves,...  14.8 us
    pallas_call x1, Pallas kernels, first_part(): pl.pallas_call(first_kernel, out_shape=tuple((jax.ShapeDtypeStruct(*shape...  10.6 us
    ppermute x18, waiting for transfers between devices, swap(): return lax.ppermute(value, 'leaf', pairs)  8.41 us
    pallas_call x1, Pallas kernels, top(): pl.pallas_call(top_kernel, out_shape=jax.ShapeDtypeStruct((rows.shape[0]...  3.88 us
  transfers between devices with their start and end apart: 18, of which 6 were waited for; matrix products, arithmetic and copies ran while one was open for 2% of the time, Pallas kernels for 49%

profile of v2, /device:TPU:0, one launch (start us, length us, event | category | flops | bytes accessed | tf_op | source)
XLA Modules:
  0.0 86.3 jit_solution(9693941644339909894)
XLA Ops:
  0.0 10.6 %order_and_subtree.1 = (bf16[16,80,256]{2,1,0:T(8,128)(2,1)}, bf16[2064,128]{1,0:T(8,128)(2,1)}, bf16[64,128,128]{2,1,0:T(8,128)(2,1)}, bf16[64,16,128]{2,1,0:T(...) custom-call(s32[4096]{0:T(1024)} %order.1, ...), custom_call_target="tpu_custom_call" | custom-call | flops 1 | bytes 1 | tf_op jit(solution)/shard_map/order_and_subtree/pallas_call | solution.py:298
  10.7 3.0 %collective-permute-start = (bf16[2064,128]{1,0:T(8,128)(2,1)}, bf16[2064,128]{1,0:T(8,128)(2,1)S(1)}, u32[]{:S(2)}, u32[]{:S(2)}) collective-permute-start(bf16[2064,128]{1,0:T(8,128)(2,1)} %get-tuple-element.56.refs_3_.refs_4_), channel_id=1, source_target_pairs={{0,2},{1,3},{2,0},{3,1},{4,6},{5,7},{6,4},{7,5},{8,10},{9,11},{10,... | collective-permute-start | bytes 1585160 | tf_op jit(solution)/shard_map/ppermute | solution.py:704
  13.7 1.6 %collective-permute-start.3 = (bf16[2064,128]{1,0:T(8,128)(2,1)}, bf16[2064,128]{1,0:T(8,128)(2,1)S(1)}, u32[]{:S(2)}, u32[]{:S(2)}) collective-permute-start(bf16[2064,128]{1,0:T(8,128)(2,1)} %get-tuple-element.56.refs_3_.refs_4_), channel_id=1, source_target_pairs={{0,8},{1,9},{2,10},{3,11},{4,12},{5,13},{6,14},{7,15},{8,0},{9,1},... | collective-permute-start | bytes 1585160 | tf_op jit(solution)/shard_map/ppermute | solution.py:704
  15.3 1.5 %collective-permute-start.4 = (bf16[16,80,256]{2,1,0:T(8,128)(2,1)}, bf16[16,80,256]{2,1,0:T(8,128)(2,1)S(1)}, u32[]{:S(2)}, u32[]{:S(2)}) collective-permute-start(bf16[16,80,256]{2,1,0:T(8,128)(2,1)} %get-tuple-element.67.refs_6_.refs_8_), channel_id=1, source_target_pairs={{0,4},{1,5},{2,6},{3,7},{4,0},{5,1},{6,2},{7,3},{8,12},{9,13},{10,... | collective-permute-start | bytes 1966088 | tf_op jit(solution)/shard_map/ppermute | solution.py:704
  16.8 2.6 %collective-permute-start.8 = (bf16[16,80,256]{2,1,0:T(8,128)(2,1)}, bf16[16,80,256]{2,1,0:T(8,128)(2,1)}, u32[]{:S(2)}, u32[]{:S(2)}) collective-permute-start(bf16[16,80,256]{2,1,0:T(8,128)(2,1)} %get-tuple-element.67.refs_6_.refs_8_), channel_id=1, source_target_pairs={{0,16},{1,17},{2,18},{3,19},{4,20},{5,21},{6,22},{7,23},{8,24},{9,... | collective-permute-start | bytes 1966088 | tf_op jit(solution)/shard_map/ppermute | solution.py:704
  19.4 0.6 fusion.6.refs_0_
  20.0 6.7 %self_and_far0.1 = (f32[256,128]{1,0:T(8,128)}, s32[2,128]{1,0:T(2,128)}, s32[2,128]{1,0:T(2,128)}, s32[2,128]{1,0:T(2,128)}) custom-call(s32[8,16]{1,0:T(8,128)} %fusion.6.refs_0_, s32[16,16]{1,0:T(8,128)} %refs_1_.1, s32[16]{0:T(128)} %refs_2_.3, bf16[64,128,128]{2,1,0:T(8,128)(2,1)} %get-tuple-element.52.refs_3_, ...), custom_call_target="tpu_custom_call" | custom-call | flops 1 | bytes 1 | tf_op jit(solution)/shard_map/self_and_far0/pallas_call | solution.py:397
  26.8 0.6 fusion.13.refs_0_
  27.6 1.0 %collective-permute-start.2 = (bf16[80,128]{1,0:T(8,128)(2,1)S(1)}, bf16[80,128]{1,0:T(8,128)(2,1)S(1)}, u32[]{:S(2)}, u32[]{:S(2)}) collective-permute-start(bf16[80,128]{1,0:T(8,128)(2,1)S(1)} %climb0.1.own), channel_id=1, source_target_pairs={{0,2},{1,3},{2,0},{3,1},{4,6},{5,7},{6,4},{7,5},{8,10},{9,11},{10,... | collective-permute-start | bytes 61448 | tf_op jit(solution)/shard_map/ppermute | solution.py:704
  28.6 8.1 %self_and_far1.1 = (f32[256,128]{1,0:T(8,128)}, s32[2,128]{1,0:T(2,128)}, s32[2,128]{1,0:T(2,128)}, s32[2,128]{1,0:T(2,128)}) custom-call(s32[8,16]{1,0:T(8,128)} %fusion.13.refs_0_, s32[16,16]{1,0:T(8,128)} %refs_1_.1, s32[16]{0:T(128)} %refs_2_.3, bf16[64,128,128]{2,1,0:T(8,128)(2,1)} %get-tuple-element.52.refs_3_, ...), custom_call_target="tpu_custom_call" | custom-call | flops 1 | bytes 1 | tf_op jit(solution)/shard_map/self_and_far1/pallas_call | solution.py:397
  36.7 0.6 collective-permute-done.3.refs_5_.refs_6_
  37.3 0.4 collective-permute-start.6
  37.8 0.7 copy-done.14
  38.5 7.4 %near0.1 = (f32[6,256,128]{2,1,0:T(8,128)S(1)}, s32[2,128]{1,0:T(2,128)S(1)}, s32[2,128]{1,0:T(2,128)S(1)}) custom-call(s32[8,16]{1,0:T(8,128)S(1)} %fusion.20.refs_0_, s32[2,128]{1,0:T(2,128)S(1)} %copy-done.13, s32[2,128]{1,0:T(2,128)S(1)} %copy-done.14, bf16[2064,128]{1,0:T(8,128)(2,1)S(1)} %copy-done.1, ...), custom_call_target="tpu_custom_call" | custom-call | flops 1 | bytes 1 | tf_op jit(solution)/shard_map/near0/pallas_call | solution.py:552
  46.0 1.7 %collective-permute-done.8.refs_12_ = bf16[16,80,256]{2,1,0:T(8,128)(2,1)} collective-permute-done((bf16[16,80,256]{2,1,0:T(8,128)(2,1)}, bf16[16,80,256]{2,1,0:T(8,128)(2,1)}, u32[]{:S(2)}, u32[]{:S(2)}) %collective-permute-start.8) | collective-permute-done | bytes 655392 | tf_op jit(solution)/shard_map/ppermute | solution.py:704
  47.7 0.5 collective-permute-start.7
  48.3 0.5 collective-permute-start.13
  48.8 1.5 %collective-permute-start.5 = (bf16[80,128]{1,0:T(8,128)(2,1)S(1)}, bf16[80,128]{1,0:T(8,128)(2,1)S(1)}, u32[]{:S(2)}, u32[]{:S(2)}) collective-permute-start(bf16[80,128]{1,0:T(8,128)(2,1)S(1)} %climb1.1.own), channel_id=1, source_target_pairs={{0,4},{1,5},{2,6},{3,7},{4,0},{5,1},{6,2},{7,3},{8,12},{9,13},{10,... | collective-permute-start | bytes 61448 | tf_op jit(solution)/shard_map/ppermute | solution.py:704
  50.3 0.8 collective-permute-done.6.refs_7_
  51.1 0.5 collective-permute-start.10
  51.6 2.4 %collective-permute-start.11 = (bf16[80,128]{1,0:T(8,128)(2,1)S(1)}, bf16[80,128]{1,0:T(8,128)(2,1)S(1)}, u32[]{:S(2)}, u32[]{:S(2)}) collective-permute-start(bf16[80,128]{1,0:T(8,128)(2,1)S(1)} %climb1.1.own), channel_id=1, source_target_pairs={{0,12},{1,13},{2,14},{3,15},{4,8},{5,9},{6,10},{7,11},{8,4},{9,5},... | collective-permute-start | bytes 61448 | tf_op jit(solution)/shard_map/ppermute | solution.py:704
  54.1 9.9 %near1.1 = (f32[8,256,128]{2,1,0:T(8,128)S(1)}, s32[2,128]{1,0:T(2,128)S(1)}) custom-call(s32[8,16]{1,0:T(8,128)S(1)} %fusion.22.refs_0_, s32[2,128]{1,0:T(2,128)S(1)} %copy-done.11, s32[2,128]{1,0:T(2,128)S(1)} %copy-done.12, s32[2,128]{1,0:T(2,128)S(1)} %get-tuple-element.73.refs_3_, bf16[2064,128]{1,0:T(8,128)(2,1)S(1)} %copy-done.1, ...), custom_call_target="tpu_custom_call" | custom-call | flops 1 | bytes 1 | tf_op jit(solution)/shard_map/near1/pallas_call | solution.py:552
  64.0 2.0 %collective-permute-done.5.one.refs_2_ = bf16[80,128]{1,0:T(8,128)(2,1)S(1)} collective-permute-done((bf16[80,128]{1,0:T(8,128)(2,1)S(1)}, bf16[80,128]{1,0:T(8,128)(2,1)S(1)}, u32[]{:S(2)}, u32[]{:S(2)}) %collective-permute-start.5) | collective-permute-done | bytes 20512 | tf_op jit(solution)/shard_map/ppermute | solution.py:704
  66.0 0.3 climb2.1
  66.6 1.9 %collective-permute-done.14.refs_9_ = bf16[16,80,256]{2,1,0:T(8,128)(2,1)S(1)} collective-permute-done((bf16[16,80,256]{2,1,0:T(8,128)(2,1)S(1)}, bf16[16,80,256]{2,1,0:T(8,128)(2,1)S(1)}, u32[]{:S(2)}, u32[]{:S(2)}) %collective-permute-start.14) | collective-permute-done | bytes 655392 | tf_op jit(solution)/shard_map/ppermute | solution.py:704
  68.5 5.7 %near2.1 = (bf16[2,256,128]{2,1,0:T(8,128)(2,1)S(1)}, bf16[2,256,128]{2,1,0:T(8,128)(2,1)S(1)}, bf16[2,256,128]{2,1,0:T(8,128)(2,1)S(1)}, bf16[2,256,128]{2,1,0:T(8,128)(2,1)S(1)}) custom-call(s32[2,128]{1,0:T(2,128)S(1)} %copy-done.9, s32[2,128]{1,0:T(2,128)S(1)} %copy-done.10, s32[2,128]{1,0:T(2,128)S(1)} %get-tuple-element.82.refs_2_, ...), custom_call_target="tpu_custom_call" | custom-call | flops 1 | bytes 1 | tf_op jit(solution)/shard_map/near2/pallas_call | solution.py:552
  74.2 2.7 %collective-permute-start.17 = (bf16[2,256,128]{2,1,0:T(8,128)(2,1)S(1)}, bf16[2,256,128]{2,1,0:T(8,128)(2,1)S(1)}, u32[]{:S(2)}, u32[]{:S(2)}) collective-permute-start(bf16[2,256,128]{2,1,0:T(8,128)(2,1)S(1)} %get-tuple-element.94), channel_id=1, source_target_pairs={{0,10},{1,11},{2,8},{3,9},{4,14},{5,15},{6,12},{7,13},{8,2},{9,3},... | collective-permute-start | bytes 393224 | tf_op jit(solution)/shard_map/ppermute | solution.py:704
  76.9 1.9 %collective-permute-start.16 = (bf16[2,256,128]{2,1,0:T(8,128)(2,1)S(1)}, bf16[2,256,128]{2,1,0:T(8,128)(2,1)S(1)}, u32[]{:S(2)}, u32[]{:S(2)}) collective-permute-start(bf16[2,256,128]{2,1,0:T(8,128)(2,1)S(1)} %get-tuple-element.92), channel_id=1, source_target_pairs={{0,8},{1,9},{2,10},{3,11},{4,12},{5,13},{6,14},{7,15},{8,0},{9,1},... | collective-permute-start | bytes 393224 | tf_op jit(solution)/shard_map/ppermute | solution.py:704
  78.8 1.4 %collective-permute-start.15 = (bf16[2,256,128]{2,1,0:T(8,128)(2,1)S(1)}, bf16[2,256,128]{2,1,0:T(8,128)(2,1)S(1)}, u32[]{:S(2)}, u32[]{:S(2)}) collective-permute-start(bf16[2,256,128]{2,1,0:T(8,128)(2,1)S(1)} %get-tuple-element.90), channel_id=1, source_target_pairs={{0,2},{1,3},{2,0},{3,1},{4,6},{5,7},{6,4},{7,5},{8,10},{9,11},{10,... | collective-permute-start | bytes 393224 | tf_op jit(solution)/shard_map/ppermute | solution.py:704
  80.2 3.9 %top.1.refs_2_ = f32[2,256,128]{2,1,0:T(8,128)S(1)} custom-call(bf16[17,80,256]{2,1,0:T(8,128)(2,1)S(1)} %collective-permute-done.1.other.refs_7_.refs_9_.refs_0_, bf16[80,128]{1,0:T(8,128)(2,1)S(1)} %collective-permute-done.2.other.refs_1_, bf16[80,128]{1,0:T(8,128)(2,1)S(1)} %collective-permute-done.5.one.refs_2_, ...), custom_call_target="tpu_custom_call" | custom-call | flops 1 | bytes 1 | tf_op jit(solution)/shard_map/top/pallas_call | solution.py:646
  84.1 1.3 %collective-permute-done.16.refs_6_ = bf16[2,256,128]{2,1,0:T(8,128)(2,1)S(1)} collective-permute-done((bf16[2,256,128]{2,1,0:T(8,128)(2,1)S(1)}, bf16[2,256,128]{2,1,0:T(8,128)(2,1)S(1)}, u32[]{:S(2)}, u32[]{:S(2)}) %collective-permute-start.16) | collective-permute-done | bytes 131104 | tf_op jit(solution)/shard_map/ppermute | solution.py:704
  85.4 0.9 %last_sum.1 = f32[16,4096]{1,0:T(8,128)} custom-call(f32[256,128]{1,0:T(8,128)S(1)} %copy-done.5, f32[256,128]{1,0:T(8,128)S(1)} %copy-done.6, f32[2,256,128]{2,1,0:T(8,128)S(1)} %top.1.refs_2_, f32[16,1,256]{2,1,0:T(1,128)S(1)} %copy-done.8, bf16[2,256,128]{2,1,0:T(8,128)(2,1)S(1)} %get-tuple-element.86.refs_4_, ...), custom_call_target="tpu_custom_call" | custom-call | flops 1 | bytes 1 | tf_op jit(solution)/shard_map/last_sum/pallas_call | solution.py:683
  (57 shorter events, 0.8 us)
Async XLA Ops:
  0.0 19.4 %copy-start.15 = (s32[16,8]{0,1:T(8,128)S(1)}, s32[16,8]{0,1:T(8,128)}, u32[]{:S(2)}) copy-start(s32[16,8]{0,1:T(8,128)} %param.17) | copy-start | bytes 1540
  0.0 19.4 %copy-start.16 = (s32[16,8]{0,1:T(8,128)S(1)}, s32[16,8]{0,1:T(8,128)}, u32[]{:S(2)}) copy-start(s32[16,8]{0,1:T(8,128)} %param.16) | copy-start | bytes 1540
  10.7 16.7 %copy-start.2 = (bf16[5,256,128]{2,1,0:T(8,128)(2,1)S(1)}, bf16[5,256,128]{2,1,0:T(8,128)(2,1)}, u32[]{:S(2)}) copy-start(bf16[5,256,128]{2,1,0:T(8,128)(2,1)} %get-tuple-element.61.interps) | copy-start | bytes 983044
  10.7 16.7 %copy-start.4 = (bf16[17,80,256]{2,1,0:T(8,128)(2,1)S(1)}, bf16[17,80,256]{2,1,0:T(8,128)(2,1)}, u32[]{:S(2)}) copy-start(bf16[17,80,256]{2,1,0:T(8,128)(2,1)} %get-tuple-element.59.own) | copy-start | bytes 2088964
  10.7 16.7 %copy-start.7 = (s32[5,1,128]{2,1,0:T(1,128)S(1)}, s32[5,1,128]{2,1,0:T(1,128)}, u32[]{:S(2)}) copy-start(s32[5,1,128]{2,1,0:T(1,128)} %get-tuple-element.60.skels) | copy-start | bytes 7684
  10.7 16.0 %collective-permute-start = (bf16[2064,128]{1,0:T(8,128)(2,1)}, bf16[2064,128]{1,0:T(8,128)(2,1)S(1)}, u32[]{:S(2)}, u32[]{:S(2)}) collective-permute-start(bf16[2064,128]{1,0:T(8,128)(2,1)} %get-tuple-element.56.refs_3_.refs_4_), channel_id=1, source_target_pairs={{0,2},{1,3},{2,0},{3,1},{4,6},{5,7},{6,4},{7,5},{8,10},{9,11},{10,... | collective-permute-start | bytes 1585160 | tf_op jit(solution)/shard_map/ppermute | solution.py:704
  13.7 23.6 %collective-permute-start.3 = (bf16[2064,128]{1,0:T(8,128)(2,1)}, bf16[2064,128]{1,0:T(8,128)(2,1)S(1)}, u32[]{:S(2)}, u32[]{:S(2)}) collective-permute-start(bf16[2064,128]{1,0:T(8,128)(2,1)} %get-tuple-element.56.refs_3_.refs_4_), channel_id=1, source_target_pairs={{0,8},{1,9},{2,10},{3,11},{4,12},{5,13},{6,14},{7,15},{8,0},{9,1},... | collective-permute-start | bytes 1585160 | tf_op jit(solution)/shard_map/ppermute | solution.py:704
  15.3 22.5 %collective-permute-start.4 = (bf16[16,80,256]{2,1,0:T(8,128)(2,1)}, bf16[16,80,256]{2,1,0:T(8,128)(2,1)S(1)}, u32[]{:S(2)}, u32[]{:S(2)}) collective-permute-start(bf16[16,80,256]{2,1,0:T(8,128)(2,1)} %get-tuple-element.67.refs_6_.refs_8_), channel_id=1, source_target_pairs={{0,4},{1,5},{2,6},{3,7},{4,0},{5,1},{6,2},{7,3},{8,12},{9,13},{10,... | collective-permute-start | bytes 1966088 | tf_op jit(solution)/shard_map/ppermute | solution.py:704
  16.8 31.0 %collective-permute-start.8 = (bf16[16,80,256]{2,1,0:T(8,128)(2,1)}, bf16[16,80,256]{2,1,0:T(8,128)(2,1)}, u32[]{:S(2)}, u32[]{:S(2)}) collective-permute-start(bf16[16,80,256]{2,1,0:T(8,128)(2,1)} %get-tuple-element.67.refs_6_.refs_8_), channel_id=1, source_target_pairs={{0,16},{1,17},{2,18},{3,19},{4,20},{5,21},{6,22},{7,23},{8,24},{9,... | collective-permute-start | bytes 1966088 | tf_op jit(solution)/shard_map/ppermute | solution.py:704
  19.4 8.0 %collective-permute-start.1 = (bf16[17,80,256]{2,1,0:T(8,128)(2,1)}, bf16[17,80,256]{2,1,0:T(8,128)(2,1)S(1)}, u32[]{:S(2)}, u32[]{:S(2)}) collective-permute-start(bf16[17,80,256]{2,1,0:T(8,128)(2,1)} %get-tuple-element.59.own), channel_id=1, source_target_pairs={{0,1},{1,0},{2,3},{3,2},{4,5},{5,4},{6,7},{7,6},{8,9},{9,8},{10,11... | collective-permute-start | bytes 2088968 | tf_op jit(solution)/shard_map/ppermute | solution.py:704
  27.6 10.2 %copy-start.1 = (bf16[2064,128]{1,0:T(8,128)(2,1)S(1)}, bf16[2064,128]{1,0:T(8,128)(2,1)}, u32[]{:S(2)}) copy-start(bf16[2064,128]{1,0:T(8,128)(2,1)} %get-tuple-element.56.refs_3_.refs_4_) | copy-start | bytes 1585156
  27.6 18.2 %collective-permute-start.2 = (bf16[80,128]{1,0:T(8,128)(2,1)S(1)}, bf16[80,128]{1,0:T(8,128)(2,1)S(1)}, u32[]{:S(2)}, u32[]{:S(2)}) collective-permute-start(bf16[80,128]{1,0:T(8,128)(2,1)S(1)} %climb0.1.own), channel_id=1, source_target_pairs={{0,2},{1,3},{2,0},{3,1},{4,6},{5,7},{6,4},{7,5},{8,10},{9,11},{10,... | collective-permute-start | bytes 61448 | tf_op jit(solution)/shard_map/ppermute | solution.py:704
  36.7 17.4 %copy-start.11 = (s32[2,128]{1,0:T(2,128)S(1)}, s32[2,128]{1,0:T(2,128)}, u32[]{:S(2)}) copy-start(s32[2,128]{1,0:T(2,128)} %get-tuple-element.71.refs_1_) | copy-start | bytes 3076
  36.7 17.4 %copy-start.12 = (s32[2,128]{1,0:T(2,128)S(1)}, s32[2,128]{1,0:T(2,128)}, u32[]{:S(2)}) copy-start(s32[2,128]{1,0:T(2,128)} %get-tuple-element.72.refs_2_) | copy-start | bytes 3076
  37.3 13.8 %collective-permute-start.6 = (bf16[2064,128]{1,0:T(8,128)(2,1)S(1)}, bf16[2064,128]{1,0:T(8,128)(2,1)S(1)}, u32[]{:S(2)}, u32[]{:S(2)}) collective-permute-start(bf16[2064,128]{1,0:T(8,128)(2,1)S(1)} %collective-permute-done.3.refs_5_.refs_6_), channel_id=1, source_target_pairs={{0,2},{1,3},{2,0},{3,1},{4,6},{5,7},{6,4},{7,5},{8,10},{9,11},{10,... | collective-permute-start | bytes 1585160 | tf_op jit(solution)/shard_map/ppermute | solution.py:704
  47.7 3.8 %collective-permute-start.9 = (bf16[16,80,256]{2,1,0:T(8,128)(2,1)}, bf16[16,80,256]{2,1,0:T(8,128)(2,1)S(1)}, u32[]{:S(2)}, u32[]{:S(2)}) collective-permute-start(bf16[16,80,256]{2,1,0:T(8,128)(2,1)} %collective-permute-done.8.refs_12_), channel_id=1, source_target_pairs={{0,1},{1,0},{2,3},{3,2},{4,5},{5,4},{6,7},{7,6},{8,9},{9,8},{10,11... | collective-permute-start | bytes 1966088 | tf_op jit(solution)/shard_map/ppermute | solution.py:704
  47.7 6.3 %collective-permute-start.7 = (bf16[16,80,256]{2,1,0:T(8,128)(2,1)S(1)}, bf16[16,80,256]{2,1,0:T(8,128)(2,1)S(1)}, u32[]{:S(2)}, u32[]{:S(2)}) collective-permute-start(bf16[16,80,256]{2,1,0:T(8,128)(2,1)S(1)} %collective-permute-done.4.refs_8_.refs_10_), channel_id=1, source_target_pairs={{0,1},{1,0},{2,3},{3,2},{4,5},{5,4},{6,7},{7,6},{8,9},{9,8},{10,11... | collective-permute-start | bytes 1966088 | tf_op jit(solution)/shard_map/ppermute | solution.py:704
  48.3 18.0 %collective-permute-start.13 = (bf16[16,80,256]{2,1,0:T(8,128)(2,1)}, bf16[16,80,256]{2,1,0:T(8,128)(2,1)S(1)}, u32[]{:S(2)}, u32[]{:S(2)}) collective-permute-start(bf16[16,80,256]{2,1,0:T(8,128)(2,1)} %collective-permute-done.8.refs_12_), channel_id=1, source_target_pairs={{0,4},{1,5},{2,6},{3,7},{4,0},{5,1},{6,2},{7,3},{8,12},{9,13},{10,... | collective-permute-start | bytes 1966088 | tf_op jit(solution)/shard_map/ppermute | solution.py:704
  48.8 17.2 %collective-permute-start.5 = (bf16[80,128]{1,0:T(8,128)(2,1)S(1)}, bf16[80,128]{1,0:T(8,128)(2,1)S(1)}, u32[]{:S(2)}, u32[]{:S(2)}) collective-permute-start(bf16[80,128]{1,0:T(8,128)(2,1)S(1)} %climb1.1.own), channel_id=1, source_target_pairs={{0,4},{1,5},{2,6},{3,7},{4,0},{5,1},{6,2},{7,3},{8,12},{9,13},{10,... | collective-permute-start | bytes 61448 | tf_op jit(solution)/shard_map/ppermute | solution.py:704
  51.1 14.9 %collective-permute-start.10 = (bf16[80,128]{1,0:T(8,128)(2,1)S(1)}, bf16[80,128]{1,0:T(8,128)(2,1)S(1)}, u32[]{:S(2)}, u32[]{:S(2)}) collective-permute-start(bf16[80,128]{1,0:T(8,128)(2,1)S(1)} %climb1.1.own), channel_id=1, source_target_pairs={{0,8},{1,9},{2,10},{3,11},{4,12},{5,13},{6,14},{7,15},{8,0},{9,1},... | collective-permute-start | bytes 61448 | tf_op jit(solution)/shard_map/ppermute | solution.py:704
  51.6 14.4 %collective-permute-start.11 = (bf16[80,128]{1,0:T(8,128)(2,1)S(1)}, bf16[80,128]{1,0:T(8,128)(2,1)S(1)}, u32[]{:S(2)}, u32[]{:S(2)}) collective-permute-start(bf16[80,128]{1,0:T(8,128)(2,1)S(1)} %climb1.1.own), channel_id=1, source_target_pairs={{0,12},{1,13},{2,14},{3,15},{4,8},{5,9},{6,10},{7,11},{8,4},{9,5},... | collective-permute-start | bytes 61448 | tf_op jit(solution)/shard_map/ppermute | solution.py:704
  54.0 14.4 %copy-start.9 = (s32[2,128]{1,0:T(2,128)S(1)}, s32[2,128]{1,0:T(2,128)}, u32[]{:S(2)}) copy-start(s32[2,128]{1,0:T(2,128)} %get-tuple-element.80.refs_0_) | copy-start | bytes 3076
  54.1 14.4 %copy-start.10 = (s32[2,128]{1,0:T(2,128)S(1)}, s32[2,128]{1,0:T(2,128)}, u32[]{:S(2)}) copy-start(s32[2,128]{1,0:T(2,128)} %get-tuple-element.81.refs_1_) | copy-start | bytes 3076
  66.3 2.2 %collective-permute-start.14 = (bf16[16,80,256]{2,1,0:T(8,128)(2,1)S(1)}, bf16[16,80,256]{2,1,0:T(8,128)(2,1)S(1)}, u32[]{:S(2)}, u32[]{:S(2)}) collective-permute-start(bf16[16,80,256]{2,1,0:T(8,128)(2,1)S(1)} %collective-permute-done.13.refs_8_), channel_id=1, source_target_pairs={{0,1},{1,0},{2,3},{3,2},{4,5},{5,4},{6,7},{7,6},{8,9},{9,8},{10,11... | collective-permute-start | bytes 1966088 | tf_op jit(solution)/shard_map/ppermute | solution.py:704
  66.4 7.8 %collective-permute-start.12 = (bf16[80,128]{1,0:T(8,128)(2,1)S(1)}, bf16[80,128]{1,0:T(8,128)(2,1)S(1)}, u32[]{:S(2)}, u32[]{:S(2)}) collective-permute-start(bf16[80,128]{1,0:T(8,128)(2,1)S(1)} %get-tuple-element.79), channel_id=1, source_target_pairs={{0,16},{1,17},{2,18},{3,19},{4,20},{5,21},{6,22},{7,23},{8,24},{9,... | collective-permute-start | bytes 61448 | tf_op jit(solution)/shard_map/ppermute | solution.py:704
  68.5 11.8 %copy-start = (bf16[16,256,128]{2,1,0:T(8,128)(2,1)S(1)}, bf16[16,256,128]{2,1,0:T(8,128)(2,1)}, u32[]{:S(2)}) copy-start(bf16[16,256,128]{2,1,0:T(8,128)(2,1)} %get-tuple-element.88.refs_5_) | copy-start | bytes 3145732
  74.1 11.3 %copy-start.5 = (f32[256,128]{1,0:T(8,128)S(1)}, f32[256,128]{1,0:T(8,128)}, u32[]{:S(2)}) copy-start(f32[256,128]{1,0:T(8,128)} %get-tuple-element.55.refs_0_) | copy-start | bytes 393220
  74.2 11.3 %copy-start.6 = (f32[256,128]{1,0:T(8,128)S(1)}, f32[256,128]{1,0:T(8,128)}, u32[]{:S(2)}) copy-start(f32[256,128]{1,0:T(8,128)} %get-tuple-element.63.refs_1_) | copy-start | bytes 393220
  74.2 11.3 %copy-start.8 = (f32[16,1,256]{2,1,0:T(1,128)S(1)}, f32[16,1,256]{2,1,0:T(1,128)}, u32[]{:S(2)}) copy-start(f32[16,1,256]{2,1,0:T(1,128)} %get-tuple-element.50.refs_3_) | copy-start | bytes 49156
  74.2 9.9 %collective-permute-start.17 = (bf16[2,256,128]{2,1,0:T(8,128)(2,1)S(1)}, bf16[2,256,128]{2,1,0:T(8,128)(2,1)S(1)}, u32[]{:S(2)}, u32[]{:S(2)}) collective-permute-start(bf16[2,256,128]{2,1,0:T(8,128)(2,1)S(1)} %get-tuple-element.94), channel_id=1, source_target_pairs={{0,10},{1,11},{2,8},{3,9},{4,14},{5,15},{6,12},{7,13},{8,2},{9,3},... | collective-permute-start | bytes 393224 | tf_op jit(solution)/shard_map/ppermute | solution.py:704
  76.9 8.5 %collective-permute-start.16 = (bf16[2,256,128]{2,1,0:T(8,128)(2,1)S(1)}, bf16[2,256,128]{2,1,0:T(8,128)(2,1)S(1)}, u32[]{:S(2)}, u32[]{:S(2)}) collective-permute-start(bf16[2,256,128]{2,1,0:T(8,128)(2,1)S(1)} %get-tuple-element.92), channel_id=1, source_target_pairs={{0,8},{1,9},{2,10},{3,11},{4,12},{5,13},{6,14},{7,15},{8,0},{9,1},... | collective-permute-start | bytes 393224 | tf_op jit(solution)/shard_map/ppermute | solution.py:704
  78.8 6.6 %collective-permute-start.15 = (bf16[2,256,128]{2,1,0:T(8,128)(2,1)S(1)}, bf16[2,256,128]{2,1,0:T(8,128)(2,1)S(1)}, u32[]{:S(2)}, u32[]{:S(2)}) collective-permute-start(bf16[2,256,128]{2,1,0:T(8,128)(2,1)S(1)} %get-tuple-element.90), channel_id=1, source_target_pairs={{0,2},{1,3},{2,0},{3,1},{4,6},{5,7},{6,4},{7,5},{8,10},{9,11},{10,... | collective-permute-start | bytes 393224 | tf_op jit(solution)/shard_map/ppermute | solution.py:704
  (3 other events, 21.1 us)

commit v3 on v2

--- a/solution.py
+++ b/solution.py
@@ -8,8 +8,7 @@
 from jax.sharding import PartitionSpec as P
 
 TARGET_BITS = (1, 3)
-FAR_UNROLL = 8
-NEAR_STEPS = (8, 4, 2)
+STEPS = (8, 4, 2)
 DUMMY = 1 << 30
 PHASE_BIT = 24
 CODE = (1 << PHASE_BIT) - 1
@@ -113,12 +112,45 @@
     return jnp.concatenate([coords, load], axis=0)
 
 
+def spread(number, bits):
+    return sum(((number >> k) & 1) << b for k, b in enumerate(bits))
+
+
+def compress(number, bits):
+    return sum(((number >> b) & 1) << k for k, b in enumerate(bits))
+
+
+def codes_of(owner, slot, first, leaves):
+    bits = lax.axis_size("leaf").bit_length() - 1
+    source_bits = [b for b in range(bits) if b not in TARGET_BITS]
+    other = owner ^ lax.axis_index("leaf")
+    place = compress(other, source_bits) * leaves + slot
+    here = jnp.where((other & sum(2**b for b in TARGET_BITS)) == 0, 1, 0)
+    half = 2 ** (len(source_bits) - 1)
+    is_late = place >= half * leaves
+    place = place & (half * leaves - 1)
+    is_last = is_late & (place >= 2 * leaves)
+    piece = place >> (leaves.bit_length() - 1)
+    is_first = jnp.logical_not(is_late) & ((piece < 2) | ((piece & 1) == 0))
+    if first != 0:
+        is_first = is_first & (piece < 0)
+    phase = jnp.where(is_last, 2, jnp.where(is_first, 0, 1))
+    first_place = place - (piece - jnp.where(piece < 2, piece, (piece >> 1) + 1)) * leaves
+    place = jnp.where(
+        is_last,
+        place - 2 * leaves,
+        jnp.where(is_late, half * leaves + place, jnp.where(is_first, first_place, place)),
+    )
+    target = lax.broadcasted_iota(jnp.int32, owner.shape, 1) & 7
+    return (here << (phase + PHASE_BIT)) | (target << 16) | place
+
+
 def first_kernel(
     order, points_in, charges_in, owner_in, slot_in,
     leaf_interp_in, leaf_skel_in, inner_interp_in, inner_skel_in, top_interp, top_skel,
-    src_out, tgt_out, cols_out, loads_out, rows_out, norms_out, mine_out, interps_out, skels_out,
+    src_out, tgt_out, cols_out, loads_out, rows_out, norms_out, mine_out, interps_out, skels_out, codes_out,
     points, charges, owner, slot, unsorted, buffer0, buffer1, src, tgt, cols, loads, rows, norms,
-    joined, root, interps, skels, leaf_interp, leaf_skel, inner_interp, inner_skel, sems,
+    joined, root, interps, skels, codes, leaf_interp, leaf_skel, inner_interp, inner_skel, sems,
 ):
     count = points.shape[1]
     chunks = 4
@@ -213,7 +245,8 @@
     process(leaves // 2 - 1, buffer1)
     for copy in near_lists + on_path:
         copy.wait()
-    rest += [begin(interps, interps_out), begin(skels, skels_out)]
+    codes[...] = codes_of(owner[...], slot[...], 0, leaves)
+    rest += [begin(interps, interps_out), begin(skels, skels_out), begin(codes, codes_out)]
     near = jnp.concatenate([owner[...].astype(f32), slot[...].astype(f32)], axis=0)
     blank = jnp.zeros((near.shape[0], 128 - near.shape[1]), f32)
     tgt[count // 2 :, :] = jnp.concatenate([near, blank], axis=1).astype(bf16)
@@ -281,6 +314,7 @@
         ((leaves + 1, 80, 256), bf16),
         ((steps, 256, 128), bf16),
         ((steps, 1, 128), jnp.int32),
+        (owner.shape, jnp.int32),
     ]
     held = [
         (points.shape, bf16),
@@ -299,7 +333,7 @@
         first_kernel,
         out_shape=tuple(jax.ShapeDtypeStruct(*shape) for shape in shapes),
         in_specs=[SMEM] + [ANY] * 10,
-        out_specs=(ANY,) * 9,
+        out_specs=(ANY,) * 10,
         scratch_shapes=[pltpu.VMEM(*shape) for shape in held]
         + [pltpu.SemaphoreType.DMA((24 + 2 * steps,))],
         compiler_params=params(FIRST_LIMIT),
@@ -342,13 +376,13 @@
         return count
 
     count = lax.fori_loop(0, n_leaves, list_leaf, 0)
-    for u in range(FAR_UNROLL):
-        tiles[count + u] = (empty << 8) | empty
-
-    def step(g, carry):
+    tiles[count] = (empty << 8) | empty
+    count = (count + 1) & ~1
+
+    def step(start, size):
         values, weights = [], []
-        for u in range(FAR_UNROLL):
-            packed = tiles[g * FAR_UNROLL + u]
+        for u in range(size):
+            packed = tiles[start + u]
             leaf = packed >> 16
             first = (packed >> 8) & 255
             second = packed & 255
@@ -357,14 +391,25 @@
             values.append(jnp.exp(dot(rows[leaf], matrix)).astype(bf16))
             weights.append(placed(load, leaf & 7))
         acc[...] += dot_nt(jnp.concatenate(values, axis=1), jnp.concatenate(weights, axis=1))
-        return carry
 
     acc[...] = jnp.zeros_like(acc)
     for k in range(n_ids):
         list_pairs(codes[k], lists[PHASES * k : PHASES * k + PHASES])
     for copy in copies:
         copy.wait()
-    lax.fori_loop(0, lax.div(count + FAR_UNROLL - 1, FAR_UNROLL), step, 0)
+    largest = STEPS[0]
+    whole = lax.div(count, largest)
+
+    def full_step(i, carry):
+        step(i * largest, largest)
+        return carry
+
+    lax.fori_loop(0, whole, full_step, 0)
+    for size in STEPS[1:]:
+
+        @pl.when((count & size) > 0)
+        def _(size=size):
+            step(count & ~(2 * size - 1), size)
 
 
 def list_pairs(codes, tables):
@@ -405,7 +450,7 @@
             pltpu.VMEM(cols.shape, bf16),
             pltpu.VMEM(loads.shape, bf16),
             pltpu.VMEM(rows.shape, bf16),
-            pltpu.SMEM((n_leaves * (1 + width // 2) + 1 + FAR_UNROLL,), jnp.int32),
+            pltpu.SMEM((n_leaves * (1 + width // 2) + 2,), jnp.int32),
             pltpu.SemaphoreType.DMA((4,)),
         ],
         compiler_params=params(FIRST_LIMIT),
@@ -432,7 +477,7 @@
     outs = take(n_targets) if not makes else []
     (acc,) = take(1) if makes else (None,)
     tables = take(PHASES - 1 - phase) if makes else []
-    sources, targets, sems, table, flat, steps = take(6)
+    sources, targets, sems, pairs, steps = take(5)
     if not makes:
         (acc,) = refs
     leaves = source_parts[0].shape[0]
@@ -443,6 +488,9 @@
         copies.append(pltpu.make_async_copy(part, place, sems.at[len(copies)]))
         copies[-1].start()
 
+    own_rows = acc.shape[0] // n_targets
+    for k, part in enumerate(lists):
+        begin(part, pairs.at[pl.ds(k * own_rows, own_rows)])
     done = 0
     for part in before:
         done = part.shape[0]
@@ -454,50 +502,34 @@
     if done < acc.shape[0]:
         acc[done:] = jnp.zeros((acc.shape[0] - done,) + acc.shape[1:], f32)
     if makes:
+        table = pairs.at[pl.ds(n_lists * own_rows, own_rows)]
         list_pairs(codes, [None] * phase + [table] + tables)
-        lists = lists + [table]
-    counts = [jnp.int32(0)] * len(NEAR_STEPS)
-    base = jnp.int32(0)
-    for number, pairs in enumerate(lists):
-        for row in range(pairs.shape[0]):
-            group = number * pairs.shape[0] + row
-            used = pairs[row, 0]
-
-            def copy_pair(i, at, pairs=pairs, row=row, group=group):
-                flat[at + i] = pairs[row, 1 + i] | (group << 19)
-                return at
-
-            lax.fori_loop(0, used, copy_pair, base)
-            start = base
-            for k, size in enumerate(NEAR_STEPS):
-                if k == 0:
-                    whole = lax.div(used, size)
-
-                    def note(i, count, start=start, size=size):
-                        steps[0, count + i] = start + i * size
-                        return count
-
-                    lax.fori_loop(0, whole, note, counts[0])
-                    counts[0] = counts[0] + whole
-                    start = start + whole * size
-                else:
-                    steps[k, counts[k]] = start
-                    has = jnp.where((used & size) > 0, 1, 0)
-                    counts[k] = counts[k] + has
-                    start = start + has * size
-            base = base + used
-
     for copy in copies:
         copy.wait()
 
-    for k, size in enumerate(NEAR_STEPS):
+    counts = [jnp.int32(0)] * len(STEPS)
+    for row in range(pairs.shape[0]):
+        used = pairs[row, 0]
+        whole = lax.div(used, STEPS[0])
+
+        def note(i, count, row=row):
+            steps[0, count + i] = row * 128 + 1 + i * STEPS[0]
+            return count
+
+        lax.fori_loop(0, whole, note, counts[0])
+        counts[0] = counts[0] + whole
+        for k, size in enumerate(STEPS[1:], 1):
+            steps[k, counts[k]] = row * 128 + 1 + (used & ~(2 * size - 1))
+            counts[k] = counts[k] + jnp.where((used & size) > 0, 1, 0)
+
+    for k, size in enumerate(STEPS):
 
         def step(i, carry, k=k, size=size):
-            start = steps[k, i]
-            group = (flat[start] >> 19) & 31
+            group = steps[k, i] >> 7
+            start = steps[k, i] & 127
 
             def exponent(u):
-                packed = flat[start + u]
+                packed = pairs[group, start + u]
                 target = (packed >> 16) & 7
                 coords = sources[packed & 65535, :64, :]
                 odd = target & 1
@@ -510,7 +542,7 @@
                 return dot(targets[pl.ds(at, 256), :], matrix) - norm_row(coords)
 
             def weight(u):
-                packed = flat[start + u]
+                packed = pairs[group, start + u]
                 place = jnp.where(packed < DUMMY, (packed >> 16) & 7, 8)
                 return placed(sources[packed & 65535, 64:, :], place)
 
@@ -532,7 +564,7 @@
     makes = phase < PHASES - 1
     args = ([codes] if makes else []) + list(lists) + list(targets) + list(sources)
     args += [] if before is None else [before]
-    n_smem = len(lists) + makes
+    n_smem = int(makes)
     n_tables = PHASES - 1 - phase
     if makes:
         out_shape = (sums,) + (pair_table(leaves),) * n_tables
@@ -542,10 +574,9 @@
     scratch = [
         pltpu.VMEM((n_sources * leaves, 80, 256), bf16),
         pltpu.VMEM((n_targets * leaves * 128, 128), bf16),
-        pltpu.SemaphoreType.DMA((n_sources + n_targets + 1,)),
-        pltpu.SMEM(pair_table(leaves).shape, jnp.int32),
-        pltpu.SMEM((n_targets * leaves * 8,), jnp.int32),
-        pltpu.SMEM((len(NEAR_STEPS), n_targets * leaves), jnp.int32),
+        pltpu.SemaphoreType.DMA((n_sources + n_targets + len(lists) + 1,)),
+        pltpu.SMEM((n_targets * leaves // 8, 128), jnp.int32),
+        pltpu.SMEM((len(STEPS), n_targets * leaves), jnp.int32),
     ]
     if not makes:
         scratch.append(pltpu.VMEM(sums.shape, f32))
@@ -689,14 +720,6 @@
         cost_estimate=cost(),
         name="last_sum",
     )(*fars, above, norms, *received)
-
-
-def spread(number, bits):
-    return sum(((number >> k) & 1) << b for k, b in enumerate(bits))
-
-
-def compress(number, bits):
-    return sum(((number >> b) & 1) << k for k, b in enumerate(bits))
 
 
 def swap(value, mask):
@@ -734,33 +757,12 @@
     early_bits = outer_bits[:-1]
     late = 2 ** outer_bits[-1]
 
-    def codes_of(owner, slot, first):
-        other = owner ^ device
-        target_mask = sum(2**b for b in TARGET_BITS)
-        place = compress(other, source_bits) * leaves + slot
-        here = jnp.where((other & target_mask) == 0, 1, 0)
-        near_half = leaves << (len(source_bits) - 1)
-        is_late = place >= near_half
-        place = place & (near_half - 1)
-        is_last = is_late & (place >= 2 * leaves)
-        piece = place // leaves
-        is_first = ~is_late & (first == 0) & ((piece < 2) | (piece % 2 == 0))
-        phase = jnp.where(is_last, 2, jnp.where(is_first, 0, 1))
-        first_place = place - (piece - jnp.where(piece < 2, piece, piece // 2 + 1)) * leaves
-        place = jnp.where(
-            is_last,
-            place - 2 * leaves,
-            jnp.where(is_late, near_half + place, jnp.where(is_first, first_place, place)),
-        )
-        target = lax.broadcasted_iota(jnp.int32, owner.shape, 1) & 7
-        return (here << (phase + PHASE_BIT)) | (target << 16) | place
-
     def payload_codes(payload, first):
         near = payload[-2 * near_owner.shape[1] :, :leaves].astype(jnp.int32)
-        return codes_of(near[: near_owner.shape[1]], near[near_owner.shape[1] :], first)
+        return codes_of(near[: near_owner.shape[1]], near[near_owner.shape[1] :], first, leaves)
 
     owner, slot = near_owner.T, near_slot.T
-    src, tgt, cols, loads, rows, norms, mine, interps, skels = first_part(
+    src, tgt, cols, loads, rows, norms, mine, interps, skels, codes = first_part(
         points, charges, leaf_order, owner, slot,
         leaf_interp, leaf_skel, inner_interp, inner_skel, top_interp, top_skel,
     )
@@ -776,7 +778,7 @@
             codes, after(far_list, token), far_count, cols, loads, rows, call, 2
         )
 
-    far0, lists0 = far(0, [codes_of(owner, slot, 0)], norms)
+    far0, lists0 = far(0, [codes], norms)
     node = climb(me, after(mine, far0, beside), pieces[1], skels, interps, 0, 0)
     siblings = [pieces[1], swap(node, 2)]
     far1, lists1 = far(1, [payload_codes(after(beside, far0), 0)], node)

time: 87.8 us -> 86.9 us (0.990); the launches traced: 86.3 us -> 87.2 us
  waiting for transfers between devices: 8.41 us -> 10.8 us
  Pallas kernels: 53.7 us -> 51.9 us
    ppermute x18, waiting for transfers between devices: 8.41 us -> 10.8 us  [swap(): return lax.ppermute(value, 'leaf', pairs)]
    pallas_call x3, Pallas kernels: 22.9 us -> 21.4 us  [near(): pl.pallas_call(functools.partial(near_kernel, n_sources=n_sources, n_targ...]
  transfers between devices with their start and end apart: 18 -> 18, of which waited for: 6 -> 6; matrix products, arithmetic and copies ran while one was open for 2% -> 1% of each run, Pallas kernels for 49% -> 46%
where the time goes in v3:
time: 86.9 us; the launch traced here: 87.2 us
  Pallas kernels  51.9 us (60%)
  starting transfers between devices  22.6 us (26%)
  waiting for transfers between devices  10.8 us (12%)
    ppermute x18, starting transfers between devices, swap(): return lax.ppermute(value, 'leaf', pairs)  22.6 us
    pallas_call x3, Pallas kernels, near(): pl.pallas_call(functools.partial(near_kernel, n_sources=n_sources, n_targ...  21.4 us
    pallas_call x2, Pallas kernels, self_and_far(): pl.pallas_call(functools.partial(far_kernel, first_leaf=call * n_leaves,...  14.6 us
    ppermute x18, waiting for transfers between devices, swap(): return lax.ppermute(value, 'leaf', pairs)  10.8 us
    pallas_call x1, Pallas kernels, first_part(): pl.pallas_call(first_kernel, out_shape=tuple((jax.ShapeDtypeStruct(*shape...  10.5 us
    pallas_call x1, Pallas kernels, top(): pl.pallas_call(top_kernel, out_shape=jax.ShapeDtypeStruct((rows.shape[0]...  3.88 us
  transfers between devices with their start and end apart: 18, of which 6 were waited for; matrix products, arithmetic and copies ran while one was open for 1% of the time, Pallas kernels for 46%

profile of v3, /device:TPU:0, one launch (start us, length us, event | category | flops | bytes accessed | tf_op | source)
XLA Modules:
  0.0 87.2 jit_solution(1350577253693897770)
XLA Ops:
  0.0 10.5 %order_and_subtree.1 = (bf16[16,80,256]{2,1,0:T(8,128)(2,1)}, bf16[2064,128]{1,0:T(8,128)(2,1)}, bf16[64,128,128]{2,1,0:T(8,128)(2,1)}, bf16[64,16,128]{2,1,0:T(...) custom-call(s32[4096]{0:T(1024)} %order.1, ...), custom_call_target="tpu_custom_call" | custom-call | flops 1 | bytes 1 | tf_op jit(solution)/shard_map/order_and_subtree/pallas_call | solution.py:332
  10.6 3.0 %collective-permute-start = (bf16[2064,128]{1,0:T(8,128)(2,1)}, bf16[2064,128]{1,0:T(8,128)(2,1)S(1)}, u32[]{:S(2)}, u32[]{:S(2)}) collective-permute-start(bf16[2064,128]{1,0:T(8,128)(2,1)} %get-tuple-element.58.refs_3_.refs_4_), channel_id=1, source_target_pairs={{0,2},{1,3},{2,0},{3,1},{4,6},{5,7},{6,4},{7,5},{8,10},{9,11},{10,... | collective-permute-start | bytes 1585160 | tf_op jit(solution)/shard_map/ppermute | solution.py:727
  13.6 1.6 %collective-permute-start.3 = (bf16[2064,128]{1,0:T(8,128)(2,1)}, bf16[2064,128]{1,0:T(8,128)(2,1)S(1)}, u32[]{:S(2)}, u32[]{:S(2)}) collective-permute-start(bf16[2064,128]{1,0:T(8,128)(2,1)} %get-tuple-element.58.refs_3_.refs_4_), channel_id=1, source_target_pairs={{0,8},{1,9},{2,10},{3,11},{4,12},{5,13},{6,14},{7,15},{8,0},{9,1},... | collective-permute-start | bytes 1585160 | tf_op jit(solution)/shard_map/ppermute | solution.py:727
  15.2 1.5 %collective-permute-start.4 = (bf16[16,80,256]{2,1,0:T(8,128)(2,1)}, bf16[16,80,256]{2,1,0:T(8,128)(2,1)S(1)}, u32[]{:S(2)}, u32[]{:S(2)}) collective-permute-start(bf16[16,80,256]{2,1,0:T(8,128)(2,1)} %get-tuple-element.69.refs_6_.refs_8_), channel_id=1, source_target_pairs={{0,4},{1,5},{2,6},{3,7},{4,0},{5,1},{6,2},{7,3},{8,12},{9,13},{10,... | collective-permute-start | bytes 1966088 | tf_op jit(solution)/shard_map/ppermute | solution.py:727
  16.7 2.6 %collective-permute-start.8 = (bf16[16,80,256]{2,1,0:T(8,128)(2,1)}, bf16[16,80,256]{2,1,0:T(8,128)(2,1)}, u32[]{:S(2)}, u32[]{:S(2)}) collective-permute-start(bf16[16,80,256]{2,1,0:T(8,128)(2,1)} %get-tuple-element.69.refs_6_.refs_8_), channel_id=1, source_target_pairs={{0,16},{1,17},{2,18},{3,19},{4,20},{5,21},{6,22},{7,23},{8,24},{9,... | collective-permute-start | bytes 1966088 | tf_op jit(solution)/shard_map/ppermute | solution.py:727
  19.3 7.8 %self_and_far0.1 = (f32[256,128]{1,0:T(8,128)}, s32[2,128]{1,0:T(2,128)}, s32[2,128]{1,0:T(2,128)}, s32[2,128]{1,0:T(2,128)}) custom-call(s32[8,16]{1,0:T(8,128)} %get-tuple-element.51.refs_0_, s32[16,16]{1,0:T(8,128)} %refs_1_.1, s32[16]{0:T(128)} %refs_2_.3, bf16[64,128,128]{2,1,0:T(8,128)(2,1)} %get-tuple-element.54.refs_3_, ...), custom_call_target="tpu_custom_call" | custom-call | flops 1 | bytes 1 | tf_op jit(solution)/shard_map/self_and_far0/pallas_call | solution.py:442
  27.2 0.6 fusion.3.refs_0_
  27.8 0.1 climb0.1.own
  28.0 0.5 collective-permute-start.2
  28.4 6.8 %self_and_far1.1 = (f32[256,128]{1,0:T(8,128)}, s32[2,128]{1,0:T(2,128)}, s32[2,128]{1,0:T(2,128)}, s32[2,128]{1,0:T(2,128)}) custom-call(s32[8,16]{1,0:T(8,128)} %fusion.3.refs_0_, s32[16,16]{1,0:T(8,128)} %refs_1_.1, s32[16]{0:T(128)} %refs_2_.3, bf16[64,128,128]{2,1,0:T(8,128)(2,1)} %get-tuple-element.54.refs_3_, ...), custom_call_target="tpu_custom_call" | custom-call | flops 1 | bytes 1 | tf_op jit(solution)/shard_map/self_and_far1/pallas_call | solution.py:442
  35.3 2.9 %collective-permute-done.3.refs_5_.refs_6_ = bf16[2064,128]{1,0:T(8,128)(2,1)S(1)} collective-permute-done((bf16[2064,128]{1,0:T(8,128)(2,1)}, bf16[2064,128]{1,0:T(8,128)(2,1)S(1)}, u32[]{:S(2)}, u32[]{:S(2)}) %collective-permute-start.3) | collective-permute-done | bytes 528416 | tf_op jit(solution)/shard_map/ppermute | solution.py:727
  38.2 0.4 collective-permute-start.6
  38.6 0.7 copy-done.14
  39.3 7.4 %near0.1 = (f32[6,256,128]{2,1,0:T(8,128)S(1)}, s32[2,128]{1,0:T(2,128)S(1)}, s32[2,128]{1,0:T(2,128)S(1)}) custom-call(s32[8,16]{1,0:T(8,128)S(1)} %fusion.7.refs_0_, s32[2,128]{1,0:T(2,128)S(1)} %copy-done.13, s32[2,128]{1,0:T(2,128)S(1)} %copy-done.14, bf16[2064,128]{1,0:T(8,128)(2,1)S(1)} %copy-done.1, ...), custom_call_target="tpu_custom_call" | custom-call | flops 1 | bytes 1 | tf_op jit(solution)/shard_map/near0/pallas_call | solution.py:583
  46.7 0.1 climb1.1.own
  46.9 1.7 %collective-permute-done.8.refs_12_ = bf16[16,80,256]{2,1,0:T(8,128)(2,1)} collective-permute-done((bf16[16,80,256]{2,1,0:T(8,128)(2,1)}, bf16[16,80,256]{2,1,0:T(8,128)(2,1)}, u32[]{:S(2)}, u32[]{:S(2)}) %collective-permute-start.8) | collective-permute-done | bytes 655392 | tf_op jit(solution)/shard_map/ppermute | solution.py:727
  48.6 0.5 collective-permute-start.7
  49.1 1.8 %collective-permute-start.13 = (bf16[16,80,256]{2,1,0:T(8,128)(2,1)}, bf16[16,80,256]{2,1,0:T(8,128)(2,1)S(1)}, u32[]{:S(2)}, u32[]{:S(2)}) collective-permute-start(bf16[16,80,256]{2,1,0:T(8,128)(2,1)} %collective-permute-done.8.refs_12_), channel_id=1, source_target_pairs={{0,4},{1,5},{2,6},{3,7},{4,0},{5,1},{6,2},{7,3},{8,12},{9,13},{10,... | collective-permute-start | bytes 1966088 | tf_op jit(solution)/shard_map/ppermute | solution.py:727
  50.9 0.2 collective-permute-start.5
  51.1 0.8 collective-permute-done.6.refs_7_
  51.9 4.0 %collective-permute-start.11 = (bf16[80,128]{1,0:T(8,128)(2,1)S(1)}, bf16[80,128]{1,0:T(8,128)(2,1)S(1)}, u32[]{:S(2)}, u32[]{:S(2)}) collective-permute-start(bf16[80,128]{1,0:T(8,128)(2,1)S(1)} %climb1.1.own), channel_id=1, source_target_pairs={{0,12},{1,13},{2,14},{3,15},{4,8},{5,9},{6,10},{7,11},{8,4},{9,5},... | collective-permute-start | bytes 61448 | tf_op jit(solution)/shard_map/ppermute | solution.py:727
  56.0 9.6 %near1.1 = (f32[8,256,128]{2,1,0:T(8,128)S(1)}, s32[2,128]{1,0:T(2,128)S(1)}) custom-call(s32[8,16]{1,0:T(8,128)S(1)} %fusion.11.refs_0_, s32[2,128]{1,0:T(2,128)S(1)} %copy-done.11, s32[2,128]{1,0:T(2,128)S(1)} %copy-done.12, s32[2,128]{1,0:T(2,128)S(1)} %get-tuple-element.75.refs_3_, bf16[2064,128]{1,0:T(8,128)(2,1)S(1)} %copy-done.1, ...), custom_call_target="tpu_custom_call" | custom-call | flops 1 | bytes 1 | tf_op jit(solution)/shard_map/near1/pallas_call | solution.py:583
  65.6 1.4 %collective-permute-done.5.one.refs_2_ = bf16[80,128]{1,0:T(8,128)(2,1)S(1)} collective-permute-done((bf16[80,128]{1,0:T(8,128)(2,1)S(1)}, bf16[80,128]{1,0:T(8,128)(2,1)S(1)}, u32[]{:S(2)}, u32[]{:S(2)}) %collective-permute-start.5) | collective-permute-done | bytes 20512 | tf_op jit(solution)/shard_map/ppermute | solution.py:727
  67.0 0.3 climb2.1
  67.3 0.1 collective-permute-start.14
  67.4 2.0 %collective-permute-done.14.refs_9_ = bf16[16,80,256]{2,1,0:T(8,128)(2,1)S(1)} collective-permute-done((bf16[16,80,256]{2,1,0:T(8,128)(2,1)S(1)}, bf16[16,80,256]{2,1,0:T(8,128)(2,1)S(1)}, u32[]{:S(2)}, u32[]{:S(2)}) %collective-permute-start.14) | collective-permute-done | bytes 655392 | tf_op jit(solution)/shard_map/ppermute | solution.py:727
  69.4 4.4 %near2.1 = (bf16[2,256,128]{2,1,0:T(8,128)(2,1)S(1)}, bf16[2,256,128]{2,1,0:T(8,128)(2,1)S(1)}, bf16[2,256,128]{2,1,0:T(8,128)(2,1)S(1)}, bf16[2,256,128]{2,1,0:T(8,128)(2,1)S(1)}) custom-call(s32[2,128]{1,0:T(2,128)S(1)} %copy-done.9, s32[2,128]{1,0:T(2,128)S(1)} %copy-done.10, s32[2,128]{1,0:T(2,128)S(1)} %get-tuple-element.84.refs_2_, ...), custom_call_target="tpu_custom_call" | custom-call | flops 1 | bytes 1 | tf_op jit(solution)/shard_map/near2/pallas_call | solution.py:583
  73.9 4.7 %collective-permute-start.17 = (bf16[2,256,128]{2,1,0:T(8,128)(2,1)S(1)}, bf16[2,256,128]{2,1,0:T(8,128)(2,1)S(1)}, u32[]{:S(2)}, u32[]{:S(2)}) collective-permute-start(bf16[2,256,128]{2,1,0:T(8,128)(2,1)S(1)} %get-tuple-element.96), channel_id=1, source_target_pairs={{0,10},{1,11},{2,8},{3,9},{4,14},{5,15},{6,12},{7,13},{8,2},{9,3},... | collective-permute-start | bytes 393224 | tf_op jit(solution)/shard_map/ppermute | solution.py:727
  78.5 1.7 %collective-permute-start.16 = (bf16[2,256,128]{2,1,0:T(8,128)(2,1)S(1)}, bf16[2,256,128]{2,1,0:T(8,128)(2,1)S(1)}, u32[]{:S(2)}, u32[]{:S(2)}) collective-permute-start(bf16[2,256,128]{2,1,0:T(8,128)(2,1)S(1)} %get-tuple-element.94), channel_id=1, source_target_pairs={{0,8},{1,9},{2,10},{3,11},{4,12},{5,13},{6,14},{7,15},{8,0},{9,1},... | collective-permute-start | bytes 393224 | tf_op jit(solution)/shard_map/ppermute | solution.py:727
  80.3 3.9 %top.1.refs_2_ = f32[2,256,128]{2,1,0:T(8,128)S(1)} custom-call(bf16[17,80,256]{2,1,0:T(8,128)(2,1)S(1)} %collective-permute-done.1.other.refs_7_.refs_9_.refs_0_, bf16[80,128]{1,0:T(8,128)(2,1)S(1)} %collective-permute-done.2.other.refs_1_, bf16[80,128]{1,0:T(8,128)(2,1)S(1)} %collective-permute-done.5.one.refs_2_, ...), custom_call_target="tpu_custom_call" | custom-call | flops 1 | bytes 1 | tf_op jit(solution)/shard_map/top/pallas_call | solution.py:677
  84.2 2.0 %collective-permute-done.16.refs_6_ = bf16[2,256,128]{2,1,0:T(8,128)(2,1)S(1)} collective-permute-done((bf16[2,256,128]{2,1,0:T(8,128)(2,1)S(1)}, bf16[2,256,128]{2,1,0:T(8,128)(2,1)S(1)}, u32[]{:S(2)}, u32[]{:S(2)}) %collective-permute-start.16) | collective-permute-done | bytes 131104 | tf_op jit(solution)/shard_map/ppermute | solution.py:727
  86.2 0.9 %last_sum.1 = f32[16,4096]{1,0:T(8,128)} custom-call(f32[256,128]{1,0:T(8,128)S(1)} %copy-done.5, f32[256,128]{1,0:T(8,128)S(1)} %copy-done.6, f32[2,256,128]{2,1,0:T(8,128)S(1)} %top.1.refs_2_, f32[16,1,256]{2,1,0:T(1,128)S(1)} %copy-done.8, bf16[2,256,128]{2,1,0:T(8,128)(2,1)S(1)} %get-tuple-element.88.refs_4_, ...), custom_call_target="tpu_custom_call" | custom-call | flops 1 | bytes 1 | tf_op jit(solution)/shard_map/last_sum/pallas_call | solution.py:714
  (52 shorter events, 0.2 us)
Async XLA Ops:
  10.6 17.2 %copy-start.2 = (bf16[5,256,128]{2,1,0:T(8,128)(2,1)S(1)}, bf16[5,256,128]{2,1,0:T(8,128)(2,1)}, u32[]{:S(2)}) copy-start(bf16[5,256,128]{2,1,0:T(8,128)(2,1)} %get-tuple-element.63.interps) | copy-start | bytes 983044
  10.6 17.2 %copy-start.4 = (bf16[17,80,256]{2,1,0:T(8,128)(2,1)S(1)}, bf16[17,80,256]{2,1,0:T(8,128)(2,1)}, u32[]{:S(2)}) copy-start(bf16[17,80,256]{2,1,0:T(8,128)(2,1)} %get-tuple-element.61.own) | copy-start | bytes 2088964
  10.6 17.2 %copy-start.7 = (s32[5,1,128]{2,1,0:T(1,128)S(1)}, s32[5,1,128]{2,1,0:T(1,128)}, u32[]{:S(2)}) copy-start(s32[5,1,128]{2,1,0:T(1,128)} %get-tuple-element.62.skels) | copy-start | bytes 7684
  10.6 16.6 %collective-permute-start = (bf16[2064,128]{1,0:T(8,128)(2,1)}, bf16[2064,128]{1,0:T(8,128)(2,1)S(1)}, u32[]{:S(2)}, u32[]{:S(2)}) collective-permute-start(bf16[2064,128]{1,0:T(8,128)(2,1)} %get-tuple-element.58.refs_3_.refs_4_), channel_id=1, source_target_pairs={{0,2},{1,3},{2,0},{3,1},{4,6},{5,7},{6,4},{7,5},{8,10},{9,11},{10,... | collective-permute-start | bytes 1585160 | tf_op jit(solution)/shard_map/ppermute | solution.py:727
  13.6 14.2 %collective-permute-start.1 = (bf16[17,80,256]{2,1,0:T(8,128)(2,1)}, bf16[17,80,256]{2,1,0:T(8,128)(2,1)S(1)}, u32[]{:S(2)}, u32[]{:S(2)}) collective-permute-start(bf16[17,80,256]{2,1,0:T(8,128)(2,1)} %get-tuple-element.61.own), channel_id=1, source_target_pairs={{0,1},{1,0},{2,3},{3,2},{4,5},{5,4},{6,7},{7,6},{8,9},{9,8},{10,11... | collective-permute-start | bytes 2088968 | tf_op jit(solution)/shard_map/ppermute | solution.py:727
  13.6 24.6 %collective-permute-start.3 = (bf16[2064,128]{1,0:T(8,128)(2,1)}, bf16[2064,128]{1,0:T(8,128)(2,1)S(1)}, u32[]{:S(2)}, u32[]{:S(2)}) collective-permute-start(bf16[2064,128]{1,0:T(8,128)(2,1)} %get-tuple-element.58.refs_3_.refs_4_), channel_id=1, source_target_pairs={{0,8},{1,9},{2,10},{3,11},{4,12},{5,13},{6,14},{7,15},{8,0},{9,1},... | collective-permute-start | bytes 1585160 | tf_op jit(solution)/shard_map/ppermute | solution.py:727
  15.2 23.4 %collective-permute-start.4 = (bf16[16,80,256]{2,1,0:T(8,128)(2,1)}, bf16[16,80,256]{2,1,0:T(8,128)(2,1)S(1)}, u32[]{:S(2)}, u32[]{:S(2)}) collective-permute-start(bf16[16,80,256]{2,1,0:T(8,128)(2,1)} %get-tuple-element.69.refs_6_.refs_8_), channel_id=1, source_target_pairs={{0,4},{1,5},{2,6},{3,7},{4,0},{5,1},{6,2},{7,3},{8,12},{9,13},{10,... | collective-permute-start | bytes 1966088 | tf_op jit(solution)/shard_map/ppermute | solution.py:727
  16.7 31.9 %collective-permute-start.8 = (bf16[16,80,256]{2,1,0:T(8,128)(2,1)}, bf16[16,80,256]{2,1,0:T(8,128)(2,1)}, u32[]{:S(2)}, u32[]{:S(2)}) collective-permute-start(bf16[16,80,256]{2,1,0:T(8,128)(2,1)} %get-tuple-element.69.refs_6_.refs_8_), channel_id=1, source_target_pairs={{0,16},{1,17},{2,18},{3,19},{4,20},{5,21},{6,22},{7,23},{8,24},{9,... | collective-permute-start | bytes 1966088 | tf_op jit(solution)/shard_map/ppermute | solution.py:727
  28.0 10.6 %copy-start.1 = (bf16[2064,128]{1,0:T(8,128)(2,1)S(1)}, bf16[2064,128]{1,0:T(8,128)(2,1)}, u32[]{:S(2)}) copy-start(bf16[2064,128]{1,0:T(8,128)(2,1)} %get-tuple-element.58.refs_3_.refs_4_) | copy-start | bytes 1585156
  28.0 10.6 %copy-start.3 = (bf16[16,80,256]{2,1,0:T(8,128)(2,1)S(1)}, bf16[16,80,256]{2,1,0:T(8,128)(2,1)}, u32[]{:S(2)}) copy-start(bf16[16,80,256]{2,1,0:T(8,128)(2,1)} %get-tuple-element.69.refs_6_.refs_8_) | copy-start | bytes 1966084
  28.0 10.6 %copy-start.13 = (s32[2,128]{1,0:T(2,128)S(1)}, s32[2,128]{1,0:T(2,128)}, u32[]{:S(2)}) copy-start(s32[2,128]{1,0:T(2,128)} %get-tuple-element.67.refs_1_) | copy-start | bytes 3076
  28.0 18.7 %collective-permute-start.2 = (bf16[80,128]{1,0:T(8,128)(2,1)S(1)}, bf16[80,128]{1,0:T(8,128)(2,1)S(1)}, u32[]{:S(2)}, u32[]{:S(2)}) collective-permute-start(bf16[80,128]{1,0:T(8,128)(2,1)S(1)} %climb0.1.own), channel_id=1, source_target_pairs={{0,2},{1,3},{2,0},{3,1},{4,6},{5,7},{6,4},{7,5},{8,10},{9,11},{10,... | collective-permute-start | bytes 61448 | tf_op jit(solution)/shard_map/ppermute | solution.py:727
  35.2 20.7 %copy-start.11 = (s32[2,128]{1,0:T(2,128)S(1)}, s32[2,128]{1,0:T(2,128)}, u32[]{:S(2)}) copy-start(s32[2,128]{1,0:T(2,128)} %get-tuple-element.73.refs_1_) | copy-start | bytes 3076
  35.2 20.7 %copy-start.12 = (s32[2,128]{1,0:T(2,128)S(1)}, s32[2,128]{1,0:T(2,128)}, u32[]{:S(2)}) copy-start(s32[2,128]{1,0:T(2,128)} %get-tuple-element.74.refs_2_) | copy-start | bytes 3076
  38.2 13.7 %collective-permute-start.6 = (bf16[2064,128]{1,0:T(8,128)(2,1)S(1)}, bf16[2064,128]{1,0:T(8,128)(2,1)S(1)}, u32[]{:S(2)}, u32[]{:S(2)}) collective-permute-start(bf16[2064,128]{1,0:T(8,128)(2,1)S(1)} %collective-permute-done.3.refs_5_.refs_6_), channel_id=1, source_target_pairs={{0,2},{1,3},{2,0},{3,1},{4,6},{5,7},{6,4},{7,5},{8,10},{9,11},{10,... | collective-permute-start | bytes 1585160 | tf_op jit(solution)/shard_map/ppermute | solution.py:727
  48.6 3.3 %collective-permute-start.9 = (bf16[16,80,256]{2,1,0:T(8,128)(2,1)}, bf16[16,80,256]{2,1,0:T(8,128)(2,1)S(1)}, u32[]{:S(2)}, u32[]{:S(2)}) collective-permute-start(bf16[16,80,256]{2,1,0:T(8,128)(2,1)} %collective-permute-done.8.refs_12_), channel_id=1, source_target_pairs={{0,1},{1,0},{2,3},{3,2},{4,5},{5,4},{6,7},{7,6},{8,9},{9,8},{10,11... | collective-permute-start | bytes 1966088 | tf_op jit(solution)/shard_map/ppermute | solution.py:727
  48.6 7.4 %collective-permute-start.7 = (bf16[16,80,256]{2,1,0:T(8,128)(2,1)S(1)}, bf16[16,80,256]{2,1,0:T(8,128)(2,1)S(1)}, u32[]{:S(2)}, u32[]{:S(2)}) collective-permute-start(bf16[16,80,256]{2,1,0:T(8,128)(2,1)S(1)} %collective-permute-done.4.refs_8_.refs_10_), channel_id=1, source_target_pairs={{0,1},{1,0},{2,3},{3,2},{4,5},{5,4},{6,7},{7,6},{8,9},{9,8},{10,11... | collective-permute-start | bytes 1966088 | tf_op jit(solution)/shard_map/ppermute | solution.py:727
  49.1 18.1 %collective-permute-start.13 = (bf16[16,80,256]{2,1,0:T(8,128)(2,1)}, bf16[16,80,256]{2,1,0:T(8,128)(2,1)S(1)}, u32[]{:S(2)}, u32[]{:S(2)}) collective-permute-start(bf16[16,80,256]{2,1,0:T(8,128)(2,1)} %collective-permute-done.8.refs_12_), channel_id=1, source_target_pairs={{0,4},{1,5},{2,6},{3,7},{4,0},{5,1},{6,2},{7,3},{8,12},{9,13},{10,... | collective-permute-start | bytes 1966088 | tf_op jit(solution)/shard_map/ppermute | solution.py:727
  50.9 16.1 %collective-permute-start.5 = (bf16[80,128]{1,0:T(8,128)(2,1)S(1)}, bf16[80,128]{1,0:T(8,128)(2,1)S(1)}, u32[]{:S(2)}, u32[]{:S(2)}) collective-permute-start(bf16[80,128]{1,0:T(8,128)(2,1)S(1)} %climb1.1.own), channel_id=1, source_target_pairs={{0,4},{1,5},{2,6},{3,7},{4,0},{5,1},{6,2},{7,3},{8,12},{9,13},{10,... | collective-permute-start | bytes 61448 | tf_op jit(solution)/shard_map/ppermute | solution.py:727
  51.9 15.1 %collective-permute-start.10 = (bf16[80,128]{1,0:T(8,128)(2,1)S(1)}, bf16[80,128]{1,0:T(8,128)(2,1)S(1)}, u32[]{:S(2)}, u32[]{:S(2)}) collective-permute-start(bf16[80,128]{1,0:T(8,128)(2,1)S(1)} %climb1.1.own), channel_id=1, source_target_pairs={{0,8},{1,9},{2,10},{3,11},{4,12},{5,13},{6,14},{7,15},{8,0},{9,1},... | collective-permute-start | bytes 61448 | tf_op jit(solution)/shard_map/ppermute | solution.py:727
  51.9 15.0 %collective-permute-start.11 = (bf16[80,128]{1,0:T(8,128)(2,1)S(1)}, bf16[80,128]{1,0:T(8,128)(2,1)S(1)}, u32[]{:S(2)}, u32[]{:S(2)}) collective-permute-start(bf16[80,128]{1,0:T(8,128)(2,1)S(1)} %climb1.1.own), channel_id=1, source_target_pairs={{0,12},{1,13},{2,14},{3,15},{4,8},{5,9},{6,10},{7,11},{8,4},{9,5},... | collective-permute-start | bytes 61448 | tf_op jit(solution)/shard_map/ppermute | solution.py:727
  56.0 13.4 %copy-start.9 = (s32[2,128]{1,0:T(2,128)S(1)}, s32[2,128]{1,0:T(2,128)}, u32[]{:S(2)}) copy-start(s32[2,128]{1,0:T(2,128)} %get-tuple-element.82.refs_0_) | copy-start | bytes 3076
  56.0 13.4 %copy-start.10 = (s32[2,128]{1,0:T(2,128)S(1)}, s32[2,128]{1,0:T(2,128)}, u32[]{:S(2)}) copy-start(s32[2,128]{1,0:T(2,128)} %get-tuple-element.83.refs_1_) | copy-start | bytes 3076
  67.3 2.2 %collective-permute-start.14 = (bf16[16,80,256]{2,1,0:T(8,128)(2,1)S(1)}, bf16[16,80,256]{2,1,0:T(8,128)(2,1)S(1)}, u32[]{:S(2)}, u32[]{:S(2)}) collective-permute-start(bf16[16,80,256]{2,1,0:T(8,128)(2,1)S(1)} %collective-permute-done.13.refs_8_), channel_id=1, source_target_pairs={{0,1},{1,0},{2,3},{3,2},{4,5},{5,4},{6,7},{7,6},{8,9},{9,8},{10,11... | collective-permute-start | bytes 1966088 | tf_op jit(solution)/shard_map/ppermute | solution.py:727
  67.4 6.5 %collective-permute-start.12 = (bf16[80,128]{1,0:T(8,128)(2,1)S(1)}, bf16[80,128]{1,0:T(8,128)(2,1)S(1)}, u32[]{:S(2)}, u32[]{:S(2)}) collective-permute-start(bf16[80,128]{1,0:T(8,128)(2,1)S(1)} %get-tuple-element.81), channel_id=1, source_target_pairs={{0,16},{1,17},{2,18},{3,19},{4,20},{5,21},{6,22},{7,23},{8,24},{9,... | collective-permute-start | bytes 61448 | tf_op jit(solution)/shard_map/ppermute | solution.py:727
  69.4 10.8 %copy-start = (bf16[16,256,128]{2,1,0:T(8,128)(2,1)S(1)}, bf16[16,256,128]{2,1,0:T(8,128)(2,1)}, u32[]{:S(2)}) copy-start(bf16[16,256,128]{2,1,0:T(8,128)(2,1)} %get-tuple-element.90.refs_5_) | copy-start | bytes 3145732
  73.8 12.4 %copy-start.5 = (f32[256,128]{1,0:T(8,128)S(1)}, f32[256,128]{1,0:T(8,128)}, u32[]{:S(2)}) copy-start(f32[256,128]{1,0:T(8,128)} %get-tuple-element.57.refs_0_) | copy-start | bytes 393220
  73.9 12.4 %copy-start.6 = (f32[256,128]{1,0:T(8,128)S(1)}, f32[256,128]{1,0:T(8,128)}, u32[]{:S(2)}) copy-start(f32[256,128]{1,0:T(8,128)} %get-tuple-element.65.refs_1_) | copy-start | bytes 393220
  73.9 12.4 %copy-start.8 = (f32[16,1,256]{2,1,0:T(1,128)S(1)}, f32[16,1,256]{2,1,0:T(1,128)}, u32[]{:S(2)}) copy-start(f32[16,1,256]{2,1,0:T(1,128)} %get-tuple-element.52.refs_3_) | copy-start | bytes 49156
  73.9 10.3 %collective-permute-start.17 = (bf16[2,256,128]{2,1,0:T(8,128)(2,1)S(1)}, bf16[2,256,128]{2,1,0:T(8,128)(2,1)S(1)}, u32[]{:S(2)}, u32[]{:S(2)}) collective-permute-start(bf16[2,256,128]{2,1,0:T(8,128)(2,1)S(1)} %get-tuple-element.96), channel_id=1, source_target_pairs={{0,10},{1,11},{2,8},{3,9},{4,14},{5,15},{6,12},{7,13},{8,2},{9,3},... | collective-permute-start | bytes 393224 | tf_op jit(solution)/shard_map/ppermute | solution.py:727
  78.5 7.7 %collective-permute-start.16 = (bf16[2,256,128]{2,1,0:T(8,128)(2,1)S(1)}, bf16[2,256,128]{2,1,0:T(8,128)(2,1)S(1)}, u32[]{:S(2)}, u32[]{:S(2)}) collective-permute-start(bf16[2,256,128]{2,1,0:T(8,128)(2,1)S(1)} %get-tuple-element.94), channel_id=1, source_target_pairs={{0,8},{1,9},{2,10},{3,11},{4,12},{5,13},{6,14},{7,15},{8,0},{9,1},... | collective-permute-start | bytes 393224 | tf_op jit(solution)/shard_map/ppermute | solution.py:727
  80.3 5.9 %collective-permute-start.15 = (bf16[2,256,128]{2,1,0:T(8,128)(2,1)S(1)}, bf16[2,256,128]{2,1,0:T(8,128)(2,1)S(1)}, u32[]{:S(2)}, u32[]{:S(2)}) collective-permute-start(bf16[2,256,128]{2,1,0:T(8,128)(2,1)S(1)} %get-tuple-element.92), channel_id=1, source_target_pairs={{0,2},{1,3},{2,0},{3,1},{4,6},{5,7},{6,4},{7,5},{8,10},{9,11},{10,... | collective-permute-start | bytes 393224 | tf_op jit(solution)/shard_map/ppermute | solution.py:727
  (1 other events, 0.7 us)

commit v4 on v3

--- a/solution.py
+++ b/solution.py
@@ -146,11 +146,11 @@
 
 
 def first_kernel(
-    order, points_in, charges_in, owner_in, slot_in,
+    order_in, points_in, charges_in, owner_in, slot_in,
     leaf_interp_in, leaf_skel_in, inner_interp_in, inner_skel_in, top_interp, top_skel,
     src_out, tgt_out, cols_out, loads_out, rows_out, norms_out, mine_out, interps_out, skels_out, codes_out,
     points, charges, owner, slot, unsorted, buffer0, buffer1, src, tgt, cols, loads, rows, norms,
-    joined, root, interps, skels, codes, leaf_interp, leaf_skel, inner_interp, inner_skel, sems,
+    joined, root, interps, skels, codes, order, leaf_interp, leaf_skel, inner_interp, inner_skel, sems,
 ):
     count = points.shape[1]
     chunks = 4
@@ -167,6 +167,7 @@
     for c in range(chunks):
         at = pl.ds(c * width, width)
         parts.append(begin(points_in.at[:, at], points.at[:, at]))
+    order_copy = begin(order_in, order)
     near_lists = [begin(owner_in, owner), begin(slot_in, slot)]
     needed = [
         begin(leaf_skel_in, leaf_skel),
@@ -230,8 +231,15 @@
             picked = dot(coords, onehot(leaf_skel[pl.ds(i, 1), :], 256)).astype(bf16)
             value = dot(load, leaf_interp[i]).astype(bf16)
             finish(i, jnp.concatenate([picked, value], axis=0))
-
-    for copy in needed:
+        node = combine(
+            joined[2 * pair],
+            joined[2 * pair + 1],
+            inner_skel[pl.ds(pair, 1), :],
+            inner_interp[pair],
+        )
+        finish(leaves + pair, node)
+
+    for copy in needed + [order_copy]:
         copy.wait()
 
     def two_pairs(i, carry):
@@ -252,10 +260,10 @@
     tgt[count // 2 :, :] = jnp.concatenate([near, blank], axis=1).astype(bf16)
     rest += [begin(src, src_out), begin(tgt, tgt_out), begin(src, mine_out.at[pl.ds(0, leaves)])]
     rest += [begin(rows, rows_out), begin(norms, norms_out)]
-    tiles = pl.ds(0, 3 * leaves)
+    tiles = pl.ds(0, 3 * leaves + leaves // 2)
     rest += [begin(cols.at[tiles], cols_out.at[tiles])]
-    first, half = 0, leaves // 2
-    number, row = leaves, 0
+    first, half = leaves, leaves // 4
+    number, row = leaves + leaves // 2, leaves // 2
     while half > 0:
         for j in range(half):
             left = joined[first + 2 * j]
@@ -269,7 +277,7 @@
     last = cols.shape[0] - 1
     cols[last] = jnp.zeros((128, 128), bf16)
     loads[last] = jnp.zeros((16, 128), bf16)
-    inner_tiles = pl.ds(3 * leaves, leaves)
+    inner_tiles = pl.ds(3 * leaves + leaves // 2, leaves // 2)
     rest += [begin(root, mine_out.at[leaves]), begin(loads, loads_out)]
     rest += [begin(cols.at[inner_tiles], cols_out.at[inner_tiles])]
     for copy in rest:
@@ -328,13 +336,16 @@
     held += shapes[:6]
     held += [((2 * leaves - 1, 80, 128), bf16), ((80, 256), bf16)]
     held += shapes[7:]
+    n_before = len(held)
     held += [(table.shape, table.dtype) for table in tables[:4]]
     return pl.pallas_call(
         first_kernel,
         out_shape=tuple(jax.ShapeDtypeStruct(*shape) for shape in shapes),
-        in_specs=[SMEM] + [ANY] * 10,
+        in_specs=[ANY] * 11,
         out_specs=(ANY,) * 10,
-        scratch_shapes=[pltpu.VMEM(*shape) for shape in held]
+        scratch_shapes=[pltpu.VMEM(*shape) for shape in held[:n_before]]
+        + [pltpu.SMEM(order.shape, jnp.int32)]
+        + [pltpu.VMEM(*shape) for shape in held[n_before:]]
         + [pltpu.SemaphoreType.DMA((24 + 2 * steps,))],
         compiler_params=params(FIRST_LIMIT),
         cost_estimate=cost(),
@@ -471,15 +482,22 @@
     makes = phase < PHASES - 1
     (codes,) = take(1) if makes else (None,)
     lists = take(n_lists)
-    target_parts = take(n_targets)
+    target_parts = take(n_targets if makes else 1)
     source_parts = take(n_sources)
     before = take(phase > 0)
     outs = take(n_targets) if not makes else []
     (acc,) = take(1) if makes else (None,)
     tables = take(PHASES - 1 - phase) if makes else []
-    sources, targets, sems, pairs, steps = take(5)
+    if phase == 1:
+        (targets,) = take(1)
+    elif phase == 2:
+        (targets,) = target_parts
+        target_parts = []
+    sources, sems, pairs, steps = take(4)
+    if phase == 0:
+        (targets,) = take(1)
     if not makes:
-        (acc,) = refs
+        (acc,) = take(1)
     leaves = source_parts[0].shape[0]
     size = leaves * 128
     copies = []
@@ -491,16 +509,11 @@
     own_rows = acc.shape[0] // n_targets
     for k, part in enumerate(lists):
         begin(part, pairs.at[pl.ds(k * own_rows, own_rows)])
-    done = 0
-    for part in before:
-        done = part.shape[0]
-        begin(part, acc.at[pl.ds(0, done)])
     for k, part in enumerate(target_parts):
         begin(part.at[pl.ds(0, size)], targets.at[pl.ds(k * size, size)])
     for k, part in enumerate(source_parts):
         begin(part.at[pl.ds(0, leaves)], sources.at[pl.ds(k * leaves, leaves)])
-    if done < acc.shape[0]:
-        acc[done:] = jnp.zeros((acc.shape[0] - done,) + acc.shape[1:], f32)
+    acc[...] = jnp.zeros_like(acc)
     if makes:
         table = pairs.at[pl.ds(n_lists * own_rows, own_rows)]
         list_pairs(codes, [None] * phase + [table] + tables)
@@ -551,33 +564,45 @@
 
         lax.fori_loop(0, counts[k], step, 0)
 
-    each = acc.shape[0] // n_targets
+    if makes:
+        for part in before:
+            acc[: part.shape[0]] += part[...]
     for k, out in enumerate(outs):
-        out[...] = acc[k * each : (k + 1) * each].astype(bf16)
+        mine = slice(k * own_rows, (k + 1) * own_rows)
+        out[...] = (acc[mine] + before[0][mine]).astype(bf16)
 
 
 def near(phase, lists, targets, sources, codes=None, before=None):
-    n_sources, n_targets = len(sources), len(targets)
+    n_sources = len(sources)
+    makes = phase < PHASES - 1
+    n_targets = len(targets) if makes else len(lists)
     leaves = min(source.shape[0] for source in sources)
     sums = jax.ShapeDtypeStruct((n_targets * leaves // 8, 256, 128), f32)
     part = jax.ShapeDtypeStruct((leaves // 8, 256, 128), bf16)
-    makes = phase < PHASES - 1
+    held_targets = jax.ShapeDtypeStruct((n_targets * leaves * 128, 128), bf16)
     args = ([codes] if makes else []) + list(lists) + list(targets) + list(sources)
-    args += [] if before is None else [before]
-    n_smem = int(makes)
-    n_tables = PHASES - 1 - phase
+    in_specs = [SMEM] * int(makes) + [ANY] * (len(args) - int(makes))
+    if not makes:
+        in_specs[len(lists)] = VMEM
+    if before is not None:
+        args.append(before)
+        in_specs.append(VMEM)
     if makes:
+        n_tables = PHASES - 1 - phase
         out_shape = (sums,) + (pair_table(leaves),) * n_tables
         out_specs = (VMEM,) + (SMEM,) * n_tables
+        if phase == 1:
+            out_shape, out_specs = out_shape + (held_targets,), out_specs + (VMEM,)
     else:
         out_shape, out_specs = (part,) * n_targets, (VMEM,) * n_targets
     scratch = [
         pltpu.VMEM((n_sources * leaves, 80, 256), bf16),
-        pltpu.VMEM((n_targets * leaves * 128, 128), bf16),
-        pltpu.SemaphoreType.DMA((n_sources + n_targets + len(lists) + 1,)),
+        pltpu.SemaphoreType.DMA((n_sources + n_targets + len(lists),)),
         pltpu.SMEM((n_targets * leaves // 8, 128), jnp.int32),
         pltpu.SMEM((len(STEPS), n_targets * leaves), jnp.int32),
     ]
+    if phase == 0:
+        scratch.append(pltpu.VMEM(held_targets.shape, bf16))
     if not makes:
         scratch.append(pltpu.VMEM(sums.shape, f32))
     return pl.pallas_call(
@@ -585,7 +610,7 @@
             near_kernel, n_sources=n_sources, n_targets=n_targets, n_lists=len(lists), phase=phase
         ),
         out_shape=out_shape,
-        in_specs=[SMEM] * n_smem + [ANY] * (len(args) - n_smem),
+        in_specs=in_specs,
         out_specs=out_specs,
         scratch_shapes=scratch,
         compiler_params=params(),
@@ -809,7 +834,7 @@
     pieces[late | 1] = swap(pieces[late], 1)
     height, row = 2, 2
     others = [swap(node, k * 2**height) for k in (1, 2, 3)]
-    sums, last_table = near(
+    sums, last_table, all_targets = near(
         1,
         [tables[1] for tables in lists] + [far_tables1],
         targets,
@@ -831,7 +856,7 @@
     parts = near(
         2,
         [tables[2] for tables in lists] + [far_tables2, after(last_table, node)],
-        targets,
+        [all_targets],
         [pieces[k | late] for k in wanted[2:]],
         before=sums,
     )

time: 86.9 us -> 87.1 us (level)
  Pallas kernels: 51.9 us -> 54.6 us
  starting transfers between devices: 22.6 us -> 20.4 us
  waiting for transfers between devices: 10.8 us -> 9.71 us
    ppermute x18, starting transfers between devices: 22.6 us -> 20.4 us  [swap(): return lax.ppermute(value, 'leaf', pairs)]
    pallas_call x3, Pallas kernels: 21.4 us -> 23.4 us  [near(): pl.pallas_call(functools.partial(near_kernel, n_sources=n_sources, n_targ...]
    ppermute x18, waiting for transfers between devices: 10.8 us -> 9.71 us  [swap(): return lax.ppermute(value, 'leaf', pairs)]
  transfers between devices with their start and end apart: 18 -> 18, of which waited for: 6 -> 5; matrix products, arithmetic and copies ran while one was open for 1% -> 1% of each run, Pallas kernels for 46% -> 50%
where the time goes in v4:
time: 87.1 us; the launch traced here: 86.6 us
  Pallas kernels  54.6 us (63%)
  starting transfers between devices  20.4 us (23%)
  waiting for transfers between devices  9.71 us (11%)
    pallas_call x3, Pallas kernels, near(): pl.pallas_call(functools.partial(near_kernel, n_sources=n_sources, n_targ...  23.4 us
    ppermute x18, starting transfers between devices, swap(): return lax.ppermute(value, 'leaf', pairs)  20.4 us
    pallas_call x2, Pallas kernels, self_and_far(): pl.pallas_call(functools.partial(far_kernel, first_leaf=call * n_leaves,...  15.3 us
    pallas_call x1, Pallas kernels, first_part(): pl.pallas_call(first_kernel, out_shape=tuple((jax.ShapeDtypeStruct(*shape...  10.5 us
    ppermute x18, waiting for transfers between devices, swap(): return lax.ppermute(value, 'leaf', pairs)  9.71 us
    pallas_call x1, Pallas kernels, top(): pl.pallas_call(top_kernel, out_shape=jax.ShapeDtypeStruct((rows.shape[0]...  3.88 us
  transfers between devices with their start and end apart: 18, of which 5 were waited for; matrix products, arithmetic and copies ran while one was open for 1% of the time, Pallas kernels for 50%

profile of v4, /device:TPU:0, one launch (start us, length us, event | category | flops | bytes accessed | tf_op | source)
XLA Modules:
  0.0 86.6 jit_solution(13650730855369010054)
XLA Ops:
  0.0 10.5 %order_and_subtree.1 = (bf16[16,80,256]{2,1,0:T(8,128)(2,1)}, bf16[2064,128]{1,0:T(8,128)(2,1)}, bf16[64,128,128]{2,1,0:T(8,128)(2,1)}, bf16[64,16,128]{2,1,0:T(...) custom-call(s32[4096]{0:T(1024)} %order_in.1, ...), custom_call_target="tpu_custom_call" | custom-call | flops 1 | bytes 1 | tf_op jit(solution)/shard_map/order_and_subtree/pallas_call | solution.py:341
  10.6 3.0 %collective-permute-start = (bf16[2064,128]{1,0:T(8,128)(2,1)}, bf16[2064,128]{1,0:T(8,128)(2,1)S(1)}, u32[]{:S(2)}, u32[]{:S(2)}) collective-permute-start(bf16[2064,128]{1,0:T(8,128)(2,1)} %get-tuple-element.59.refs_3_.refs_4_), channel_id=1, source_target_pairs={{0,2},{1,3},{2,0},{3,1},{4,6},{5,7},{6,4},{7,5},{8,10},{9,11},{10,... | collective-permute-start | bytes 1585160 | tf_op jit(solution)/shard_map/ppermute | solution.py:752
  13.6 1.6 %collective-permute-start.3 = (bf16[2064,128]{1,0:T(8,128)(2,1)}, bf16[2064,128]{1,0:T(8,128)(2,1)S(1)}, u32[]{:S(2)}, u32[]{:S(2)}) collective-permute-start(bf16[2064,128]{1,0:T(8,128)(2,1)} %get-tuple-element.59.refs_3_.refs_4_), channel_id=1, source_target_pairs={{0,8},{1,9},{2,10},{3,11},{4,12},{5,13},{6,14},{7,15},{8,0},{9,1},... | collective-permute-start | bytes 1585160 | tf_op jit(solution)/shard_map/ppermute | solution.py:752
  15.2 1.5 %collective-permute-start.4 = (bf16[16,80,256]{2,1,0:T(8,128)(2,1)}, bf16[16,80,256]{2,1,0:T(8,128)(2,1)S(1)}, u32[]{:S(2)}, u32[]{:S(2)}) collective-permute-start(bf16[16,80,256]{2,1,0:T(8,128)(2,1)} %get-tuple-element.70.refs_6_.refs_8_), channel_id=1, source_target_pairs={{0,4},{1,5},{2,6},{3,7},{4,0},{5,1},{6,2},{7,3},{8,12},{9,13},{10,... | collective-permute-start | bytes 1966088 | tf_op jit(solution)/shard_map/ppermute | solution.py:752
  16.7 2.6 %collective-permute-start.8 = (bf16[16,80,256]{2,1,0:T(8,128)(2,1)}, bf16[16,80,256]{2,1,0:T(8,128)(2,1)}, u32[]{:S(2)}, u32[]{:S(2)}) collective-permute-start(bf16[16,80,256]{2,1,0:T(8,128)(2,1)} %get-tuple-element.70.refs_6_.refs_8_), channel_id=1, source_target_pairs={{0,16},{1,17},{2,18},{3,19},{4,20},{5,21},{6,22},{7,23},{8,24},{9,... | collective-permute-start | bytes 1966088 | tf_op jit(solution)/shard_map/ppermute | solution.py:752
  19.3 8.5 %self_and_far0.1 = (f32[256,128]{1,0:T(8,128)}, s32[2,128]{1,0:T(2,128)}, s32[2,128]{1,0:T(2,128)}, s32[2,128]{1,0:T(2,128)}) custom-call(s32[8,16]{1,0:T(8,128)} %get-tuple-element.52.refs_0_, s32[16,16]{1,0:T(8,128)} %refs_1_.1, s32[16]{0:T(128)} %refs_2_.3, bf16[64,128,128]{2,1,0:T(8,128)(2,1)} %get-tuple-element.55.refs_3_, ...), custom_call_target="tpu_custom_call" | custom-call | flops 1 | bytes 1 | tf_op jit(solution)/shard_map/self_and_far0/pallas_call | solution.py:453
  27.8 0.6 fusion.3.refs_0_
  28.4 0.1 climb0.1.own
  28.6 0.2 collective-permute-start.2
  28.8 6.8 %self_and_far1.1 = (f32[256,128]{1,0:T(8,128)}, s32[2,128]{1,0:T(2,128)}, s32[2,128]{1,0:T(2,128)}, s32[2,128]{1,0:T(2,128)}) custom-call(s32[8,16]{1,0:T(8,128)} %fusion.3.refs_0_, s32[16,16]{1,0:T(8,128)} %refs_1_.1, s32[16]{0:T(128)} %refs_2_.3, bf16[64,128,128]{2,1,0:T(8,128)(2,1)} %get-tuple-element.55.refs_3_, ...), custom_call_target="tpu_custom_call" | custom-call | flops 1 | bytes 1 | tf_op jit(solution)/shard_map/self_and_far1/pallas_call | solution.py:453
  35.7 2.5 %collective-permute-done.3.refs_5_.refs_6_ = bf16[2064,128]{1,0:T(8,128)(2,1)S(1)} collective-permute-done((bf16[2064,128]{1,0:T(8,128)(2,1)}, bf16[2064,128]{1,0:T(8,128)(2,1)S(1)}, u32[]{:S(2)}, u32[]{:S(2)}) %collective-permute-start.3) | collective-permute-done | bytes 528416 | tf_op jit(solution)/shard_map/ppermute | solution.py:752
  38.2 0.4 collective-permute-start.6
  38.6 0.7 copy-done.14
  39.3 7.6 %near0.1 = (f32[6,256,128]{2,1,0:T(8,128)S(1)}, s32[2,128]{1,0:T(2,128)S(1)}, s32[2,128]{1,0:T(2,128)S(1)}) custom-call(s32[8,16]{1,0:T(8,128)S(1)} %fusion.7.refs_0_, s32[2,128]{1,0:T(2,128)S(1)} %copy-done.13, s32[2,128]{1,0:T(2,128)S(1)} %copy-done.14, bf16[2064,128]{1,0:T(8,128)(2,1)S(1)} %copy-done.3, ...), custom_call_target="tpu_custom_call" | custom-call | flops 1 | bytes 1 | tf_op jit(solution)/shard_map/near0/pallas_call | solution.py:608
  46.9 0.1 climb1.1.own
  47.1 1.5 %collective-permute-done.8.refs_12_ = bf16[16,80,256]{2,1,0:T(8,128)(2,1)} collective-permute-done((bf16[16,80,256]{2,1,0:T(8,128)(2,1)}, bf16[16,80,256]{2,1,0:T(8,128)(2,1)}, u32[]{:S(2)}, u32[]{:S(2)}) %collective-permute-start.8) | collective-permute-done | bytes 655392 | tf_op jit(solution)/shard_map/ppermute | solution.py:752
  48.6 0.5 collective-permute-start.7
  49.1 0.5 collective-permute-start.13
  49.6 1.5 %collective-permute-start.5 = (bf16[80,128]{1,0:T(8,128)(2,1)S(1)}, bf16[80,128]{1,0:T(8,128)(2,1)S(1)}, u32[]{:S(2)}, u32[]{:S(2)}) collective-permute-start(bf16[80,128]{1,0:T(8,128)(2,1)S(1)} %climb1.1.own), channel_id=1, source_target_pairs={{0,4},{1,5},{2,6},{3,7},{4,0},{5,1},{6,2},{7,3},{8,12},{9,13},{10,... | collective-permute-start | bytes 61448 | tf_op jit(solution)/shard_map/ppermute | solution.py:752
  51.1 0.8 collective-permute-done.6.refs_7_
  51.9 4.0 %collective-permute-start.11 = (bf16[80,128]{1,0:T(8,128)(2,1)S(1)}, bf16[80,128]{1,0:T(8,128)(2,1)S(1)}, u32[]{:S(2)}, u32[]{:S(2)}) collective-permute-start(bf16[80,128]{1,0:T(8,128)(2,1)S(1)} %climb1.1.own), channel_id=1, source_target_pairs={{0,12},{1,13},{2,14},{3,15},{4,8},{5,9},{6,10},{7,11},{8,4},{9,5},... | collective-permute-start | bytes 61448 | tf_op jit(solution)/shard_map/ppermute | solution.py:752
  56.0 11.5 %near1.1 = (f32[8,256,128]{2,1,0:T(8,128)S(1)}, s32[2,128]{1,0:T(2,128)S(1)}, bf16[8192,128]{1,0:T(8,128)(2,1)S(1)}) custom-call(s32[8,16]{1,0:T(8,128)S(1)} %fusion.11.refs_0_, s32[2,128]{1,0:T(2,128)S(1)} %copy-done.11, s32[2,128]{1,0:T(2,128)S(1)} %copy-done.12, s32[2,128]{1,0:T(2,128)S(1)} %get-tuple-element.76.refs_3_, bf16[2064,128]{1,0:T(8,128)(2,1)S(1)} %copy-done.3, ...), custom_call_target="tpu_custom_call" | custom-call | flops 1 | bytes 1 | tf_op jit(solution)/shard_map/near1/pallas_call | solution.py:608
  67.5 0.3 climb2.1
  67.8 0.1 collective-permute-start.14
  67.9 0.1 collective-permute-start.12
  68.0 2.0 %collective-permute-done.14.refs_6_ = bf16[16,80,256]{2,1,0:T(8,128)(2,1)S(1)} collective-permute-done((bf16[16,80,256]{2,1,0:T(8,128)(2,1)S(1)}, bf16[16,80,256]{2,1,0:T(8,128)(2,1)S(1)}, u32[]{:S(2)}, u32[]{:S(2)}) %collective-permute-start.14) | collective-permute-done | bytes 655392 | tf_op jit(solution)/shard_map/ppermute | solution.py:752
  70.0 4.3 %near2.1 = (bf16[2,256,128]{2,1,0:T(8,128)(2,1)S(1)}, bf16[2,256,128]{2,1,0:T(8,128)(2,1)S(1)}, bf16[2,256,128]{2,1,0:T(8,128)(2,1)S(1)}, bf16[2,256,128]{2,1,0:T(8,128)(2,1)S(1)}) custom-call(s32[2,128]{1,0:T(2,128)S(1)} %copy-done.9, s32[2,128]{1,0:T(2,128)S(1)} %copy-done.10, s32[2,128]{1,0:T(2,128)S(1)} %get-tuple-element.85.refs_2_, ...), custom_call_target="tpu_custom_call" | custom-call | flops 1 | bytes 1 | tf_op jit(solution)/shard_map/near2/pallas_call | solution.py:608
  74.3 3.2 %collective-permute-start.17 = (bf16[2,256,128]{2,1,0:T(8,128)(2,1)S(1)}, bf16[2,256,128]{2,1,0:T(8,128)(2,1)S(1)}, u32[]{:S(2)}, u32[]{:S(2)}) collective-permute-start(bf16[2,256,128]{2,1,0:T(8,128)(2,1)S(1)} %get-tuple-element.98), channel_id=1, source_target_pairs={{0,10},{1,11},{2,8},{3,9},{4,14},{5,15},{6,12},{7,13},{8,2},{9,3},... | collective-permute-start | bytes 393224 | tf_op jit(solution)/shard_map/ppermute | solution.py:752
  77.6 1.2 %collective-permute-start.16 = (bf16[2,256,128]{2,1,0:T(8,128)(2,1)S(1)}, bf16[2,256,128]{2,1,0:T(8,128)(2,1)S(1)}, u32[]{:S(2)}, u32[]{:S(2)}) collective-permute-start(bf16[2,256,128]{2,1,0:T(8,128)(2,1)S(1)} %get-tuple-element.96), channel_id=1, source_target_pairs={{0,8},{1,9},{2,10},{3,11},{4,12},{5,13},{6,14},{7,15},{8,0},{9,1},... | collective-permute-start | bytes 393224 | tf_op jit(solution)/shard_map/ppermute | solution.py:752
  78.8 3.9 %top.1.refs_2_ = f32[2,256,128]{2,1,0:T(8,128)S(1)} custom-call(bf16[17,80,256]{2,1,0:T(8,128)(2,1)S(1)} %collective-permute-done.1.other.refs_7_.refs_9_.refs_0_, bf16[80,128]{1,0:T(8,128)(2,1)S(1)} %collective-permute-done.2.other.refs_1_, bf16[80,128]{1,0:T(8,128)(2,1)S(1)} %collective-permute-done.5.one.refs_2_, ...), custom_call_target="tpu_custom_call" | custom-call | flops 1 | bytes 1 | tf_op jit(solution)/shard_map/top/pallas_call | solution.py:702
  82.7 2.9 %collective-permute-done.16.refs_6_ = bf16[2,256,128]{2,1,0:T(8,128)(2,1)S(1)} collective-permute-done((bf16[2,256,128]{2,1,0:T(8,128)(2,1)S(1)}, bf16[2,256,128]{2,1,0:T(8,128)(2,1)S(1)}, u32[]{:S(2)}, u32[]{:S(2)}) %collective-permute-start.16) | collective-permute-done | bytes 131104 | tf_op jit(solution)/shard_map/ppermute | solution.py:752
  85.7 0.9 %last_sum.1 = f32[16,4096]{1,0:T(8,128)} custom-call(f32[256,128]{1,0:T(8,128)S(1)} %copy-done.5, f32[256,128]{1,0:T(8,128)S(1)} %copy-done.6, f32[2,256,128]{2,1,0:T(8,128)S(1)} %top.1.refs_2_, f32[16,1,256]{2,1,0:T(1,128)S(1)} %copy-done.8, bf16[2,256,128]{2,1,0:T(8,128)(2,1)S(1)} %get-tuple-element.90.refs_4_, ...), custom_call_target="tpu_custom_call" | custom-call | flops 1 | bytes 1 | tf_op jit(solution)/shard_map/last_sum/pallas_call | solution.py:739
  (52 shorter events, 0.2 us)
Async XLA Ops:
  10.5 17.9 %copy-start.1 = (bf16[5,256,128]{2,1,0:T(8,128)(2,1)S(1)}, bf16[5,256,128]{2,1,0:T(8,128)(2,1)}, u32[]{:S(2)}) copy-start(bf16[5,256,128]{2,1,0:T(8,128)(2,1)} %get-tuple-element.64.interps) | copy-start | bytes 983044
  10.5 17.8 %copy-start.4 = (bf16[17,80,256]{2,1,0:T(8,128)(2,1)S(1)}, bf16[17,80,256]{2,1,0:T(8,128)(2,1)}, u32[]{:S(2)}) copy-start(bf16[17,80,256]{2,1,0:T(8,128)(2,1)} %get-tuple-element.62.own) | copy-start | bytes 2088964
  10.6 17.8 %copy-start.7 = (s32[5,1,128]{2,1,0:T(1,128)S(1)}, s32[5,1,128]{2,1,0:T(1,128)}, u32[]{:S(2)}) copy-start(s32[5,1,128]{2,1,0:T(1,128)} %get-tuple-element.63.skels) | copy-start | bytes 7684
  10.6 17.2 %collective-permute-start = (bf16[2064,128]{1,0:T(8,128)(2,1)}, bf16[2064,128]{1,0:T(8,128)(2,1)S(1)}, u32[]{:S(2)}, u32[]{:S(2)}) collective-permute-start(bf16[2064,128]{1,0:T(8,128)(2,1)} %get-tuple-element.59.refs_3_.refs_4_), channel_id=1, source_target_pairs={{0,2},{1,3},{2,0},{3,1},{4,6},{5,7},{6,4},{7,5},{8,10},{9,11},{10,... | collective-permute-start | bytes 1585160 | tf_op jit(solution)/shard_map/ppermute | solution.py:752
  13.6 14.8 %collective-permute-start.1 = (bf16[17,80,256]{2,1,0:T(8,128)(2,1)}, bf16[17,80,256]{2,1,0:T(8,128)(2,1)S(1)}, u32[]{:S(2)}, u32[]{:S(2)}) collective-permute-start(bf16[17,80,256]{2,1,0:T(8,128)(2,1)} %get-tuple-element.62.own), channel_id=1, source_target_pairs={{0,1},{1,0},{2,3},{3,2},{4,5},{5,4},{6,7},{7,6},{8,9},{9,8},{10,11... | collective-permute-start | bytes 2088968 | tf_op jit(solution)/shard_map/ppermute | solution.py:752
  13.6 24.6 %collective-permute-start.3 = (bf16[2064,128]{1,0:T(8,128)(2,1)}, bf16[2064,128]{1,0:T(8,128)(2,1)S(1)}, u32[]{:S(2)}, u32[]{:S(2)}) collective-permute-start(bf16[2064,128]{1,0:T(8,128)(2,1)} %get-tuple-element.59.refs_3_.refs_4_), channel_id=1, source_target_pairs={{0,8},{1,9},{2,10},{3,11},{4,12},{5,13},{6,14},{7,15},{8,0},{9,1},... | collective-permute-start | bytes 1585160 | tf_op jit(solution)/shard_map/ppermute | solution.py:752
  15.2 23.4 %collective-permute-start.4 = (bf16[16,80,256]{2,1,0:T(8,128)(2,1)}, bf16[16,80,256]{2,1,0:T(8,128)(2,1)S(1)}, u32[]{:S(2)}, u32[]{:S(2)}) collective-permute-start(bf16[16,80,256]{2,1,0:T(8,128)(2,1)} %get-tuple-element.70.refs_6_.refs_8_), channel_id=1, source_target_pairs={{0,4},{1,5},{2,6},{3,7},{4,0},{5,1},{6,2},{7,3},{8,12},{9,13},{10,... | collective-permute-start | bytes 1966088 | tf_op jit(solution)/shard_map/ppermute | solution.py:752
  16.7 31.9 %collective-permute-start.8 = (bf16[16,80,256]{2,1,0:T(8,128)(2,1)}, bf16[16,80,256]{2,1,0:T(8,128)(2,1)}, u32[]{:S(2)}, u32[]{:S(2)}) collective-permute-start(bf16[16,80,256]{2,1,0:T(8,128)(2,1)} %get-tuple-element.70.refs_6_.refs_8_), channel_id=1, source_target_pairs={{0,16},{1,17},{2,18},{3,19},{4,20},{5,21},{6,22},{7,23},{8,24},{9,... | collective-permute-start | bytes 1966088 | tf_op jit(solution)/shard_map/ppermute | solution.py:752
  28.6 10.0 %copy-start.2 = (bf16[16,80,256]{2,1,0:T(8,128)(2,1)S(1)}, bf16[16,80,256]{2,1,0:T(8,128)(2,1)}, u32[]{:S(2)}) copy-start(bf16[16,80,256]{2,1,0:T(8,128)(2,1)} %get-tuple-element.70.refs_6_.refs_8_) | copy-start | bytes 1966084
  28.6 10.0 %copy-start.3 = (bf16[2064,128]{1,0:T(8,128)(2,1)S(1)}, bf16[2064,128]{1,0:T(8,128)(2,1)}, u32[]{:S(2)}) copy-start(bf16[2064,128]{1,0:T(8,128)(2,1)} %get-tuple-element.59.refs_3_.refs_4_) | copy-start | bytes 1585156
  28.6 10.0 %copy-start.13 = (s32[2,128]{1,0:T(2,128)S(1)}, s32[2,128]{1,0:T(2,128)}, u32[]{:S(2)}) copy-start(s32[2,128]{1,0:T(2,128)} %get-tuple-element.68.refs_1_) | copy-start | bytes 3076
  28.6 18.3 %collective-permute-start.2 = (bf16[80,128]{1,0:T(8,128)(2,1)S(1)}, bf16[80,128]{1,0:T(8,128)(2,1)S(1)}, u32[]{:S(2)}, u32[]{:S(2)}) collective-permute-start(bf16[80,128]{1,0:T(8,128)(2,1)S(1)} %climb0.1.own), channel_id=1, source_target_pairs={{0,2},{1,3},{2,0},{3,1},{4,6},{5,7},{6,4},{7,5},{8,10},{9,11},{10,... | collective-permute-start | bytes 61448 | tf_op jit(solution)/shard_map/ppermute | solution.py:752
  35.7 20.3 %copy-start.11 = (s32[2,128]{1,0:T(2,128)S(1)}, s32[2,128]{1,0:T(2,128)}, u32[]{:S(2)}) copy-start(s32[2,128]{1,0:T(2,128)} %get-tuple-element.74.refs_1_) | copy-start | bytes 3076
  35.7 20.3 %copy-start.12 = (s32[2,128]{1,0:T(2,128)S(1)}, s32[2,128]{1,0:T(2,128)}, u32[]{:S(2)}) copy-start(s32[2,128]{1,0:T(2,128)} %get-tuple-element.75.refs_2_) | copy-start | bytes 3076
  38.2 13.7 %collective-permute-start.6 = (bf16[2064,128]{1,0:T(8,128)(2,1)S(1)}, bf16[2064,128]{1,0:T(8,128)(2,1)S(1)}, u32[]{:S(2)}, u32[]{:S(2)}) collective-permute-start(bf16[2064,128]{1,0:T(8,128)(2,1)S(1)} %collective-permute-done.3.refs_5_.refs_6_), channel_id=1, source_target_pairs={{0,2},{1,3},{2,0},{3,1},{4,6},{5,7},{6,4},{7,5},{8,10},{9,11},{10,... | collective-permute-start | bytes 1585160 | tf_op jit(solution)/shard_map/ppermute | solution.py:752
  48.6 3.3 %collective-permute-start.9 = (bf16[16,80,256]{2,1,0:T(8,128)(2,1)}, bf16[16,80,256]{2,1,0:T(8,128)(2,1)S(1)}, u32[]{:S(2)}, u32[]{:S(2)}) collective-permute-start(bf16[16,80,256]{2,1,0:T(8,128)(2,1)} %collective-permute-done.8.refs_12_), channel_id=1, source_target_pairs={{0,1},{1,0},{2,3},{3,2},{4,5},{5,4},{6,7},{7,6},{8,9},{9,8},{10,11... | collective-permute-start | bytes 1966088 | tf_op jit(solution)/shard_map/ppermute | solution.py:752
  48.6 7.4 %collective-permute-start.7 = (bf16[16,80,256]{2,1,0:T(8,128)(2,1)S(1)}, bf16[16,80,256]{2,1,0:T(8,128)(2,1)S(1)}, u32[]{:S(2)}, u32[]{:S(2)}) collective-permute-start(bf16[16,80,256]{2,1,0:T(8,128)(2,1)S(1)} %collective-permute-done.4.refs_8_.refs_10_), channel_id=1, source_target_pairs={{0,1},{1,0},{2,3},{3,2},{4,5},{5,4},{6,7},{7,6},{8,9},{9,8},{10,11... | collective-permute-start | bytes 1966088 | tf_op jit(solution)/shard_map/ppermute | solution.py:752
  49.1 18.8 %collective-permute-start.13 = (bf16[16,80,256]{2,1,0:T(8,128)(2,1)}, bf16[16,80,256]{2,1,0:T(8,128)(2,1)S(1)}, u32[]{:S(2)}, u32[]{:S(2)}) collective-permute-start(bf16[16,80,256]{2,1,0:T(8,128)(2,1)} %collective-permute-done.8.refs_12_), channel_id=1, source_target_pairs={{0,4},{1,5},{2,6},{3,7},{4,0},{5,1},{6,2},{7,3},{8,12},{9,13},{10,... | collective-permute-start | bytes 1966088 | tf_op jit(solution)/shard_map/ppermute | solution.py:752
  49.6 17.9 %collective-permute-start.5 = (bf16[80,128]{1,0:T(8,128)(2,1)S(1)}, bf16[80,128]{1,0:T(8,128)(2,1)S(1)}, u32[]{:S(2)}, u32[]{:S(2)}) collective-permute-start(bf16[80,128]{1,0:T(8,128)(2,1)S(1)} %climb1.1.own), channel_id=1, source_target_pairs={{0,4},{1,5},{2,6},{3,7},{4,0},{5,1},{6,2},{7,3},{8,12},{9,13},{10,... | collective-permute-start | bytes 61448 | tf_op jit(solution)/shard_map/ppermute | solution.py:752
  51.9 15.6 %collective-permute-start.10 = (bf16[80,128]{1,0:T(8,128)(2,1)S(1)}, bf16[80,128]{1,0:T(8,128)(2,1)S(1)}, u32[]{:S(2)}, u32[]{:S(2)}) collective-permute-start(bf16[80,128]{1,0:T(8,128)(2,1)S(1)} %climb1.1.own), channel_id=1, source_target_pairs={{0,8},{1,9},{2,10},{3,11},{4,12},{5,13},{6,14},{7,15},{8,0},{9,1},... | collective-permute-start | bytes 61448 | tf_op jit(solution)/shard_map/ppermute | solution.py:752
  51.9 15.6 %collective-permute-start.11 = (bf16[80,128]{1,0:T(8,128)(2,1)S(1)}, bf16[80,128]{1,0:T(8,128)(2,1)S(1)}, u32[]{:S(2)}, u32[]{:S(2)}) collective-permute-start(bf16[80,128]{1,0:T(8,128)(2,1)S(1)} %climb1.1.own), channel_id=1, source_target_pairs={{0,12},{1,13},{2,14},{3,15},{4,8},{5,9},{6,10},{7,11},{8,4},{9,5},... | collective-permute-start | bytes 61448 | tf_op jit(solution)/shard_map/ppermute | solution.py:752
  56.0 14.0 %copy-start.9 = (s32[2,128]{1,0:T(2,128)S(1)}, s32[2,128]{1,0:T(2,128)}, u32[]{:S(2)}) copy-start(s32[2,128]{1,0:T(2,128)} %get-tuple-element.83.refs_0_) | copy-start | bytes 3076
  56.0 14.0 %copy-start.10 = (s32[2,128]{1,0:T(2,128)S(1)}, s32[2,128]{1,0:T(2,128)}, u32[]{:S(2)}) copy-start(s32[2,128]{1,0:T(2,128)} %get-tuple-element.84.refs_1_) | copy-start | bytes 3076
  67.8 2.2 %collective-permute-start.14 = (bf16[16,80,256]{2,1,0:T(8,128)(2,1)S(1)}, bf16[16,80,256]{2,1,0:T(8,128)(2,1)S(1)}, u32[]{:S(2)}, u32[]{:S(2)}) collective-permute-start(bf16[16,80,256]{2,1,0:T(8,128)(2,1)S(1)} %collective-permute-done.13.refs_5_), channel_id=1, source_target_pairs={{0,1},{1,0},{2,3},{3,2},{4,5},{5,4},{6,7},{7,6},{8,9},{9,8},{10,11... | collective-permute-start | bytes 1966088 | tf_op jit(solution)/shard_map/ppermute | solution.py:752
  67.9 6.4 %collective-permute-start.12 = (bf16[80,128]{1,0:T(8,128)(2,1)S(1)}, bf16[80,128]{1,0:T(8,128)(2,1)S(1)}, u32[]{:S(2)}, u32[]{:S(2)}) collective-permute-start(bf16[80,128]{1,0:T(8,128)(2,1)S(1)} %get-tuple-element.82), channel_id=1, source_target_pairs={{0,16},{1,17},{2,18},{3,19},{4,20},{5,21},{6,22},{7,23},{8,24},{9,... | collective-permute-start | bytes 61448 | tf_op jit(solution)/shard_map/ppermute | solution.py:752
  70.0 8.8 %copy-start = (bf16[16,256,128]{2,1,0:T(8,128)(2,1)S(1)}, bf16[16,256,128]{2,1,0:T(8,128)(2,1)}, u32[]{:S(2)}) copy-start(bf16[16,256,128]{2,1,0:T(8,128)(2,1)} %get-tuple-element.92.refs_5_) | copy-start | bytes 3145732
  74.3 11.3 %copy-start.5 = (f32[256,128]{1,0:T(8,128)S(1)}, f32[256,128]{1,0:T(8,128)}, u32[]{:S(2)}) copy-start(f32[256,128]{1,0:T(8,128)} %get-tuple-element.58.refs_0_) | copy-start | bytes 393220
  74.3 11.3 %copy-start.6 = (f32[256,128]{1,0:T(8,128)S(1)}, f32[256,128]{1,0:T(8,128)}, u32[]{:S(2)}) copy-start(f32[256,128]{1,0:T(8,128)} %get-tuple-element.66.refs_1_) | copy-start | bytes 393220
  74.3 11.3 %copy-start.8 = (f32[16,1,256]{2,1,0:T(1,128)S(1)}, f32[16,1,256]{2,1,0:T(1,128)}, u32[]{:S(2)}) copy-start(f32[16,1,256]{2,1,0:T(1,128)} %get-tuple-element.53.refs_3_) | copy-start | bytes 49156
  74.3 8.4 %collective-permute-start.17 = (bf16[2,256,128]{2,1,0:T(8,128)(2,1)S(1)}, bf16[2,256,128]{2,1,0:T(8,128)(2,1)S(1)}, u32[]{:S(2)}, u32[]{:S(2)}) collective-permute-start(bf16[2,256,128]{2,1,0:T(8,128)(2,1)S(1)} %get-tuple-element.98), channel_id=1, source_target_pairs={{0,10},{1,11},{2,8},{3,9},{4,14},{5,15},{6,12},{7,13},{8,2},{9,3},... | collective-permute-start | bytes 393224 | tf_op jit(solution)/shard_map/ppermute | solution.py:752
  77.6 8.1 %collective-permute-start.16 = (bf16[2,256,128]{2,1,0:T(8,128)(2,1)S(1)}, bf16[2,256,128]{2,1,0:T(8,128)(2,1)S(1)}, u32[]{:S(2)}, u32[]{:S(2)}) collective-permute-start(bf16[2,256,128]{2,1,0:T(8,128)(2,1)S(1)} %get-tuple-element.96), channel_id=1, source_target_pairs={{0,8},{1,9},{2,10},{3,11},{4,12},{5,13},{6,14},{7,15},{8,0},{9,1},... | collective-permute-start | bytes 393224 | tf_op jit(solution)/shard_map/ppermute | solution.py:752
  78.8 6.8 %collective-permute-start.15 = (bf16[2,256,128]{2,1,0:T(8,128)(2,1)S(1)}, bf16[2,256,128]{2,1,0:T(8,128)(2,1)S(1)}, u32[]{:S(2)}, u32[]{:S(2)}) collective-permute-start(bf16[2,256,128]{2,1,0:T(8,128)(2,1)S(1)} %get-tuple-element.94), channel_id=1, source_target_pairs={{0,2},{1,3},{2,0},{3,1},{4,6},{5,7},{6,4},{7,5},{8,10},{9,11},{10,... | collective-permute-start | bytes 393224 | tf_op jit(solution)/shard_map/ppermute | solution.py:752
  (1 other events, 0.7 us)

commit v5 on v4

--- a/solution.py
+++ b/solution.py
@@ -471,7 +471,7 @@
     return out[0], [out[1 + PHASES * k : 1 + PHASES * k + PHASES] for k in range(len(codes))]
 
 
-def near_kernel(*refs, n_sources, n_targets, n_lists, phase):
+def near_kernel(*refs, n_sources, n_targets, n_lists, n_codes, phase):
     refs = list(refs)
 
     def take(n):
@@ -480,14 +480,14 @@
         return taken
 
     makes = phase < PHASES - 1
-    (codes,) = take(1) if makes else (None,)
+    codes = take(n_codes)
     lists = take(n_lists)
     target_parts = take(n_targets if makes else 1)
     source_parts = take(n_sources)
     before = take(phase > 0)
     outs = take(n_targets) if not makes else []
     (acc,) = take(1) if makes else (None,)
-    tables = take(PHASES - 1 - phase) if makes else []
+    tables = [take(PHASES - 1 - phase) for _ in range(n_codes)]
     if phase == 1:
         (targets,) = take(1)
     elif phase == 2:
@@ -514,9 +514,9 @@
     for k, part in enumerate(source_parts):
         begin(part.at[pl.ds(0, leaves)], sources.at[pl.ds(k * leaves, leaves)])
     acc[...] = jnp.zeros_like(acc)
-    if makes:
-        table = pairs.at[pl.ds(n_lists * own_rows, own_rows)]
-        list_pairs(codes, [None] * phase + [table] + tables)
+    for k in range(n_codes):
+        table = pairs.at[pl.ds((n_lists + k) * own_rows, own_rows)]
+        list_pairs(codes[k], [None] * phase + [table] + tables[k])
     for copy in copies:
         copy.wait()
 
@@ -572,23 +572,23 @@
         out[...] = (acc[mine] + before[0][mine]).astype(bf16)
 
 
-def near(phase, lists, targets, sources, codes=None, before=None):
-    n_sources = len(sources)
+def near(phase, lists, targets, sources, codes=(), before=None):
+    n_sources, n_codes = len(sources), len(codes)
     makes = phase < PHASES - 1
     n_targets = len(targets) if makes else len(lists)
     leaves = min(source.shape[0] for source in sources)
     sums = jax.ShapeDtypeStruct((n_targets * leaves // 8, 256, 128), f32)
     part = jax.ShapeDtypeStruct((leaves // 8, 256, 128), bf16)
     held_targets = jax.ShapeDtypeStruct((n_targets * leaves * 128, 128), bf16)
-    args = ([codes] if makes else []) + list(lists) + list(targets) + list(sources)
-    in_specs = [SMEM] * int(makes) + [ANY] * (len(args) - int(makes))
+    args = list(codes) + list(lists) + list(targets) + list(sources)
+    in_specs = [SMEM] * n_codes + [ANY] * (len(args) - n_codes)
     if not makes:
         in_specs[len(lists)] = VMEM
     if before is not None:
         args.append(before)
         in_specs.append(VMEM)
     if makes:
-        n_tables = PHASES - 1 - phase
+        n_tables = n_codes * (PHASES - 1 - phase)
         out_shape = (sums,) + (pair_table(leaves),) * n_tables
         out_specs = (VMEM,) + (SMEM,) * n_tables
         if phase == 1:
@@ -607,7 +607,12 @@
         scratch.append(pltpu.VMEM(sums.shape, f32))
     return pl.pallas_call(
         functools.partial(
-            near_kernel, n_sources=n_sources, n_targets=n_targets, n_lists=len(lists), phase=phase
+            near_kernel,
+            n_sources=n_sources,
+            n_targets=n_targets,
+            n_lists=len(lists),
+            n_codes=n_codes,
+            phase=phase,
         ),
         out_shape=out_shape,
         in_specs=in_specs,
@@ -804,9 +809,10 @@
         )
 
     far0, lists0 = far(0, [codes], norms)
-    node = climb(me, after(mine, far0, beside), pieces[1], skels, interps, 0, 0)
+    node = climb(me, after(mine, far0), pieces[1], skels, interps, 0, 0)
     siblings = [pieces[1], swap(node, 2)]
-    far1, lists1 = far(1, [payload_codes(after(beside, far0), 0)], node)
+    far1, _ = far(1, [], node)
+    node = climb(me, node, after(siblings[1], far1), skels, interps, 1, 1)
     last_targets = swap(after(far_away, far1), 2 ** TARGET_BITS[0])
     for n, b in enumerate(early_bits):
         for low in range(2**n):
@@ -815,15 +821,23 @@
                 pieces[place | 2**b] = swap(pieces[place], 2**b)
     wanted = [spread(k, source_bits) for k in range(2 ** (len(source_bits) - 1))]
     targets = [tgt, beside, far_away, last_targets]
-    lists = lists0 + lists1
-    sums, far_tables1, far_tables2 = near(
+    lists = lists0
+    height, row = 2, 2
+    others = [swap(node, k * 2**height) for k in (1, 2, 3)]
+    sums, *tables = near(
         0,
-        [tables[0] for tables in lists],
+        [lists[0][0]],
         targets[:3],
         [pieces[k] for k in wanted if k == 1 or not k & 1],
-        codes=payload_codes(after(far_away, far1), 0),
+        codes=[payload_codes(after(part, far1, node), 0) for part in (beside, far_away)],
     )
-    node = climb(me, node, after(siblings[1], sums), skels, interps, 1, 1)
+    others[0] = after(others[0], sums)
+    while height + 1 < bits:
+        if height > 2:
+            others = [swap(node, k * 2**height) for k in (1, 2, 3)]
+        sibling, node = climb_two(me, node, others, skels, interps, height, row)
+        siblings += [others[0], sibling]
+        height, row = height + 2, row + 3
     for k in wanted[2::2]:
         pieces[k | 1] = swap(after(pieces[k], node), 1)
     pieces[late] = after(pieces[late], node)
@@ -832,30 +846,21 @@
             place = spread(low, early_bits[:n]) | late
             pieces[place | 2**b] = swap(pieces[place], 2**b)
     pieces[late | 1] = swap(pieces[late], 1)
-    height, row = 2, 2
-    others = [swap(node, k * 2**height) for k in (1, 2, 3)]
+    if height < bits:
+        siblings.append(swap(node, 2**height))
     sums, last_table, all_targets = near(
         1,
-        [tables[1] for tables in lists] + [far_tables1],
+        [lists[0][1], tables[0], tables[2]],
         targets,
         [pieces[k] for k in wanted + [late, late | 1]],
-        codes=payload_codes(after(last_targets, node), 1),
+        codes=[payload_codes(after(last_targets, node), 1)],
         before=sums,
     )
-    others[0] = after(others[0], sums)
-    while height + 1 < bits:
-        if height > 2:
-            others = [swap(node, k * 2**height) for k in (1, 2, 3)]
-        sibling, node = climb_two(me, node, others, skels, interps, height, row)
-        siblings += [others[0], sibling]
-        height, row = height + 2, row + 3
-    if height < bits:
-        siblings.append(swap(node, 2**height))
     for k in wanted[2::2]:
-        pieces[k | late | 1] = swap(after(pieces[k | late], node), 1)
+        pieces[k | late | 1] = swap(after(pieces[k | late], sums), 1)
     parts = near(
         2,
-        [tables[2] for tables in lists] + [far_tables2, after(last_table, node)],
+        [lists[0][2], tables[1], tables[3], last_table],
         [all_targets],
         [pieces[k | late] for k in wanted[2:]],
         before=sums,

time: 87.1 us -> 87.6 us (level)
  starting transfers between devices: 20.4 us -> 24.4 us
  waiting for transfers between devices: 9.71 us -> 7.66 us
    ppermute x18, starting transfers between devices: 20.4 us -> 24.4 us  [swap(): return lax.ppermute(value, 'leaf', pairs)]
    ppermute x18, waiting for transfers between devices: 9.71 us -> 7.66 us  [swap(): return lax.ppermute(value, 'leaf', pairs)]
    pallas_call x2, Pallas kernels: 15.3 us -> 14.2 us  [self_and_far(): pl.pallas_call(functools.partial(far_kernel, first_leaf=call * n_leaves,...]
    pallas_call x3, Pallas kernels: 23.4 us -> 24.5 us  [near(): pl.pallas_call(functools.partial(near_kernel, n_sources=n_sources, n_targ...]
  transfers between devices with their start and end apart: 18 -> 18, of which waited for: 5 -> 5; matrix products, arithmetic and copies ran while one was open for 1% -> 0% of each run, Pallas kernels for 50% -> 50%
where the time goes in v5:
time: 87.6 us; the launch traced here: 87 us
  Pallas kernels  54.6 us (62%)
  starting transfers between devices  24.4 us (28%)
  waiting for transfers between devices  7.66 us (9%)
    pallas_call x3, Pallas kernels, near(): pl.pallas_call(functools.partial(near_kernel, n_sources=n_sources, n_targ...  24.5 us
    ppermute x18, starting transfers between devices, swap(): return lax.ppermute(value, 'leaf', pairs)  24.4 us
    pallas_call x2, Pallas kernels, self_and_far(): pl.pallas_call(functools.partial(far_kernel, first_leaf=call * n_leaves,...  14.2 us
    pallas_call x1, Pallas kernels, first_part(): pl.pallas_call(first_kernel, out_shape=tuple((jax.ShapeDtypeStruct(*shape...  10.5 us
    ppermute x18, waiting for transfers between devices, swap(): return lax.ppermute(value, 'leaf', pairs)  7.66 us
    pallas_call x1, Pallas kernels, top(): pl.pallas_call(top_kernel, out_shape=jax.ShapeDtypeStruct((rows.shape[0]...  3.87 us
  transfers between devices with their start and end apart: 18, of which 5 were waited for; matrix products, arithmetic and copies ran while one was open for 0% of the time, Pallas kernels for 50%

profile of v5, /device:TPU:0, one launch (start us, length us, event | category | flops | bytes accessed | tf_op | source)
XLA Modules:
  0.0 87.0 jit_solution(8323103671730032561)
XLA Ops:
  0.0 10.5 %order_and_subtree.1 = (bf16[16,80,256]{2,1,0:T(8,128)(2,1)}, bf16[2064,128]{1,0:T(8,128)(2,1)}, bf16[64,128,128]{2,1,0:T(8,128)(2,1)}, bf16[64,16,128]{2,1,0:T(...) custom-call(s32[4096]{0:T(1024)} %order_in.1, ...), custom_call_target="tpu_custom_call" | custom-call | flops 1 | bytes 1 | tf_op jit(solution)/shard_map/order_and_subtree/pallas_call | solution.py:341
  10.6 0.5 collective-permute-start
  11.1 2.6 %collective-permute-start.4 = (bf16[2064,128]{1,0:T(8,128)(2,1)}, bf16[2064,128]{1,0:T(8,128)(2,1)S(1)}, u32[]{:S(2)}, u32[]{:S(2)}) collective-permute-start(bf16[2064,128]{1,0:T(8,128)(2,1)} %get-tuple-element.63.refs_3_.refs_4_), channel_id=1, source_target_pairs={{0,8},{1,9},{2,10},{3,11},{4,12},{5,13},{6,14},{7,15},{8,0},{9,1},... | collective-permute-start | bytes 1585160 | tf_op jit(solution)/shard_map/ppermute | solution.py:757
  13.7 1.5 %collective-permute-start.3 = (bf16[2064,128]{1,0:T(8,128)(2,1)}, bf16[2064,128]{1,0:T(8,128)(2,1)S(1)}, u32[]{:S(2)}, u32[]{:S(2)}) collective-permute-start(bf16[2064,128]{1,0:T(8,128)(2,1)} %get-tuple-element.63.refs_3_.refs_4_), channel_id=1, source_target_pairs={{0,2},{1,3},{2,0},{3,1},{4,6},{5,7},{6,4},{7,5},{8,10},{9,11},{10,... | collective-permute-start | bytes 1585160 | tf_op jit(solution)/shard_map/ppermute | solution.py:757
  15.2 1.5 %collective-permute-start.5 = (bf16[16,80,256]{2,1,0:T(8,128)(2,1)}, bf16[16,80,256]{2,1,0:T(8,128)(2,1)S(1)}, u32[]{:S(2)}, u32[]{:S(2)}) collective-permute-start(bf16[16,80,256]{2,1,0:T(8,128)(2,1)} %get-tuple-element.67.refs_6_.refs_8_), channel_id=1, source_target_pairs={{0,4},{1,5},{2,6},{3,7},{4,0},{5,1},{6,2},{7,3},{8,12},{9,13},{10,... | collective-permute-start | bytes 1966088 | tf_op jit(solution)/shard_map/ppermute | solution.py:757
  16.7 2.6 %collective-permute-start.11 = (bf16[16,80,256]{2,1,0:T(8,128)(2,1)}, bf16[16,80,256]{2,1,0:T(8,128)(2,1)}, u32[]{:S(2)}, u32[]{:S(2)}) collective-permute-start(bf16[16,80,256]{2,1,0:T(8,128)(2,1)} %get-tuple-element.67.refs_6_.refs_8_), channel_id=1, source_target_pairs={{0,16},{1,17},{2,18},{3,19},{4,20},{5,21},{6,22},{7,23},{8,24},{9,... | collective-permute-start | bytes 1966088 | tf_op jit(solution)/shard_map/ppermute | solution.py:757
  19.3 7.1 %self_and_far0.1 = (f32[256,128]{1,0:T(8,128)}, s32[2,128]{1,0:T(2,128)}, s32[2,128]{1,0:T(2,128)}, s32[2,128]{1,0:T(2,128)}) custom-call(s32[8,16]{1,0:T(8,128)} %get-tuple-element.50.refs_0_, s32[16,16]{1,0:T(8,128)} %refs_0_, s32[16]{0:T(128)} %refs_1_.2, bf16[64,128,128]{2,1,0:T(8,128)(2,1)} %get-tuple-element.53.refs_3_.refs_2_, ...), custom_call_target="tpu_custom_call" | custom-call | flops 1 | bytes 1 | tf_op jit(solution)/shard_map/self_and_far0/pallas_call | solution.py:453
  26.5 0.1 climb0.1.own
  26.7 1.2 %collective-permute-start.1 = (bf16[80,128]{1,0:T(8,128)(2,1)S(1)}, bf16[80,128]{1,0:T(8,128)(2,1)S(1)}, u32[]{:S(2)}, u32[]{:S(2)}) collective-permute-start(bf16[80,128]{1,0:T(8,128)(2,1)S(1)} %climb0.1.own), channel_id=1, source_target_pairs={{0,2},{1,3},{2,0},{3,1},{4,6},{5,7},{6,4},{7,5},{8,10},{9,11},{10,... | collective-permute-start | bytes 61448 | tf_op jit(solution)/shard_map/ppermute | solution.py:757
  27.9 7.1 %self_and_far1.1.refs_1_ = f32[256,128]{1,0:T(8,128)} custom-call(s32[16,16]{1,0:T(8,128)} %refs_0_, s32[16]{0:T(128)} %refs_1_.2, bf16[64,128,128]{2,1,0:T(8,128)(2,1)} %get-tuple-element.53.refs_3_.refs_2_, bf16[64,16,128]{2,1,0:T(8,128)(2,1)} %get-tuple-element.54.refs_4_.refs_3_, bf16[16,256,128]{2,1,0:T(8,128)(2,1)} %get-tuple-element.88.refs_5_.refs_4_), custom_call_target="tpu_custom_call" | custom-call | flops 1 | bytes 1 | tf_op jit(solution)/shard_map/self_and_far1/pallas_call | solution.py:453
  35.0 0.3 collective-permute-done.4.refs_5_.refs_6_
  35.3 2.6 %collective-permute-start.9 = (bf16[2064,128]{1,0:T(8,128)(2,1)S(1)}, bf16[2064,128]{1,0:T(8,128)(2,1)S(1)}, u32[]{:S(2)}, u32[]{:S(2)}) collective-permute-start(bf16[2064,128]{1,0:T(8,128)(2,1)S(1)} %collective-permute-done.4.refs_5_.refs_6_), channel_id=1, source_target_pairs={{0,2},{1,3},{2,0},{3,1},{4,6},{5,7},{6,4},{7,5},{8,10},{9,11},{10,... | collective-permute-start | bytes 1585160 | tf_op jit(solution)/shard_map/ppermute | solution.py:757
  37.9 0.1 climb1.1.own
  38.1 2.6 %collective-permute-start.2 = (bf16[80,128]{1,0:T(8,128)(2,1)S(1)}, bf16[80,128]{1,0:T(8,128)(2,1)S(1)}, u32[]{:S(2)}, u32[]{:S(2)}) collective-permute-start(bf16[80,128]{1,0:T(8,128)(2,1)S(1)} %climb1.1.own), channel_id=1, source_target_pairs={{0,4},{1,5},{2,6},{3,7},{4,0},{5,1},{6,2},{7,3},{8,12},{9,13},{10,... | collective-permute-start | bytes 61448 | tf_op jit(solution)/shard_map/ppermute | solution.py:757
  40.7 1.6 %collective-permute-start.7 = (bf16[80,128]{1,0:T(8,128)(2,1)S(1)}, bf16[80,128]{1,0:T(8,128)(2,1)S(1)}, u32[]{:S(2)}, u32[]{:S(2)}) collective-permute-start(bf16[80,128]{1,0:T(8,128)(2,1)S(1)} %climb1.1.own), channel_id=1, source_target_pairs={{0,12},{1,13},{2,14},{3,15},{4,8},{5,9},{6,10},{7,11},{8,4},{9,5},... | collective-permute-start | bytes 61448 | tf_op jit(solution)/shard_map/ppermute | solution.py:757
  42.4 8.8 %near0.1 = (f32[6,256,128]{2,1,0:T(8,128)S(1)}, s32[2,128]{1,0:T(2,128)S(1)}, s32[2,128]{1,0:T(2,128)S(1)}, s32[2,128]{1,0:T(2,128)S(1)}, s32[2,128]{1,0:T(2,128)S(1)}) custom-call(s32[8,16]{1,0:T(8,128)S(1)} %get-tuple-element.96.refs_0_, s32[8,16]{1,0:T(8,128)S(1)} %get-tuple-element.95.refs_1_, s32[2,128]{1,0:T(2,128)S(1)} %copy-done.11, ...), custom_call_target="tpu_custom_call" | custom-call | flops 1 | bytes 1 | tf_op jit(solution)/shard_map/near0/pallas_call | solution.py:608
  51.2 0.3 climb2.1
  51.5 0.1 collective-permute-start.10
  51.5 0.5 collective-permute-start.12
  52.0 2.3 %collective-permute-start.13 = (bf16[16,80,256]{2,1,0:T(8,128)(2,1)}, bf16[16,80,256]{2,1,0:T(8,128)(2,1)S(1)}, u32[]{:S(2)}, u32[]{:S(2)}) collective-permute-start(bf16[16,80,256]{2,1,0:T(8,128)(2,1)} %collective-permute-done.11.refs_12_), channel_id=1, source_target_pairs={{0,4},{1,5},{2,6},{3,7},{4,0},{5,1},{6,2},{7,3},{8,12},{9,13},{10,... | collective-permute-start | bytes 1966088 | tf_op jit(solution)/shard_map/ppermute | solution.py:757
  54.4 0.4 collective-permute-done.12.refs_13_
  54.8 10.5 %near1.1 = (f32[8,256,128]{2,1,0:T(8,128)S(1)}, s32[2,128]{1,0:T(2,128)S(1)}, bf16[8192,128]{1,0:T(8,128)(2,1)S(1)}) custom-call(s32[8,16]{1,0:T(8,128)S(1)} %fusion.11.refs_0_, s32[2,128]{1,0:T(2,128)S(1)} %copy-done.10, s32[2,128]{1,0:T(2,128)S(1)} %get-tuple-element.78.refs_2_, s32[2,128]{1,0:T(2,128)S(1)} %get-tuple-element.79.refs_3_, ...), custom_call_target="tpu_custom_call" | custom-call | flops 1 | bytes 1 | tf_op jit(solution)/shard_map/near1/pallas_call | solution.py:608
  65.3 4.2 %collective-permute-done.13.refs_5_ = bf16[16,80,256]{2,1,0:T(8,128)(2,1)S(1)} collective-permute-done((bf16[16,80,256]{2,1,0:T(8,128)(2,1)}, bf16[16,80,256]{2,1,0:T(8,128)(2,1)S(1)}, u32[]{:S(2)}, u32[]{:S(2)}) %collective-permute-start.13) | collective-permute-done | bytes 655392 | tf_op jit(solution)/shard_map/ppermute | solution.py:757
  69.5 1.1 %collective-permute-start.8 = (bf16[80,128]{1,0:T(8,128)(2,1)S(1)}, bf16[80,128]{1,0:T(8,128)(2,1)S(1)}, u32[]{:S(2)}, u32[]{:S(2)}) collective-permute-start(bf16[80,128]{1,0:T(8,128)(2,1)S(1)} %get-tuple-element.71), channel_id=1, source_target_pairs={{0,16},{1,17},{2,18},{3,19},{4,20},{5,21},{6,22},{7,23},{8,24},{9,... | collective-permute-start | bytes 61448 | tf_op jit(solution)/shard_map/ppermute | solution.py:757
  70.6 1.0 %collective-permute-done.14.refs_6_ = bf16[16,80,256]{2,1,0:T(8,128)(2,1)S(1)} collective-permute-done((bf16[16,80,256]{2,1,0:T(8,128)(2,1)S(1)}, bf16[16,80,256]{2,1,0:T(8,128)(2,1)S(1)}, u32[]{:S(2)}, u32[]{:S(2)}) %collective-permute-start.14) | collective-permute-done | bytes 655392 | tf_op jit(solution)/shard_map/ppermute | solution.py:757
  71.6 5.2 %near2.1 = (bf16[2,256,128]{2,1,0:T(8,128)(2,1)S(1)}, bf16[2,256,128]{2,1,0:T(8,128)(2,1)S(1)}, bf16[2,256,128]{2,1,0:T(8,128)(2,1)S(1)}, bf16[2,256,128]{2,1,0:T(8,128)(2,1)S(1)}) custom-call(s32[2,128]{1,0:T(2,128)S(1)} %copy-done.9, s32[2,128]{1,0:T(2,128)S(1)} %get-tuple-element.73.refs_1_, s32[2,128]{1,0:T(2,128)S(1)} %get-tuple-element.74.refs_2_, ...), custom_call_target="tpu_custom_call" | custom-call | flops 1 | bytes 1 | tf_op jit(solution)/shard_map/near2/pallas_call | solution.py:608
  76.9 0.3 collective-permute-start.15
  77.2 1.4 %collective-permute-start.16 = (bf16[2,256,128]{2,1,0:T(8,128)(2,1)S(1)}, bf16[2,256,128]{2,1,0:T(8,128)(2,1)S(1)}, u32[]{:S(2)}, u32[]{:S(2)}) collective-permute-start(bf16[2,256,128]{2,1,0:T(8,128)(2,1)S(1)} %get-tuple-element.92), channel_id=1, source_target_pairs={{0,8},{1,9},{2,10},{3,11},{4,12},{5,13},{6,14},{7,15},{8,0},{9,1},... | collective-permute-start | bytes 393224 | tf_op jit(solution)/shard_map/ppermute | solution.py:757
  78.6 1.8 %collective-permute-start.17 = (bf16[2,256,128]{2,1,0:T(8,128)(2,1)S(1)}, bf16[2,256,128]{2,1,0:T(8,128)(2,1)S(1)}, u32[]{:S(2)}, u32[]{:S(2)}) collective-permute-start(bf16[2,256,128]{2,1,0:T(8,128)(2,1)S(1)} %get-tuple-element.94), channel_id=1, source_target_pairs={{0,10},{1,11},{2,8},{3,9},{4,14},{5,15},{6,12},{7,13},{8,2},{9,3},... | collective-permute-start | bytes 393224 | tf_op jit(solution)/shard_map/ppermute | solution.py:757
  80.5 3.9 %top.1.refs_2_ = f32[2,256,128]{2,1,0:T(8,128)S(1)} custom-call(bf16[17,80,256]{2,1,0:T(8,128)(2,1)S(1)} %collective-permute-done.other.refs_7_.refs_9_.refs_0_, bf16[80,128]{1,0:T(8,128)(2,1)S(1)} %collective-permute-done.1.other.refs_1_, bf16[80,128]{1,0:T(8,128)(2,1)S(1)} %collective-permute-done.2.one.refs_2_, ...), custom_call_target="tpu_custom_call" | custom-call | flops 1 | bytes 1 | tf_op jit(solution)/shard_map/top/pallas_call | solution.py:707
  84.4 1.7 %collective-permute-done.17.refs_7_ = bf16[2,256,128]{2,1,0:T(8,128)(2,1)S(1)} collective-permute-done((bf16[2,256,128]{2,1,0:T(8,128)(2,1)S(1)}, bf16[2,256,128]{2,1,0:T(8,128)(2,1)S(1)}, u32[]{:S(2)}, u32[]{:S(2)}) %collective-permute-start.17) | collective-permute-done | bytes 131104 | tf_op jit(solution)/shard_map/ppermute | solution.py:757
  86.1 0.9 %last_sum.1 = f32[16,4096]{1,0:T(8,128)} custom-call(f32[256,128]{1,0:T(8,128)S(1)} %copy-done.6, f32[256,128]{1,0:T(8,128)S(1)} %copy-done.5, f32[2,256,128]{2,1,0:T(8,128)S(1)} %top.1.refs_2_, f32[16,1,256]{2,1,0:T(1,128)S(1)} %copy-done.8, bf16[2,256,128]{2,1,0:T(8,128)(2,1)S(1)} %get-tuple-element.86.refs_4_, ...), custom_call_target="tpu_custom_call" | custom-call | flops 1 | bytes 1 | tf_op jit(solution)/shard_map/last_sum/pallas_call | solution.py:744
  (44 shorter events, 0.2 us)
Async XLA Ops:
  10.5 16.0 %copy-start.1 = (bf16[5,256,128]{2,1,0:T(8,128)(2,1)S(1)}, bf16[5,256,128]{2,1,0:T(8,128)(2,1)}, u32[]{:S(2)}) copy-start(bf16[5,256,128]{2,1,0:T(8,128)(2,1)} %get-tuple-element.60.interps) | copy-start | bytes 983044
  10.5 16.0 %copy-start.4 = (bf16[17,80,256]{2,1,0:T(8,128)(2,1)S(1)}, bf16[17,80,256]{2,1,0:T(8,128)(2,1)}, u32[]{:S(2)}) copy-start(bf16[17,80,256]{2,1,0:T(8,128)(2,1)} %get-tuple-element.58.own) | copy-start | bytes 2088964
  10.5 16.0 %copy-start.7 = (s32[5,1,128]{2,1,0:T(1,128)S(1)}, s32[5,1,128]{2,1,0:T(1,128)}, u32[]{:S(2)}) copy-start(s32[5,1,128]{2,1,0:T(1,128)} %get-tuple-element.59.skels) | copy-start | bytes 7684
  10.6 15.9 %collective-permute-start = (bf16[17,80,256]{2,1,0:T(8,128)(2,1)}, bf16[17,80,256]{2,1,0:T(8,128)(2,1)S(1)}, u32[]{:S(2)}, u32[]{:S(2)}) collective-permute-start(bf16[17,80,256]{2,1,0:T(8,128)(2,1)} %get-tuple-element.58.own), channel_id=1, source_target_pairs={{0,1},{1,0},{2,3},{3,2},{4,5},{5,4},{6,7},{7,6},{8,9},{9,8},{10,11... | collective-permute-start | bytes 2088968 | tf_op jit(solution)/shard_map/ppermute | solution.py:757
  11.1 24.2 %collective-permute-start.4 = (bf16[2064,128]{1,0:T(8,128)(2,1)}, bf16[2064,128]{1,0:T(8,128)(2,1)S(1)}, u32[]{:S(2)}, u32[]{:S(2)}) collective-permute-start(bf16[2064,128]{1,0:T(8,128)(2,1)} %get-tuple-element.63.refs_3_.refs_4_), channel_id=1, source_target_pairs={{0,8},{1,9},{2,10},{3,11},{4,12},{5,13},{6,14},{7,15},{8,0},{9,1},... | collective-permute-start | bytes 1585160 | tf_op jit(solution)/shard_map/ppermute | solution.py:757
  13.7 27.0 %collective-permute-start.3 = (bf16[2064,128]{1,0:T(8,128)(2,1)}, bf16[2064,128]{1,0:T(8,128)(2,1)S(1)}, u32[]{:S(2)}, u32[]{:S(2)}) collective-permute-start(bf16[2064,128]{1,0:T(8,128)(2,1)} %get-tuple-element.63.refs_3_.refs_4_), channel_id=1, source_target_pairs={{0,2},{1,3},{2,0},{3,1},{4,6},{5,7},{6,4},{7,5},{8,10},{9,11},{10,... | collective-permute-start | bytes 1585160 | tf_op jit(solution)/shard_map/ppermute | solution.py:757
  15.2 25.5 %collective-permute-start.5 = (bf16[16,80,256]{2,1,0:T(8,128)(2,1)}, bf16[16,80,256]{2,1,0:T(8,128)(2,1)S(1)}, u32[]{:S(2)}, u32[]{:S(2)}) collective-permute-start(bf16[16,80,256]{2,1,0:T(8,128)(2,1)} %get-tuple-element.67.refs_6_.refs_8_), channel_id=1, source_target_pairs={{0,4},{1,5},{2,6},{3,7},{4,0},{5,1},{6,2},{7,3},{8,12},{9,13},{10,... | collective-permute-start | bytes 1966088 | tf_op jit(solution)/shard_map/ppermute | solution.py:757
  16.7 34.8 %collective-permute-start.11 = (bf16[16,80,256]{2,1,0:T(8,128)(2,1)}, bf16[16,80,256]{2,1,0:T(8,128)(2,1)}, u32[]{:S(2)}, u32[]{:S(2)}) collective-permute-start(bf16[16,80,256]{2,1,0:T(8,128)(2,1)} %get-tuple-element.67.refs_6_.refs_8_), channel_id=1, source_target_pairs={{0,16},{1,17},{2,18},{3,19},{4,20},{5,21},{6,22},{7,23},{8,24},{9,... | collective-permute-start | bytes 1966088 | tf_op jit(solution)/shard_map/ppermute | solution.py:757
  26.7 15.7 %copy-start.2 = (bf16[16,80,256]{2,1,0:T(8,128)(2,1)S(1)}, bf16[16,80,256]{2,1,0:T(8,128)(2,1)}, u32[]{:S(2)}) copy-start(bf16[16,80,256]{2,1,0:T(8,128)(2,1)} %get-tuple-element.67.refs_6_.refs_8_) | copy-start | bytes 1966084
  26.7 15.7 %copy-start.3 = (bf16[2064,128]{1,0:T(8,128)(2,1)S(1)}, bf16[2064,128]{1,0:T(8,128)(2,1)}, u32[]{:S(2)}) copy-start(bf16[2064,128]{1,0:T(8,128)(2,1)} %get-tuple-element.63.refs_3_.refs_4_) | copy-start | bytes 1585156
  26.7 15.7 %copy-start.11 = (s32[2,128]{1,0:T(2,128)S(1)}, s32[2,128]{1,0:T(2,128)}, u32[]{:S(2)}) copy-start(s32[2,128]{1,0:T(2,128)} %get-tuple-element.66.refs_2_) | copy-start | bytes 3076
  26.7 11.2 %collective-permute-start.1 = (bf16[80,128]{1,0:T(8,128)(2,1)S(1)}, bf16[80,128]{1,0:T(8,128)(2,1)S(1)}, u32[]{:S(2)}, u32[]{:S(2)}) collective-permute-start(bf16[80,128]{1,0:T(8,128)(2,1)S(1)} %climb0.1.own), channel_id=1, source_target_pairs={{0,2},{1,3},{2,0},{3,1},{4,6},{5,7},{6,4},{7,5},{8,10},{9,11},{10,... | collective-permute-start | bytes 61448 | tf_op jit(solution)/shard_map/ppermute | solution.py:757
  35.3 19.0 %collective-permute-start.9 = (bf16[2064,128]{1,0:T(8,128)(2,1)S(1)}, bf16[2064,128]{1,0:T(8,128)(2,1)S(1)}, u32[]{:S(2)}, u32[]{:S(2)}) collective-permute-start(bf16[2064,128]{1,0:T(8,128)(2,1)S(1)} %collective-permute-done.4.refs_5_.refs_6_), channel_id=1, source_target_pairs={{0,2},{1,3},{2,0},{3,1},{4,6},{5,7},{6,4},{7,5},{8,10},{9,11},{10,... | collective-permute-start | bytes 1585160 | tf_op jit(solution)/shard_map/ppermute | solution.py:757
  38.1 16.7 %copy-start.10 = (s32[2,128]{1,0:T(2,128)S(1)}, s32[2,128]{1,0:T(2,128)}, u32[]{:S(2)}) copy-start(s32[2,128]{1,0:T(2,128)} %get-tuple-element.77.refs_1_) | copy-start | bytes 3076
  38.1 13.0 %collective-permute-start.2 = (bf16[80,128]{1,0:T(8,128)(2,1)S(1)}, bf16[80,128]{1,0:T(8,128)(2,1)S(1)}, u32[]{:S(2)}, u32[]{:S(2)}) collective-permute-start(bf16[80,128]{1,0:T(8,128)(2,1)S(1)} %climb1.1.own), channel_id=1, source_target_pairs={{0,4},{1,5},{2,6},{3,7},{4,0},{5,1},{6,2},{7,3},{8,12},{9,13},{10,... | collective-permute-start | bytes 61448 | tf_op jit(solution)/shard_map/ppermute | solution.py:757
  40.7 10.5 %collective-permute-start.6 = (bf16[80,128]{1,0:T(8,128)(2,1)S(1)}, bf16[80,128]{1,0:T(8,128)(2,1)S(1)}, u32[]{:S(2)}, u32[]{:S(2)}) collective-permute-start(bf16[80,128]{1,0:T(8,128)(2,1)S(1)} %climb1.1.own), channel_id=1, source_target_pairs={{0,8},{1,9},{2,10},{3,11},{4,12},{5,13},{6,14},{7,15},{8,0},{9,1},... | collective-permute-start | bytes 61448 | tf_op jit(solution)/shard_map/ppermute | solution.py:757
  40.7 10.4 %collective-permute-start.7 = (bf16[80,128]{1,0:T(8,128)(2,1)S(1)}, bf16[80,128]{1,0:T(8,128)(2,1)S(1)}, u32[]{:S(2)}, u32[]{:S(2)}) collective-permute-start(bf16[80,128]{1,0:T(8,128)(2,1)S(1)} %climb1.1.own), channel_id=1, source_target_pairs={{0,12},{1,13},{2,14},{3,15},{4,8},{5,9},{6,10},{7,11},{8,4},{9,5},... | collective-permute-start | bytes 61448 | tf_op jit(solution)/shard_map/ppermute | solution.py:757
  51.5 2.9 %collective-permute-start.10 = (bf16[16,80,256]{2,1,0:T(8,128)(2,1)S(1)}, bf16[16,80,256]{2,1,0:T(8,128)(2,1)S(1)}, u32[]{:S(2)}, u32[]{:S(2)}) collective-permute-start(bf16[16,80,256]{2,1,0:T(8,128)(2,1)S(1)} %collective-permute-done.5.refs_8_.refs_10_), channel_id=1, source_target_pairs={{0,1},{1,0},{2,3},{3,2},{4,5},{5,4},{6,7},{7,6},{8,9},{9,8},{10,11... | collective-permute-start | bytes 1966088 | tf_op jit(solution)/shard_map/ppermute | solution.py:757
  51.5 3.2 %collective-permute-start.12 = (bf16[16,80,256]{2,1,0:T(8,128)(2,1)}, bf16[16,80,256]{2,1,0:T(8,128)(2,1)S(1)}, u32[]{:S(2)}, u32[]{:S(2)}) collective-permute-start(bf16[16,80,256]{2,1,0:T(8,128)(2,1)} %collective-permute-done.11.refs_12_), channel_id=1, source_target_pairs={{0,1},{1,0},{2,3},{3,2},{4,5},{5,4},{6,7},{7,6},{8,9},{9,8},{10,11... | collective-permute-start | bytes 1966088 | tf_op jit(solution)/shard_map/ppermute | solution.py:757
  52.0 17.5 %collective-permute-start.13 = (bf16[16,80,256]{2,1,0:T(8,128)(2,1)}, bf16[16,80,256]{2,1,0:T(8,128)(2,1)S(1)}, u32[]{:S(2)}, u32[]{:S(2)}) collective-permute-start(bf16[16,80,256]{2,1,0:T(8,128)(2,1)} %collective-permute-done.11.refs_12_), channel_id=1, source_target_pairs={{0,4},{1,5},{2,6},{3,7},{4,0},{5,1},{6,2},{7,3},{8,12},{9,13},{10,... | collective-permute-start | bytes 1966088 | tf_op jit(solution)/shard_map/ppermute | solution.py:757
  54.8 16.8 %copy-start.9 = (s32[2,128]{1,0:T(2,128)S(1)}, s32[2,128]{1,0:T(2,128)}, u32[]{:S(2)}) copy-start(s32[2,128]{1,0:T(2,128)} %get-tuple-element.72.refs_0_) | copy-start | bytes 3076
  69.5 2.1 %collective-permute-start.14 = (bf16[16,80,256]{2,1,0:T(8,128)(2,1)S(1)}, bf16[16,80,256]{2,1,0:T(8,128)(2,1)S(1)}, u32[]{:S(2)}, u32[]{:S(2)}) collective-permute-start(bf16[16,80,256]{2,1,0:T(8,128)(2,1)S(1)} %collective-permute-done.13.refs_5_), channel_id=1, source_target_pairs={{0,1},{1,0},{2,3},{3,2},{4,5},{5,4},{6,7},{7,6},{8,9},{9,8},{10,11... | collective-permute-start | bytes 1966088 | tf_op jit(solution)/shard_map/ppermute | solution.py:757
  69.5 7.4 %collective-permute-start.8 = (bf16[80,128]{1,0:T(8,128)(2,1)S(1)}, bf16[80,128]{1,0:T(8,128)(2,1)S(1)}, u32[]{:S(2)}, u32[]{:S(2)}) collective-permute-start(bf16[80,128]{1,0:T(8,128)(2,1)S(1)} %get-tuple-element.71), channel_id=1, source_target_pairs={{0,16},{1,17},{2,18},{3,19},{4,20},{5,21},{6,22},{7,23},{8,24},{9,... | collective-permute-start | bytes 61448 | tf_op jit(solution)/shard_map/ppermute | solution.py:757
  71.6 8.8 %copy-start = (bf16[16,256,128]{2,1,0:T(8,128)(2,1)S(1)}, bf16[16,256,128]{2,1,0:T(8,128)(2,1)}, u32[]{:S(2)}) copy-start(bf16[16,256,128]{2,1,0:T(8,128)(2,1)} %get-tuple-element.88.refs_5_.refs_4_) | copy-start | bytes 3145732
  76.9 9.3 %copy-start.5 = (f32[256,128]{1,0:T(8,128)S(1)}, f32[256,128]{1,0:T(8,128)}, u32[]{:S(2)}) copy-start(f32[256,128]{1,0:T(8,128)} %self_and_far1.1.refs_1_) | copy-start | bytes 393220
  76.9 9.2 %copy-start.6 = (f32[256,128]{1,0:T(8,128)S(1)}, f32[256,128]{1,0:T(8,128)}, u32[]{:S(2)}) copy-start(f32[256,128]{1,0:T(8,128)} %get-tuple-element.56.refs_0_) | copy-start | bytes 393220
  76.9 9.2 %copy-start.8 = (f32[16,1,256]{2,1,0:T(1,128)S(1)}, f32[16,1,256]{2,1,0:T(1,128)}, u32[]{:S(2)}) copy-start(f32[16,1,256]{2,1,0:T(1,128)} %get-tuple-element.51.refs_3_) | copy-start | bytes 49156
  76.9 7.4 %collective-permute-start.15 = (bf16[2,256,128]{2,1,0:T(8,128)(2,1)S(1)}, bf16[2,256,128]{2,1,0:T(8,128)(2,1)S(1)}, u32[]{:S(2)}, u32[]{:S(2)}) collective-permute-start(bf16[2,256,128]{2,1,0:T(8,128)(2,1)S(1)} %get-tuple-element.90), channel_id=1, source_target_pairs={{0,2},{1,3},{2,0},{3,1},{4,6},{5,7},{6,4},{7,5},{8,10},{9,11},{10,... | collective-permute-start | bytes 393224 | tf_op jit(solution)/shard_map/ppermute | solution.py:757
  77.2 7.2 %collective-permute-start.16 = (bf16[2,256,128]{2,1,0:T(8,128)(2,1)S(1)}, bf16[2,256,128]{2,1,0:T(8,128)(2,1)S(1)}, u32[]{:S(2)}, u32[]{:S(2)}) collective-permute-start(bf16[2,256,128]{2,1,0:T(8,128)(2,1)S(1)} %get-tuple-element.92), channel_id=1, source_target_pairs={{0,8},{1,9},{2,10},{3,11},{4,12},{5,13},{6,14},{7,15},{8,0},{9,1},... | collective-permute-start | bytes 393224 | tf_op jit(solution)/shard_map/ppermute | solution.py:757
  78.6 7.5 %collective-permute-start.17 = (bf16[2,256,128]{2,1,0:T(8,128)(2,1)S(1)}, bf16[2,256,128]{2,1,0:T(8,128)(2,1)S(1)}, u32[]{:S(2)}, u32[]{:S(2)}) collective-permute-start(bf16[2,256,128]{2,1,0:T(8,128)(2,1)S(1)} %get-tuple-element.94), channel_id=1, source_target_pairs={{0,10},{1,11},{2,8},{3,9},{4,14},{5,15},{6,12},{7,13},{8,2},{9,3},... | collective-permute-start | bytes 393224 | tf_op jit(solution)/shard_map/ppermute | solution.py:757

commit v6 on v5

--- a/solution.py
+++ b/solution.py
@@ -812,26 +812,25 @@
     node = climb(me, after(mine, far0), pieces[1], skels, interps, 0, 0)
     siblings = [pieces[1], swap(node, 2)]
     far1, _ = far(1, [], node)
-    node = climb(me, node, after(siblings[1], far1), skels, interps, 1, 1)
-    last_targets = swap(after(far_away, far1), 2 ** TARGET_BITS[0])
     for n, b in enumerate(early_bits):
         for low in range(2**n):
             place = spread(low, early_bits[:n])
             if low:
                 pieces[place | 2**b] = swap(pieces[place], 2**b)
     wanted = [spread(k, source_bits) for k in range(2 ** (len(source_bits) - 1))]
-    targets = [tgt, beside, far_away, last_targets]
     lists = lists0
-    height, row = 2, 2
-    others = [swap(node, k * 2**height) for k in (1, 2, 3)]
+    node = climb(me, node, after(siblings[1], far1), skels, interps, 1, 1)
     sums, *tables = near(
         0,
         [lists[0][0]],
-        targets[:3],
+        [tgt, beside],
         [pieces[k] for k in wanted if k == 1 or not k & 1],
-        codes=[payload_codes(after(part, far1, node), 0) for part in (beside, far_away)],
+        codes=[payload_codes(after(beside, far1, node), 0)],
     )
-    others[0] = after(others[0], sums)
+    last_targets = swap(after(far_away, sums), 2 ** TARGET_BITS[0])
+    targets = [tgt, beside, far_away, last_targets]
+    height, row = 2, 2
+    others = [swap(node, k * 2**height) for k in (1, 2, 3)]
     while height + 1 < bits:
         if height > 2:
             others = [swap(node, k * 2**height) for k in (1, 2, 3)]
@@ -848,19 +847,19 @@
     pieces[late | 1] = swap(pieces[late], 1)
     if height < bits:
         siblings.append(swap(node, 2**height))
-    sums, last_table, all_targets = near(
+    sums, far_table, last_table, all_targets = near(
         1,
-        [lists[0][1], tables[0], tables[2]],
+        [lists[0][1], tables[0]],
         targets,
         [pieces[k] for k in wanted + [late, late | 1]],
-        codes=[payload_codes(after(last_targets, node), 1)],
+        codes=[payload_codes(after(part, node), 1) for part in targets[2:]],
         before=sums,
     )
     for k in wanted[2::2]:
         pieces[k | late | 1] = swap(after(pieces[k | late], sums), 1)
     parts = near(
         2,
-        [lists[0][2], tables[1], tables[3], last_table],
+        [lists[0][2], tables[1], far_table, last_table],
         [all_targets],
         [pieces[k | late] for k in wanted[2:]],
         before=sums,

time: 87.6 us -> 86.8 us (level); the launches traced: 87 us -> 87.3 us
  waiting for transfers between devices: 7.66 us -> 11.9 us
  Pallas kernels: 54.6 us -> 50.8 us
    ppermute x18, waiting for transfers between devices: 7.66 us -> 11.9 us  [swap(): return lax.ppermute(value, 'leaf', pairs)]
    pallas_call x3, Pallas kernels: 24.5 us -> 21.2 us  [near(): pl.pallas_call(functools.partial(near_kernel, n_sources=n_sources, n_targ...]
  transfers between devices with their start and end apart: 18 -> 18, of which waited for: 5 -> 7; matrix products, arithmetic and copies ran while one was open for 0% -> 0% of each run, Pallas kernels for 50% -> 45%
where the time goes in v6:
time: 86.8 us; the launch traced here: 87.3 us
  Pallas kernels  50.8 us (59%)
  starting transfers between devices  24.1 us (28%)
  waiting for transfers between devices  11.9 us (14%)
    ppermute x18, starting transfers between devices, swap(): return lax.ppermute(value, 'leaf', pairs)  24.1 us
    pallas_call x3, Pallas kernels, near(): pl.pallas_call(functools.partial(near_kernel, n_sources=n_sources, n_targ...  21.2 us
    pallas_call x2, Pallas kernels, self_and_far(): pl.pallas_call(functools.partial(far_kernel, first_leaf=call * n_leaves,...  13.7 us
    ppermute x18, waiting for transfers between devices, swap(): return lax.ppermute(value, 'leaf', pairs)  11.9 us
    pallas_call x1, Pallas kernels, first_part(): pl.pallas_call(first_kernel, out_shape=tuple((jax.ShapeDtypeStruct(*shape...  10.5 us
    pallas_call x1, Pallas kernels, top(): pl.pallas_call(top_kernel, out_shape=jax.ShapeDtypeStruct((rows.shape[0]...  3.88 us
  transfers between devices with their start and end apart: 18, of which 7 were waited for; matrix products, arithmetic and copies ran while one was open for 0% of the time, Pallas kernels for 45%

profile of v6, /device:TPU:0, one launch (start us, length us, event | category | flops | bytes accessed | tf_op | source)
XLA Modules:
  0.0 87.3 jit_solution(14977575907987162201)
XLA Ops:
  0.0 10.5 %order_and_subtree.1 = (bf16[16,80,256]{2,1,0:T(8,128)(2,1)}, bf16[2064,128]{1,0:T(8,128)(2,1)}, bf16[64,128,128]{2,1,0:T(8,128)(2,1)}, bf16[64,16,128]{2,1,0:T(...) custom-call(s32[4096]{0:T(1024)} %order_in.1, ...), custom_call_target="tpu_custom_call" | custom-call | flops 1 | bytes 1 | tf_op jit(solution)/shard_map/order_and_subtree/pallas_call | solution.py:341
  10.6 0.5 collective-permute-start
  11.1 2.6 %collective-permute-start.6 = (bf16[2064,128]{1,0:T(8,128)(2,1)}, bf16[2064,128]{1,0:T(8,128)(2,1)S(1)}, u32[]{:S(2)}, u32[]{:S(2)}) collective-permute-start(bf16[2064,128]{1,0:T(8,128)(2,1)} %get-tuple-element.64.refs_2_.refs_4_), channel_id=1, source_target_pairs={{0,2},{1,3},{2,0},{3,1},{4,6},{5,7},{6,4},{7,5},{8,10},{9,11},{10,... | collective-permute-start | bytes 1585160 | tf_op jit(solution)/shard_map/ppermute | solution.py:757
  13.6 1.5 %collective-permute-start.7 = (bf16[16,80,256]{2,1,0:T(8,128)(2,1)}, bf16[16,80,256]{2,1,0:T(8,128)(2,1)S(1)}, u32[]{:S(2)}, u32[]{:S(2)}) collective-permute-start(bf16[16,80,256]{2,1,0:T(8,128)(2,1)} %get-tuple-element.67.refs_4_.refs_8_), channel_id=1, source_target_pairs={{0,4},{1,5},{2,6},{3,7},{4,0},{5,1},{6,2},{7,3},{8,12},{9,13},{10,... | collective-permute-start | bytes 1966088 | tf_op jit(solution)/shard_map/ppermute | solution.py:757
  15.2 1.6 %collective-permute-start.8 = (bf16[2064,128]{1,0:T(8,128)(2,1)}, bf16[2064,128]{1,0:T(8,128)(2,1)S(1)}, u32[]{:S(2)}, u32[]{:S(2)}) collective-permute-start(bf16[2064,128]{1,0:T(8,128)(2,1)} %get-tuple-element.64.refs_2_.refs_4_), channel_id=1, source_target_pairs={{0,8},{1,9},{2,10},{3,11},{4,12},{5,13},{6,14},{7,15},{8,0},{9,1},... | collective-permute-start | bytes 1585160 | tf_op jit(solution)/shard_map/ppermute | solution.py:757
  16.7 2.6 %collective-permute-start.11 = (bf16[16,80,256]{2,1,0:T(8,128)(2,1)}, bf16[16,80,256]{2,1,0:T(8,128)(2,1)}, u32[]{:S(2)}, u32[]{:S(2)}) collective-permute-start(bf16[16,80,256]{2,1,0:T(8,128)(2,1)} %get-tuple-element.67.refs_4_.refs_8_), channel_id=1, source_target_pairs={{0,16},{1,17},{2,18},{3,19},{4,20},{5,21},{6,22},{7,23},{8,24},{9,... | collective-permute-start | bytes 1966088 | tf_op jit(solution)/shard_map/ppermute | solution.py:757
  19.3 6.7 %self_and_far0.1 = (f32[256,128]{1,0:T(8,128)}, s32[2,128]{1,0:T(2,128)}, s32[2,128]{1,0:T(2,128)}, s32[2,128]{1,0:T(2,128)}) custom-call(s32[8,16]{1,0:T(8,128)} %get-tuple-element.48.refs_0_, s32[16,16]{1,0:T(8,128)} %refs_0_, s32[16]{0:T(128)} %refs_1_.2, bf16[64,128,128]{2,1,0:T(8,128)(2,1)} %get-tuple-element.51.refs_3_.refs_2_, ...), custom_call_target="tpu_custom_call" | custom-call | flops 1 | bytes 1 | tf_op jit(solution)/shard_map/self_and_far0/pallas_call | solution.py:453
  26.3 1.3 %collective-permute-start.1 = (bf16[80,128]{1,0:T(8,128)(2,1)S(1)}, bf16[80,128]{1,0:T(8,128)(2,1)S(1)}, u32[]{:S(2)}, u32[]{:S(2)}) collective-permute-start(bf16[80,128]{1,0:T(8,128)(2,1)S(1)} %climb0.1.own), channel_id=1, source_target_pairs={{0,2},{1,3},{2,0},{3,1},{4,6},{5,7},{6,4},{7,5},{8,10},{9,11},{10,... | collective-permute-start | bytes 61448 | tf_op jit(solution)/shard_map/ppermute | solution.py:757
  27.6 7.0 %self_and_far1.1.refs_1_ = f32[256,128]{1,0:T(8,128)} custom-call(s32[16,16]{1,0:T(8,128)} %refs_0_, s32[16]{0:T(128)} %refs_1_.2, bf16[64,128,128]{2,1,0:T(8,128)(2,1)} %get-tuple-element.51.refs_3_.refs_2_, bf16[64,16,128]{2,1,0:T(8,128)(2,1)} %get-tuple-element.52.refs_4_.refs_3_, bf16[16,256,128]{2,1,0:T(8,128)(2,1)} %get-tuple-element.84.refs_5_.refs_4_), custom_call_target="tpu_custom_call" | custom-call | flops 1 | bytes 1 | tf_op jit(solution)/shard_map/self_and_far1/pallas_call | solution.py:453
  34.8 5.5 %near0.1 = (f32[4,256,128]{2,1,0:T(8,128)S(1)}, s32[2,128]{1,0:T(2,128)S(1)}, s32[2,128]{1,0:T(2,128)S(1)}) custom-call(s32[8,16]{1,0:T(8,128)S(1)} %fusion.3.refs_0_, s32[2,128]{1,0:T(2,128)S(1)} %copy-done.11, bf16[2064,128]{1,0:T(8,128)(2,1)S(1)} %copy-done.3, bf16[2064,128]{1,0:T(8,128)(2,1)S(1)} %collective-permute-done.6.refs_3_.refs_5_, ...), custom_call_target="tpu_custom_call" | custom-call | flops 1 | bytes 1 | tf_op jit(solution)/shard_map/near0/pallas_call | solution.py:608
  40.4 0.9 %collective-permute-start.9 = (bf16[2064,128]{1,0:T(8,128)(2,1)S(1)}, bf16[2064,128]{1,0:T(8,128)(2,1)S(1)}, u32[]{:S(2)}, u32[]{:S(2)}) collective-permute-start(bf16[2064,128]{1,0:T(8,128)(2,1)S(1)} %collective-permute-done.8.refs_6_), channel_id=1, source_target_pairs={{0,2},{1,3},{2,0},{3,1},{4,6},{5,7},{6,4},{7,5},{8,10},{9,11},{10,... | collective-permute-start | bytes 1585160 | tf_op jit(solution)/shard_map/ppermute | solution.py:757
  41.3 0.5 collective-permute-start.2
  41.8 2.4 %collective-permute-start.3 = (bf16[80,128]{1,0:T(8,128)(2,1)S(1)}, bf16[80,128]{1,0:T(8,128)(2,1)S(1)}, u32[]{:S(2)}, u32[]{:S(2)}) collective-permute-start(bf16[80,128]{1,0:T(8,128)(2,1)S(1)} %climb1.1.own), channel_id=1, source_target_pairs={{0,8},{1,9},{2,10},{3,11},{4,12},{5,13},{6,14},{7,15},{8,0},{9,1},... | collective-permute-start | bytes 61448 | tf_op jit(solution)/shard_map/ppermute | solution.py:757
  44.2 1.5 %collective-permute-start.4 = (bf16[80,128]{1,0:T(8,128)(2,1)S(1)}, bf16[80,128]{1,0:T(8,128)(2,1)S(1)}, u32[]{:S(2)}, u32[]{:S(2)}) collective-permute-start(bf16[80,128]{1,0:T(8,128)(2,1)S(1)} %climb1.1.own), channel_id=1, source_target_pairs={{0,12},{1,13},{2,14},{3,15},{4,8},{5,9},{6,10},{7,11},{8,4},{9,5},... | collective-permute-start | bytes 61448 | tf_op jit(solution)/shard_map/ppermute | solution.py:757
  45.7 2.9 %collective-permute-done.3.two = bf16[80,128]{1,0:T(8,128)(2,1)S(1)} collective-permute-done((bf16[80,128]{1,0:T(8,128)(2,1)S(1)}, bf16[80,128]{1,0:T(8,128)(2,1)S(1)}, u32[]{:S(2)}, u32[]{:S(2)}) %collective-permute-start.3) | collective-permute-done | bytes 20512 | tf_op jit(solution)/shard_map/ppermute | solution.py:757
  48.6 0.4 collective-permute-done.4.three
  49.0 0.3 climb2.1
  49.4 0.5 collective-permute-start.12
  49.9 2.0 %collective-permute-start.13 = (bf16[16,80,256]{2,1,0:T(8,128)(2,1)}, bf16[16,80,256]{2,1,0:T(8,128)(2,1)S(1)}, u32[]{:S(2)}, u32[]{:S(2)}) collective-permute-start(bf16[16,80,256]{2,1,0:T(8,128)(2,1)} %collective-permute-done.11.refs_12_), channel_id=1, source_target_pairs={{0,4},{1,5},{2,6},{3,7},{4,0},{5,1},{6,2},{7,3},{8,12},{9,13},{10,... | collective-permute-start | bytes 1966088 | tf_op jit(solution)/shard_map/ppermute | solution.py:757
  51.8 2.1 %collective-permute-done.9.refs_7_ = bf16[2064,128]{1,0:T(8,128)(2,1)S(1)} collective-permute-done((bf16[2064,128]{1,0:T(8,128)(2,1)S(1)}, bf16[2064,128]{1,0:T(8,128)(2,1)S(1)}, u32[]{:S(2)}, u32[]{:S(2)}) %collective-permute-start.9) | collective-permute-done | bytes 528416 | tf_op jit(solution)/shard_map/ppermute | solution.py:757
  54.0 11.2 %near1.1 = (f32[8,256,128]{2,1,0:T(8,128)S(1)}, s32[2,128]{1,0:T(2,128)S(1)}, s32[2,128]{1,0:T(2,128)S(1)}, bf16[8192,128]{1,0:T(8,128)(2,1)S(1)}) custom-call(s32[8,16]{1,0:T(8,128)S(1)} %get-tuple-element.92.refs_0_, s32[8,16]{1,0:T(8,128)S(1)} %get-tuple-element.91.refs_1_, s32[2,128]{1,0:T(2,128)S(1)} %copy-done.10, ...), custom_call_target="tpu_custom_call" | custom-call | flops 1 | bytes 1 | tf_op jit(solution)/shard_map/near1/pallas_call | solution.py:608
  65.2 1.8 %collective-permute-done.13.refs_5_ = bf16[16,80,256]{2,1,0:T(8,128)(2,1)S(1)} collective-permute-done((bf16[16,80,256]{2,1,0:T(8,128)(2,1)}, bf16[16,80,256]{2,1,0:T(8,128)(2,1)S(1)}, u32[]{:S(2)}, u32[]{:S(2)}) %collective-permute-start.13) | collective-permute-done | bytes 655392 | tf_op jit(solution)/shard_map/ppermute | solution.py:757
  67.0 0.2 collective-permute-start.5
  67.2 1.9 %collective-permute-done.14.refs_6_ = bf16[16,80,256]{2,1,0:T(8,128)(2,1)S(1)} collective-permute-done((bf16[16,80,256]{2,1,0:T(8,128)(2,1)S(1)}, bf16[16,80,256]{2,1,0:T(8,128)(2,1)S(1)}, u32[]{:S(2)}, u32[]{:S(2)}) %collective-permute-start.14) | collective-permute-done | bytes 655392 | tf_op jit(solution)/shard_map/ppermute | solution.py:757
  69.1 4.5 %near2.1 = (bf16[2,256,128]{2,1,0:T(8,128)(2,1)S(1)}, bf16[2,256,128]{2,1,0:T(8,128)(2,1)S(1)}, bf16[2,256,128]{2,1,0:T(8,128)(2,1)S(1)}, bf16[2,256,128]{2,1,0:T(8,128)(2,1)S(1)}) custom-call(s32[2,128]{1,0:T(2,128)S(1)} %copy-done.9, s32[2,128]{1,0:T(2,128)S(1)} %get-tuple-element.68.refs_1_, s32[2,128]{1,0:T(2,128)S(1)} %get-tuple-element.77.refs_2_, ...), custom_call_target="tpu_custom_call" | custom-call | flops 1 | bytes 1 | tf_op jit(solution)/shard_map/near2/pallas_call | solution.py:608
  73.7 4.5 %collective-permute-start.15 = (bf16[2,256,128]{2,1,0:T(8,128)(2,1)S(1)}, bf16[2,256,128]{2,1,0:T(8,128)(2,1)S(1)}, u32[]{:S(2)}, u32[]{:S(2)}) collective-permute-start(bf16[2,256,128]{2,1,0:T(8,128)(2,1)S(1)} %get-tuple-element.86), channel_id=1, source_target_pairs={{0,2},{1,3},{2,0},{3,1},{4,6},{5,7},{6,4},{7,5},{8,10},{9,11},{10,... | collective-permute-start | bytes 393224 | tf_op jit(solution)/shard_map/ppermute | solution.py:757
  78.1 1.4 %collective-permute-start.16 = (bf16[2,256,128]{2,1,0:T(8,128)(2,1)S(1)}, bf16[2,256,128]{2,1,0:T(8,128)(2,1)S(1)}, u32[]{:S(2)}, u32[]{:S(2)}) collective-permute-start(bf16[2,256,128]{2,1,0:T(8,128)(2,1)S(1)} %get-tuple-element.88), channel_id=1, source_target_pairs={{0,8},{1,9},{2,10},{3,11},{4,12},{5,13},{6,14},{7,15},{8,0},{9,1},... | collective-permute-start | bytes 393224 | tf_op jit(solution)/shard_map/ppermute | solution.py:757
  79.5 0.2 collective-permute-start.17
  79.7 3.9 %top.1.refs_2_ = f32[2,256,128]{2,1,0:T(8,128)S(1)} custom-call(bf16[17,80,256]{2,1,0:T(8,128)(2,1)S(1)} %collective-permute-done.other.refs_5_.refs_9_.refs_0_, bf16[80,128]{1,0:T(8,128)(2,1)S(1)} %collective-permute-done.1.other.refs_1_, bf16[80,128]{1,0:T(8,128)(2,1)S(1)} %collective-permute-done.2.one.refs_2_, ...), custom_call_target="tpu_custom_call" | custom-call | flops 1 | bytes 1 | tf_op jit(solution)/shard_map/top/pallas_call | solution.py:707
  83.6 0.9 %collective-permute-done.16.refs_6_ = bf16[2,256,128]{2,1,0:T(8,128)(2,1)S(1)} collective-permute-done((bf16[2,256,128]{2,1,0:T(8,128)(2,1)S(1)}, bf16[2,256,128]{2,1,0:T(8,128)(2,1)S(1)}, u32[]{:S(2)}, u32[]{:S(2)}) %collective-permute-start.16) | collective-permute-done | bytes 131104 | tf_op jit(solution)/shard_map/ppermute | solution.py:757
  84.5 1.9 %collective-permute-done.17.refs_7_ = bf16[2,256,128]{2,1,0:T(8,128)(2,1)S(1)} collective-permute-done((bf16[2,256,128]{2,1,0:T(8,128)(2,1)S(1)}, bf16[2,256,128]{2,1,0:T(8,128)(2,1)S(1)}, u32[]{:S(2)}, u32[]{:S(2)}) %collective-permute-start.17) | collective-permute-done | bytes 131104 | tf_op jit(solution)/shard_map/ppermute | solution.py:757
  86.4 0.9 %last_sum.1 = f32[16,4096]{1,0:T(8,128)} custom-call(f32[256,128]{1,0:T(8,128)S(1)} %copy-done.6, f32[256,128]{1,0:T(8,128)S(1)} %copy-done.5, f32[2,256,128]{2,1,0:T(8,128)S(1)} %top.1.refs_2_, f32[16,1,256]{2,1,0:T(1,128)S(1)} %copy-done.8, bf16[2,256,128]{2,1,0:T(8,128)(2,1)S(1)} %get-tuple-element.82.refs_4_, ...), custom_call_target="tpu_custom_call" | custom-call | flops 1 | bytes 1 | tf_op jit(solution)/shard_map/last_sum/pallas_call | solution.py:744
  (44 shorter events, 0.5 us)
Async XLA Ops:
  10.5 15.5 %copy-start.1 = (bf16[5,256,128]{2,1,0:T(8,128)(2,1)S(1)}, bf16[5,256,128]{2,1,0:T(8,128)(2,1)}, u32[]{:S(2)}) copy-start(bf16[5,256,128]{2,1,0:T(8,128)(2,1)} %get-tuple-element.58.interps) | copy-start | bytes 983044
  10.5 15.5 %copy-start.4 = (bf16[17,80,256]{2,1,0:T(8,128)(2,1)S(1)}, bf16[17,80,256]{2,1,0:T(8,128)(2,1)}, u32[]{:S(2)}) copy-start(bf16[17,80,256]{2,1,0:T(8,128)(2,1)} %get-tuple-element.56.own) | copy-start | bytes 2088964
  10.5 15.5 %copy-start.7 = (s32[5,1,128]{2,1,0:T(1,128)S(1)}, s32[5,1,128]{2,1,0:T(1,128)}, u32[]{:S(2)}) copy-start(s32[5,1,128]{2,1,0:T(1,128)} %get-tuple-element.57.skels) | copy-start | bytes 7684
  10.6 15.5 %collective-permute-start = (bf16[17,80,256]{2,1,0:T(8,128)(2,1)}, bf16[17,80,256]{2,1,0:T(8,128)(2,1)S(1)}, u32[]{:S(2)}, u32[]{:S(2)}) collective-permute-start(bf16[17,80,256]{2,1,0:T(8,128)(2,1)} %get-tuple-element.56.own), channel_id=1, source_target_pairs={{0,1},{1,0},{2,3},{3,2},{4,5},{5,4},{6,7},{7,6},{8,9},{9,8},{10,11... | collective-permute-start | bytes 2088968 | tf_op jit(solution)/shard_map/ppermute | solution.py:757
  11.1 23.7 %collective-permute-start.6 = (bf16[2064,128]{1,0:T(8,128)(2,1)}, bf16[2064,128]{1,0:T(8,128)(2,1)S(1)}, u32[]{:S(2)}, u32[]{:S(2)}) collective-permute-start(bf16[2064,128]{1,0:T(8,128)(2,1)} %get-tuple-element.64.refs_2_.refs_4_), channel_id=1, source_target_pairs={{0,2},{1,3},{2,0},{3,1},{4,6},{5,7},{6,4},{7,5},{8,10},{9,11},{10,... | collective-permute-start | bytes 1585160 | tf_op jit(solution)/shard_map/ppermute | solution.py:757
  13.6 21.2 %collective-permute-start.7 = (bf16[16,80,256]{2,1,0:T(8,128)(2,1)}, bf16[16,80,256]{2,1,0:T(8,128)(2,1)S(1)}, u32[]{:S(2)}, u32[]{:S(2)}) collective-permute-start(bf16[16,80,256]{2,1,0:T(8,128)(2,1)} %get-tuple-element.67.refs_4_.refs_8_), channel_id=1, source_target_pairs={{0,4},{1,5},{2,6},{3,7},{4,0},{5,1},{6,2},{7,3},{8,12},{9,13},{10,... | collective-permute-start | bytes 1966088 | tf_op jit(solution)/shard_map/ppermute | solution.py:757
  15.2 25.2 %collective-permute-start.8 = (bf16[2064,128]{1,0:T(8,128)(2,1)}, bf16[2064,128]{1,0:T(8,128)(2,1)S(1)}, u32[]{:S(2)}, u32[]{:S(2)}) collective-permute-start(bf16[2064,128]{1,0:T(8,128)(2,1)} %get-tuple-element.64.refs_2_.refs_4_), channel_id=1, source_target_pairs={{0,8},{1,9},{2,10},{3,11},{4,12},{5,13},{6,14},{7,15},{8,0},{9,1},... | collective-permute-start | bytes 1585160 | tf_op jit(solution)/shard_map/ppermute | solution.py:757
  16.7 32.6 %collective-permute-start.11 = (bf16[16,80,256]{2,1,0:T(8,128)(2,1)}, bf16[16,80,256]{2,1,0:T(8,128)(2,1)}, u32[]{:S(2)}, u32[]{:S(2)}) collective-permute-start(bf16[16,80,256]{2,1,0:T(8,128)(2,1)} %get-tuple-element.67.refs_4_.refs_8_), channel_id=1, source_target_pairs={{0,16},{1,17},{2,18},{3,19},{4,20},{5,21},{6,22},{7,23},{8,24},{9,... | collective-permute-start | bytes 1966088 | tf_op jit(solution)/shard_map/ppermute | solution.py:757
  26.2 8.6 %copy-start.2 = (bf16[16,80,256]{2,1,0:T(8,128)(2,1)S(1)}, bf16[16,80,256]{2,1,0:T(8,128)(2,1)}, u32[]{:S(2)}) copy-start(bf16[16,80,256]{2,1,0:T(8,128)(2,1)} %get-tuple-element.67.refs_4_.refs_8_) | copy-start | bytes 1966084
  26.3 8.6 %copy-start.3 = (bf16[2064,128]{1,0:T(8,128)(2,1)S(1)}, bf16[2064,128]{1,0:T(8,128)(2,1)}, u32[]{:S(2)}) copy-start(bf16[2064,128]{1,0:T(8,128)(2,1)} %get-tuple-element.64.refs_2_.refs_4_) | copy-start | bytes 1585156
  26.3 8.6 %copy-start.11 = (s32[2,128]{1,0:T(2,128)S(1)}, s32[2,128]{1,0:T(2,128)}, u32[]{:S(2)}) copy-start(s32[2,128]{1,0:T(2,128)} %get-tuple-element.66.refs_1_) | copy-start | bytes 3076
  26.3 8.3 %collective-permute-start.1 = (bf16[80,128]{1,0:T(8,128)(2,1)S(1)}, bf16[80,128]{1,0:T(8,128)(2,1)S(1)}, u32[]{:S(2)}, u32[]{:S(2)}) collective-permute-start(bf16[80,128]{1,0:T(8,128)(2,1)S(1)} %climb0.1.own), channel_id=1, source_target_pairs={{0,2},{1,3},{2,0},{3,1},{4,6},{5,7},{6,4},{7,5},{8,10},{9,11},{10,... | collective-permute-start | bytes 61448 | tf_op jit(solution)/shard_map/ppermute | solution.py:757
  34.6 19.4 %copy-start.10 = (s32[2,128]{1,0:T(2,128)S(1)}, s32[2,128]{1,0:T(2,128)}, u32[]{:S(2)}) copy-start(s32[2,128]{1,0:T(2,128)} %get-tuple-element.73.refs_2_) | copy-start | bytes 3076
  40.4 13.5 %collective-permute-start.9 = (bf16[2064,128]{1,0:T(8,128)(2,1)S(1)}, bf16[2064,128]{1,0:T(8,128)(2,1)S(1)}, u32[]{:S(2)}, u32[]{:S(2)}) collective-permute-start(bf16[2064,128]{1,0:T(8,128)(2,1)S(1)} %collective-permute-done.8.refs_6_), channel_id=1, source_target_pairs={{0,2},{1,3},{2,0},{3,1},{4,6},{5,7},{6,4},{7,5},{8,10},{9,11},{10,... | collective-permute-start | bytes 1585160 | tf_op jit(solution)/shard_map/ppermute | solution.py:757
  41.3 4.4 %collective-permute-start.2 = (bf16[80,128]{1,0:T(8,128)(2,1)S(1)}, bf16[80,128]{1,0:T(8,128)(2,1)S(1)}, u32[]{:S(2)}, u32[]{:S(2)}) collective-permute-start(bf16[80,128]{1,0:T(8,128)(2,1)S(1)} %climb1.1.own), channel_id=1, source_target_pairs={{0,4},{1,5},{2,6},{3,7},{4,0},{5,1},{6,2},{7,3},{8,12},{9,13},{10,... | collective-permute-start | bytes 61448 | tf_op jit(solution)/shard_map/ppermute | solution.py:757
  41.8 6.8 %collective-permute-start.3 = (bf16[80,128]{1,0:T(8,128)(2,1)S(1)}, bf16[80,128]{1,0:T(8,128)(2,1)S(1)}, u32[]{:S(2)}, u32[]{:S(2)}) collective-permute-start(bf16[80,128]{1,0:T(8,128)(2,1)S(1)} %climb1.1.own), channel_id=1, source_target_pairs={{0,8},{1,9},{2,10},{3,11},{4,12},{5,13},{6,14},{7,15},{8,0},{9,1},... | collective-permute-start | bytes 61448 | tf_op jit(solution)/shard_map/ppermute | solution.py:757
  44.2 4.8 %collective-permute-start.4 = (bf16[80,128]{1,0:T(8,128)(2,1)S(1)}, bf16[80,128]{1,0:T(8,128)(2,1)S(1)}, u32[]{:S(2)}, u32[]{:S(2)}) collective-permute-start(bf16[80,128]{1,0:T(8,128)(2,1)S(1)} %climb1.1.own), channel_id=1, source_target_pairs={{0,12},{1,13},{2,14},{3,15},{4,8},{5,9},{6,10},{7,11},{8,4},{9,5},... | collective-permute-start | bytes 61448 | tf_op jit(solution)/shard_map/ppermute | solution.py:757
  49.3 4.7 %collective-permute-start.10 = (bf16[16,80,256]{2,1,0:T(8,128)(2,1)S(1)}, bf16[16,80,256]{2,1,0:T(8,128)(2,1)S(1)}, u32[]{:S(2)}, u32[]{:S(2)}) collective-permute-start(bf16[16,80,256]{2,1,0:T(8,128)(2,1)S(1)} %collective-permute-done.7.refs_6_.refs_10_), channel_id=1, source_target_pairs={{0,1},{1,0},{2,3},{3,2},{4,5},{5,4},{6,7},{7,6},{8,9},{9,8},{10,11... | collective-permute-start | bytes 1966088 | tf_op jit(solution)/shard_map/ppermute | solution.py:757
  49.4 4.6 %collective-permute-start.12 = (bf16[16,80,256]{2,1,0:T(8,128)(2,1)}, bf16[16,80,256]{2,1,0:T(8,128)(2,1)S(1)}, u32[]{:S(2)}, u32[]{:S(2)}) collective-permute-start(bf16[16,80,256]{2,1,0:T(8,128)(2,1)} %collective-permute-done.11.refs_12_), channel_id=1, source_target_pairs={{0,1},{1,0},{2,3},{3,2},{4,5},{5,4},{6,7},{7,6},{8,9},{9,8},{10,11... | collective-permute-start | bytes 1966088 | tf_op jit(solution)/shard_map/ppermute | solution.py:757
  49.9 17.1 %collective-permute-start.13 = (bf16[16,80,256]{2,1,0:T(8,128)(2,1)}, bf16[16,80,256]{2,1,0:T(8,128)(2,1)S(1)}, u32[]{:S(2)}, u32[]{:S(2)}) collective-permute-start(bf16[16,80,256]{2,1,0:T(8,128)(2,1)} %collective-permute-done.11.refs_12_), channel_id=1, source_target_pairs={{0,4},{1,5},{2,6},{3,7},{4,0},{5,1},{6,2},{7,3},{8,12},{9,13},{10,... | collective-permute-start | bytes 1966088 | tf_op jit(solution)/shard_map/ppermute | solution.py:757
  54.0 15.1 %copy-start.9 = (s32[2,128]{1,0:T(2,128)S(1)}, s32[2,128]{1,0:T(2,128)}, u32[]{:S(2)}) copy-start(s32[2,128]{1,0:T(2,128)} %get-tuple-element.63.refs_0_) | copy-start | bytes 3076
  67.0 2.1 %collective-permute-start.14 = (bf16[16,80,256]{2,1,0:T(8,128)(2,1)S(1)}, bf16[16,80,256]{2,1,0:T(8,128)(2,1)S(1)}, u32[]{:S(2)}, u32[]{:S(2)}) collective-permute-start(bf16[16,80,256]{2,1,0:T(8,128)(2,1)S(1)} %collective-permute-done.13.refs_5_), channel_id=1, source_target_pairs={{0,1},{1,0},{2,3},{3,2},{4,5},{5,4},{6,7},{7,6},{8,9},{9,8},{10,11... | collective-permute-start | bytes 1966088 | tf_op jit(solution)/shard_map/ppermute | solution.py:757
  67.0 6.6 %collective-permute-start.5 = (bf16[80,128]{1,0:T(8,128)(2,1)S(1)}, bf16[80,128]{1,0:T(8,128)(2,1)S(1)}, u32[]{:S(2)}, u32[]{:S(2)}) collective-permute-start(bf16[80,128]{1,0:T(8,128)(2,1)S(1)} %get-tuple-element.62), channel_id=1, source_target_pairs={{0,16},{1,17},{2,18},{3,19},{4,20},{5,21},{6,22},{7,23},{8,24},{9,... | collective-permute-start | bytes 61448 | tf_op jit(solution)/shard_map/ppermute | solution.py:757
  69.1 10.6 %copy-start = (bf16[16,256,128]{2,1,0:T(8,128)(2,1)S(1)}, bf16[16,256,128]{2,1,0:T(8,128)(2,1)}, u32[]{:S(2)}) copy-start(bf16[16,256,128]{2,1,0:T(8,128)(2,1)} %get-tuple-element.84.refs_5_.refs_4_) | copy-start | bytes 3145732
  73.6 12.7 %copy-start.5 = (f32[256,128]{1,0:T(8,128)S(1)}, f32[256,128]{1,0:T(8,128)}, u32[]{:S(2)}) copy-start(f32[256,128]{1,0:T(8,128)} %self_and_far1.1.refs_1_) | copy-start | bytes 393220
  73.6 12.7 %copy-start.6 = (f32[256,128]{1,0:T(8,128)S(1)}, f32[256,128]{1,0:T(8,128)}, u32[]{:S(2)}) copy-start(f32[256,128]{1,0:T(8,128)} %get-tuple-element.54.refs_0_) | copy-start | bytes 393220
  73.6 12.7 %copy-start.8 = (f32[16,1,256]{2,1,0:T(1,128)S(1)}, f32[16,1,256]{2,1,0:T(1,128)}, u32[]{:S(2)}) copy-start(f32[16,1,256]{2,1,0:T(1,128)} %get-tuple-element.49.refs_3_) | copy-start | bytes 49156
  73.7 9.9 %collective-permute-start.15 = (bf16[2,256,128]{2,1,0:T(8,128)(2,1)S(1)}, bf16[2,256,128]{2,1,0:T(8,128)(2,1)S(1)}, u32[]{:S(2)}, u32[]{:S(2)}) collective-permute-start(bf16[2,256,128]{2,1,0:T(8,128)(2,1)S(1)} %get-tuple-element.86), channel_id=1, source_target_pairs={{0,2},{1,3},{2,0},{3,1},{4,6},{5,7},{6,4},{7,5},{8,10},{9,11},{10,... | collective-permute-start | bytes 393224 | tf_op jit(solution)/shard_map/ppermute | solution.py:757
  78.1 6.3 %collective-permute-start.16 = (bf16[2,256,128]{2,1,0:T(8,128)(2,1)S(1)}, bf16[2,256,128]{2,1,0:T(8,128)(2,1)S(1)}, u32[]{:S(2)}, u32[]{:S(2)}) collective-permute-start(bf16[2,256,128]{2,1,0:T(8,128)(2,1)S(1)} %get-tuple-element.88), channel_id=1, source_target_pairs={{0,8},{1,9},{2,10},{3,11},{4,12},{5,13},{6,14},{7,15},{8,0},{9,1},... | collective-permute-start | bytes 393224 | tf_op jit(solution)/shard_map/ppermute | solution.py:757
  79.5 6.8 %collective-permute-start.17 = (bf16[2,256,128]{2,1,0:T(8,128)(2,1)S(1)}, bf16[2,256,128]{2,1,0:T(8,128)(2,1)S(1)}, u32[]{:S(2)}, u32[]{:S(2)}) collective-permute-start(bf16[2,256,128]{2,1,0:T(8,128)(2,1)S(1)} %get-tuple-element.90), channel_id=1, source_target_pairs={{0,10},{1,11},{2,8},{3,9},{4,14},{5,15},{6,12},{7,13},{8,2},{9,3},... | collective-permute-start | bytes 393224 | tf_op jit(solution)/shard_map/ppermute | solution.py:757

commit v7 on v6

--- a/solution.py
+++ b/solution.py
@@ -14,7 +14,7 @@
 CODE = (1 << PHASE_BIT) - 1
 VMEM_LIMIT = 24 * 1024 * 1024
 FIRST_LIMIT = 58 * 1024 * 1024
-PHASES = 3
+PHASES = 4
 bf16 = jnp.bfloat16
 f32 = jnp.float32
 
@@ -134,7 +134,7 @@
     is_first = jnp.logical_not(is_late) & ((piece < 2) | ((piece & 1) == 0))
     if first != 0:
         is_first = is_first & (piece < 0)
-    phase = jnp.where(is_last, 2, jnp.where(is_first, 0, 1))
+    phase = jnp.where(is_last, PHASES - 1, jnp.where(is_first, 0, max(first, 1)))
     first_place = place - (piece - jnp.where(piece < 2, piece, (piece >> 1) + 1)) * leaves
     place = jnp.where(
         is_last,
@@ -471,7 +471,7 @@
     return out[0], [out[1 + PHASES * k : 1 + PHASES * k + PHASES] for k in range(len(codes))]
 
 
-def near_kernel(*refs, n_sources, n_targets, n_lists, n_codes, phase):
+def near_kernel(*refs, n_sources, n_targets, n_lists, n_codes, n_before, phase):
     refs = list(refs)
 
     def take(n):
@@ -482,20 +482,13 @@
     makes = phase < PHASES - 1
     codes = take(n_codes)
     lists = take(n_lists)
-    target_parts = take(n_targets if makes else 1)
+    target_parts = take(n_targets)
     source_parts = take(n_sources)
-    before = take(phase > 0)
+    before = take(n_before)
     outs = take(n_targets) if not makes else []
     (acc,) = take(1) if makes else (None,)
     tables = [take(PHASES - 1 - phase) for _ in range(n_codes)]
-    if phase == 1:
-        (targets,) = take(1)
-    elif phase == 2:
-        (targets,) = target_parts
-        target_parts = []
-    sources, sems, pairs, steps = take(4)
-    if phase == 0:
-        (targets,) = take(1)
+    sources, sems, pairs, steps, targets = take(5)
     if not makes:
         (acc,) = take(1)
     leaves = source_parts[0].shape[0]
@@ -567,32 +560,27 @@
     if makes:
         for part in before:
             acc[: part.shape[0]] += part[...]
+    earlier = [(part, at) for part in before for at in range(0, part.shape[0], own_rows)]
     for k, out in enumerate(outs):
         mine = slice(k * own_rows, (k + 1) * own_rows)
-        out[...] = (acc[mine] + before[0][mine]).astype(bf16)
-
-
-def near(phase, lists, targets, sources, codes=(), before=None):
-    n_sources, n_codes = len(sources), len(codes)
+        part, at = earlier[k]
+        out[...] = (acc[mine] + part[at : at + own_rows]).astype(bf16)
+
+
+def near(phase, lists, targets, sources, codes=(), before=()):
+    n_sources, n_codes, n_targets = len(sources), len(codes), len(targets)
     makes = phase < PHASES - 1
-    n_targets = len(targets) if makes else len(lists)
     leaves = min(source.shape[0] for source in sources)
     sums = jax.ShapeDtypeStruct((n_targets * leaves // 8, 256, 128), f32)
     part = jax.ShapeDtypeStruct((leaves // 8, 256, 128), bf16)
-    held_targets = jax.ShapeDtypeStruct((n_targets * leaves * 128, 128), bf16)
     args = list(codes) + list(lists) + list(targets) + list(sources)
     in_specs = [SMEM] * n_codes + [ANY] * (len(args) - n_codes)
-    if not makes:
-        in_specs[len(lists)] = VMEM
-    if before is not None:
-        args.append(before)
-        in_specs.append(VMEM)
+    args += list(before)
+    in_specs += [VMEM] * len(before)
     if makes:
         n_tables = n_codes * (PHASES - 1 - phase)
         out_shape = (sums,) + (pair_table(leaves),) * n_tables
         out_specs = (VMEM,) + (SMEM,) * n_tables
-        if phase == 1:
-            out_shape, out_specs = out_shape + (held_targets,), out_specs + (VMEM,)
     else:
         out_shape, out_specs = (part,) * n_targets, (VMEM,) * n_targets
     scratch = [
@@ -600,9 +588,8 @@
         pltpu.SemaphoreType.DMA((n_sources + n_targets + len(lists),)),
         pltpu.SMEM((n_targets * leaves // 8, 128), jnp.int32),
         pltpu.SMEM((len(STEPS), n_targets * leaves), jnp.int32),
+        pltpu.VMEM((n_targets * leaves * 128, 128), bf16),
     ]
-    if phase == 0:
-        scratch.append(pltpu.VMEM(held_targets.shape, bf16))
     if not makes:
         scratch.append(pltpu.VMEM(sums.shape, f32))
     return pl.pallas_call(
@@ -612,6 +599,7 @@
             n_targets=n_targets,
             n_lists=len(lists),
             n_codes=n_codes,
+            n_before=len(before),
             phase=phase,
         ),
         out_shape=out_shape,
@@ -828,41 +816,46 @@
         codes=[payload_codes(after(beside, far1, node), 0)],
     )
     last_targets = swap(after(far_away, sums), 2 ** TARGET_BITS[0])
-    targets = [tgt, beside, far_away, last_targets]
+    for k in wanted[2::2]:
+        pieces[k | 1] = swap(after(pieces[k], sums), 1)
+    pieces[late] = after(pieces[late], sums)
+    for n, b in enumerate(early_bits):
+        for low in range(2**n):
+            place = spread(low, early_bits[:n]) | late
+            pieces[place | 2**b] = swap(pieces[place], 2**b)
+    pieces[late | 1] = swap(pieces[late], 1)
+    present = [pieces[k] for k in wanted + [late, late | 1]]
+    sums, *far_tables = near(
+        1,
+        [lists[0][1], tables[0]],
+        [tgt, beside, far_away],
+        present,
+        codes=[payload_codes(after(far_away, node, sums), 1)],
+        before=[sums],
+    )
     height, row = 2, 2
+    node = after(node, sums)
     others = [swap(node, k * 2**height) for k in (1, 2, 3)]
+    last_sums, last_table = near(
+        2, [], [last_targets], present, codes=[payload_codes(after(last_targets, sums), 2)]
+    )
+    others[0] = after(others[0], last_sums)
     while height + 1 < bits:
         if height > 2:
             others = [swap(node, k * 2**height) for k in (1, 2, 3)]
         sibling, node = climb_two(me, node, others, skels, interps, height, row)
         siblings += [others[0], sibling]
         height, row = height + 2, row + 3
-    for k in wanted[2::2]:
-        pieces[k | 1] = swap(after(pieces[k], node), 1)
-    pieces[late] = after(pieces[late], node)
-    for n, b in enumerate(early_bits):
-        for low in range(2**n):
-            place = spread(low, early_bits[:n]) | late
-            pieces[place | 2**b] = swap(pieces[place], 2**b)
-    pieces[late | 1] = swap(pieces[late], 1)
     if height < bits:
         siblings.append(swap(node, 2**height))
-    sums, far_table, last_table, all_targets = near(
-        1,
-        [lists[0][1], tables[0]],
-        targets,
-        [pieces[k] for k in wanted + [late, late | 1]],
-        codes=[payload_codes(after(part, node), 1) for part in targets[2:]],
-        before=sums,
-    )
     for k in wanted[2::2]:
-        pieces[k | late | 1] = swap(after(pieces[k | late], sums), 1)
+        pieces[k | late | 1] = swap(after(pieces[k | late], node), 1)
     parts = near(
-        2,
-        [lists[0][2], tables[1], far_table, last_table],
-        [all_targets],
+        3,
+        [lists[0][3], tables[2], far_tables[1], last_table],
+        [tgt, beside, far_away, last_targets],
         [pieces[k | late] for k in wanted[2:]],
-        before=sums,
+        before=[sums, last_sums],
     )
     siblings[-1] = after(siblings[-1], parts[0])
     received = [parts[0]] + [

time: 86.8 us -> 89 us (1.025); the launches traced: 87.3 us -> 88.4 us
  Pallas kernels: 50.8 us -> 58.5 us
  waiting for transfers between devices: 11.9 us -> 7.09 us
  starting transfers between devices: 24.1 us -> 21.2 us
  local copies, waits for them, and re-layouts: 0.05 us -> 1.14 us
    pallas_call x3 -> x4, Pallas kernels: 21.2 us -> 29.3 us  [near(): pl.pallas_call(functools.partial(near_kernel, n_sources=n_sources, n_targ...]
    ppermute x18, waiting for transfers between devices: 11.9 us -> 7.09 us  [swap(): return lax.ppermute(value, 'leaf', pairs)]
    ppermute x18, starting transfers between devices: 24.1 us -> 21.2 us  [swap(): return lax.ppermute(value, 'leaf', pairs)]
    unnamed x24, local copies, waits for them, and re-layouts: 0.05 us -> 1.14 us
  transfers between devices with their start and end apart: 18 -> 18, of which waited for: 7 -> 3; matrix products, arithmetic and copies ran while one was open for 0% -> 0% of each run, Pallas kernels for 45% -> 53%
where the time goes in v7:
time: 89 us; the launch traced here: 88.4 us
  Pallas kernels  58.5 us (66%)
  starting transfers between devices  21.2 us (24%)
  waiting for transfers between devices  7.09 us (8%)
  local copies, waits for them, and re-layouts  1.14 us (1%)
    pallas_call x4, Pallas kernels, near(): pl.pallas_call(functools.partial(near_kernel, n_sources=n_sources, n_targ...  29.3 us
    ppermute x18, starting transfers between devices, swap(): return lax.ppermute(value, 'leaf', pairs)  21.2 us
    pallas_call x2, Pallas kernels, self_and_far(): pl.pallas_call(functools.partial(far_kernel, first_leaf=call * n_leaves,...  13.3 us
    pallas_call x1, Pallas kernels, first_part(): pl.pallas_call(first_kernel, out_shape=tuple((jax.ShapeDtypeStruct(*shape...  10.5 us
    ppermute x18, waiting for transfers between devices, swap(): return lax.ppermute(value, 'leaf', pairs)  7.09 us
    pallas_call x1, Pallas kernels, top(): pl.pallas_call(top_kernel, out_shape=jax.ShapeDtypeStruct((rows.shape[0]...  3.88 us
  transfers between devices with their start and end apart: 18, of which 3 were waited for; matrix products, arithmetic and copies ran while one was open for 0% of the time, Pallas kernels for 53%

profile of v7, /device:TPU:0, one launch (start us, length us, event | category | flops | bytes accessed | tf_op | source)
XLA Modules:
  0.0 88.4 jit_solution(3688719038360428921)
XLA Ops:
  0.0 10.5 %order_and_subtree.1 = (bf16[16,80,256]{2,1,0:T(8,128)(2,1)}, bf16[2064,128]{1,0:T(8,128)(2,1)}, bf16[64,128,128]{2,1,0:T(8,128)(2,1)}, bf16[64,16,128]{2,1,0:T(...) custom-call(s32[4096]{0:T(1024)} %order_in.1, ...), custom_call_target="tpu_custom_call" | custom-call | flops 1 | bytes 1 | tf_op jit(solution)/shard_map/order_and_subtree/pallas_call | solution.py:341
  10.5 0.5 collective-permute-start
  11.1 2.6 %collective-permute-start.3 = (bf16[2064,128]{1,0:T(8,128)(2,1)}, bf16[2064,128]{1,0:T(8,128)(2,1)S(1)}, u32[]{:S(2)}, u32[]{:S(2)}) collective-permute-start(bf16[2064,128]{1,0:T(8,128)(2,1)} %get-tuple-element.63.refs_2_.refs_3_.refs_4_), channel_id=1, source_target_pairs={{0,2},{1,3},{2,0},{3,1},{4,6},{5,7},{6,4},{7,5},{8,10},{9,11},{10,... | collective-permute-start | bytes 1585160 | tf_op jit(solution)/shard_map/ppermute | solution.py:745
  13.6 1.5 %collective-permute-start.4 = (bf16[16,80,256]{2,1,0:T(8,128)(2,1)}, bf16[16,80,256]{2,1,0:T(8,128)(2,1)S(1)}, u32[]{:S(2)}, u32[]{:S(2)}) collective-permute-start(bf16[16,80,256]{2,1,0:T(8,128)(2,1)} %get-tuple-element.66.refs_4_.refs_6_.refs_2_), channel_id=1, source_target_pairs={{0,4},{1,5},{2,6},{3,7},{4,0},{5,1},{6,2},{7,3},{8,12},{9,13},{10,... | collective-permute-start | bytes 1966088 | tf_op jit(solution)/shard_map/ppermute | solution.py:745
  15.1 2.6 %collective-permute-start.6 = (bf16[16,80,256]{2,1,0:T(8,128)(2,1)}, bf16[16,80,256]{2,1,0:T(8,128)(2,1)S(1)}, u32[]{:S(2)}, u32[]{:S(2)}) collective-permute-start(bf16[16,80,256]{2,1,0:T(8,128)(2,1)} %get-tuple-element.66.refs_4_.refs_6_.refs_2_), channel_id=1, source_target_pairs={{0,16},{1,17},{2,18},{3,19},{4,20},{5,21},{6,22},{7,23},{8,24},{9,... | collective-permute-start | bytes 1966088 | tf_op jit(solution)/shard_map/ppermute | solution.py:745
  17.7 1.6 %collective-permute-start.2 = (bf16[2064,128]{1,0:T(8,128)(2,1)}, bf16[2064,128]{1,0:T(8,128)(2,1)S(1)}, u32[]{:S(2)}, u32[]{:S(2)}) collective-permute-start(bf16[2064,128]{1,0:T(8,128)(2,1)} %get-tuple-element.63.refs_2_.refs_3_.refs_4_), channel_id=1, source_target_pairs={{0,8},{1,9},{2,10},{3,11},{4,12},{5,13},{6,14},{7,15},{8,0},{9,1},... | collective-permute-start | bytes 1585160 | tf_op jit(solution)/shard_map/ppermute | solution.py:745
  19.3 6.7 %self_and_far0.1 = (f32[256,128]{1,0:T(8,128)}, s32[2,128]{1,0:T(2,128)}, s32[2,128]{1,0:T(2,128)}, s32[2,128]{1,0:T(2,128)}, s32[2,128]{1,0:T(2,128)}) custom-call(s32[8,16]{1,0:T(8,128)} %get-tuple-element.50.refs_0_, s32[16,16]{1,0:T(8,128)} %refs_0_, s32[16]{0:T(128)} %refs_1_.2, bf16[64,128,128]{2,1,0:T(8,128)(2,1)} %get-tuple-element.53.refs_3_.refs_2_, ...), custom_call_target="tpu_custom_call" | custom-call | flops 1 | bytes 1 | tf_op jit(solution)/shard_map/self_and_far0/pallas_call | solution.py:453
  26.1 1.1 %copy-done.4 = bf16[17,80,256]{2,1,0:T(8,128)(2,1)S(1)} copy-done((bf16[17,80,256]{2,1,0:T(8,128)(2,1)S(1)}, bf16[17,80,256]{2,1,0:T(8,128)(2,1)}, u32[]{:S(2)}) %copy-start.4) | copy-done | bytes 696344
  27.2 0.1 climb0.1.own
  27.4 1.7 %collective-permute-start.1 = (bf16[80,128]{1,0:T(8,128)(2,1)S(1)}, bf16[80,128]{1,0:T(8,128)(2,1)S(1)}, u32[]{:S(2)}, u32[]{:S(2)}) collective-permute-start(bf16[80,128]{1,0:T(8,128)(2,1)S(1)} %climb0.1.own), channel_id=1, source_target_pairs={{0,2},{1,3},{2,0},{3,1},{4,6},{5,7},{6,4},{7,5},{8,10},{9,11},{10,... | collective-permute-start | bytes 61448 | tf_op jit(solution)/shard_map/ppermute | solution.py:745
  29.1 6.6 %self_and_far1.1.refs_1_ = f32[256,128]{1,0:T(8,128)} custom-call(s32[16,16]{1,0:T(8,128)} %refs_0_, s32[16]{0:T(128)} %refs_1_.2, bf16[64,128,128]{2,1,0:T(8,128)(2,1)} %get-tuple-element.53.refs_3_.refs_2_, bf16[64,16,128]{2,1,0:T(8,128)(2,1)} %get-tuple-element.54.refs_4_.refs_3_, bf16[16,256,128]{2,1,0:T(8,128)(2,1)} %get-tuple-element.88.refs_5_.refs_4_), custom_call_target="tpu_custom_call" | custom-call | flops 1 | bytes 1 | tf_op jit(solution)/shard_map/self_and_far1/pallas_call | solution.py:453
  35.7 0.1 climb1.1.own
  36.0 6.5 %near0.1 = (f32[4,256,128]{2,1,0:T(8,128)S(1)}, s32[2,128]{1,0:T(2,128)S(1)}, s32[2,128]{1,0:T(2,128)}, s32[2,128]{1,0:T(2,128)S(1)}) custom-call(s32[8,16]{1,0:T(8,128)S(1)} %fusion.3.refs_0_, s32[2,128]{1,0:T(2,128)S(1)} %copy-done.10, bf16[2064,128]{1,0:T(8,128)(2,1)S(1)} %copy-done.2, ...), custom_call_target="tpu_custom_call" | custom-call | flops 1 | bytes 1 | tf_op jit(solution)/shard_map/near0/pallas_call | solution.py:595
  42.5 0.1 collective-permute-start.5
  42.6 4.2 %collective-permute-done.6.refs_10_.refs_6_ = bf16[16,80,256]{2,1,0:T(8,128)(2,1)S(1)} collective-permute-done((bf16[16,80,256]{2,1,0:T(8,128)(2,1)}, bf16[16,80,256]{2,1,0:T(8,128)(2,1)S(1)}, u32[]{:S(2)}, u32[]{:S(2)}) %collective-permute-start.6) | collective-permute-done | bytes 655392 | tf_op jit(solution)/shard_map/ppermute | solution.py:745
  46.8 0.5 collective-permute-start.9
  47.4 0.5 collective-permute-start.13
  47.9 1.0 %collective-permute-done.7.refs_11_.refs_7_ = bf16[16,80,256]{2,1,0:T(8,128)(2,1)S(1)} collective-permute-done((bf16[16,80,256]{2,1,0:T(8,128)(2,1)S(1)}, bf16[16,80,256]{2,1,0:T(8,128)(2,1)S(1)}, u32[]{:S(2)}, u32[]{:S(2)}) %collective-permute-start.7) | collective-permute-done | bytes 655392 | tf_op jit(solution)/shard_map/ppermute | solution.py:745
  48.9 9.9 %near1.1 = (f32[6,256,128]{2,1,0:T(8,128)S(1)}, s32[2,128]{1,0:T(2,128)}, s32[2,128]{1,0:T(2,128)S(1)}) custom-call(s32[8,16]{1,0:T(8,128)S(1)} %fusion.7.refs_0_, s32[2,128]{1,0:T(2,128)S(1)} %copy-done.11, s32[2,128]{1,0:T(2,128)S(1)} %get-tuple-element.70.refs_2_, bf16[2064,128]{1,0:T(8,128)(2,1)S(1)} %copy-done.2, ...), custom_call_target="tpu_custom_call" | custom-call | flops 1 | bytes 1 | tf_op jit(solution)/shard_map/near1/pallas_call | solution.py:595
  58.8 0.7 collective-permute-start.8
  59.5 1.8 %collective-permute-start.10 = (bf16[80,128]{1,0:T(8,128)(2,1)S(1)}, bf16[80,128]{1,0:T(8,128)(2,1)S(1)}, u32[]{:S(2)}, u32[]{:S(2)}) collective-permute-start(bf16[80,128]{1,0:T(8,128)(2,1)S(1)} %climb1.1.own), channel_id=1, source_target_pairs={{0,8},{1,9},{2,10},{3,11},{4,12},{5,13},{6,14},{7,15},{8,0},{9,1},... | collective-permute-start | bytes 61448 | tf_op jit(solution)/shard_map/ppermute | solution.py:745
  61.3 1.1 %collective-permute-start.11 = (bf16[80,128]{1,0:T(8,128)(2,1)S(1)}, bf16[80,128]{1,0:T(8,128)(2,1)S(1)}, u32[]{:S(2)}, u32[]{:S(2)}) collective-permute-start(bf16[80,128]{1,0:T(8,128)(2,1)S(1)} %climb1.1.own), channel_id=1, source_target_pairs={{0,12},{1,13},{2,14},{3,15},{4,8},{5,9},{6,10},{7,11},{8,4},{9,5},... | collective-permute-start | bytes 61448 | tf_op jit(solution)/shard_map/ppermute | solution.py:745
  62.4 6.1 %near2.1 = (f32[2,256,128]{2,1,0:T(8,128)S(1)}, s32[2,128]{1,0:T(2,128)S(1)}) custom-call(s32[8,16]{1,0:T(8,128)S(1)} %fusion.11.refs_0_, bf16[2064,128]{1,0:T(8,128)(2,1)S(1)} %collective-permute-done.9.refs_1_.refs_7_, bf16[16,80,256]{2,1,0:T(8,128)(2,1)S(1)} %copy-done.1, ...), custom_call_target="tpu_custom_call" | custom-call | flops 1 | bytes 1 | tf_op jit(solution)/shard_map/near2/pallas_call | solution.py:595
  68.5 0.3 climb2.1
  68.9 2.5 %collective-permute-start.12 = (bf16[80,128]{1,0:T(8,128)(2,1)S(1)}, bf16[80,128]{1,0:T(8,128)(2,1)S(1)}, u32[]{:S(2)}, u32[]{:S(2)}) collective-permute-start(bf16[80,128]{1,0:T(8,128)(2,1)S(1)} %get-tuple-element.80), channel_id=1, source_target_pairs={{0,16},{1,17},{2,18},{3,19},{4,20},{5,21},{6,22},{7,23},{8,24},{9,... | collective-permute-start | bytes 61448 | tf_op jit(solution)/shard_map/ppermute | solution.py:745
  71.4 6.8 %near3.1 = (bf16[2,256,128]{2,1,0:T(8,128)(2,1)S(1)}, bf16[2,256,128]{2,1,0:T(8,128)(2,1)S(1)}, bf16[2,256,128]{2,1,0:T(8,128)(2,1)S(1)}, bf16[2,256,128]{2,1,0:T(8,128)(2,1)S(1)}) custom-call(s32[2,128]{1,0:T(2,128)S(1)} %copy-done.9, s32[2,128]{1,0:T(2,128)S(1)} %get-tuple-element.82.refs_1_, s32[2,128]{1,0:T(2,128)S(1)} %get-tuple-element.83.refs_2_, ...), custom_call_target="tpu_custom_call" | custom-call | flops 1 | bytes 1 | tf_op jit(solution)/shard_map/near3/pallas_call | solution.py:595
  78.3 0.1 collective-permute-start.15
  78.3 1.3 %collective-permute-start.16 = (bf16[2,256,128]{2,1,0:T(8,128)(2,1)S(1)}, bf16[2,256,128]{2,1,0:T(8,128)(2,1)S(1)}, u32[]{:S(2)}, u32[]{:S(2)}) collective-permute-start(bf16[2,256,128]{2,1,0:T(8,128)(2,1)S(1)} %get-tuple-element.92), channel_id=1, source_target_pairs={{0,8},{1,9},{2,10},{3,11},{4,12},{5,13},{6,14},{7,15},{8,0},{9,1},... | collective-permute-start | bytes 393224 | tf_op jit(solution)/shard_map/ppermute | solution.py:745
  79.7 2.2 %collective-permute-start.17 = (bf16[2,256,128]{2,1,0:T(8,128)(2,1)S(1)}, bf16[2,256,128]{2,1,0:T(8,128)(2,1)S(1)}, u32[]{:S(2)}, u32[]{:S(2)}) collective-permute-start(bf16[2,256,128]{2,1,0:T(8,128)(2,1)S(1)} %get-tuple-element.94), channel_id=1, source_target_pairs={{0,10},{1,11},{2,8},{3,9},{4,14},{5,15},{6,12},{7,13},{8,2},{9,3},... | collective-permute-start | bytes 393224 | tf_op jit(solution)/shard_map/ppermute | solution.py:745
  81.8 3.9 %top.1.refs_2_ = f32[2,256,128]{2,1,0:T(8,128)S(1)} custom-call(bf16[17,80,256]{2,1,0:T(8,128)(2,1)S(1)} %collective-permute-done.other.refs_5_.refs_7_.refs_3_.refs_0_, bf16[80,128]{1,0:T(8,128)(2,1)S(1)} %collective-permute-done.1.other.refs_1_, bf16[80,128]{1,0:T(8,128)(2,1)S(1)} %collective-permute-done.8.one.refs_2_, ...), custom_call_target="tpu_custom_call" | custom-call | flops 1 | bytes 1 | tf_op jit(solution)/shard_map/top/pallas_call | solution.py:695
  85.7 1.8 %collective-permute-done.17.refs_7_ = bf16[2,256,128]{2,1,0:T(8,128)(2,1)S(1)} collective-permute-done((bf16[2,256,128]{2,1,0:T(8,128)(2,1)S(1)}, bf16[2,256,128]{2,1,0:T(8,128)(2,1)S(1)}, u32[]{:S(2)}, u32[]{:S(2)}) %collective-permute-start.17) | collective-permute-done | bytes 131104 | tf_op jit(solution)/shard_map/ppermute | solution.py:745
  87.5 0.9 %last_sum.1 = f32[16,4096]{1,0:T(8,128)} custom-call(f32[256,128]{1,0:T(8,128)S(1)} %copy-done.6, f32[256,128]{1,0:T(8,128)S(1)} %copy-done.5, f32[2,256,128]{2,1,0:T(8,128)S(1)} %top.1.refs_2_, f32[16,1,256]{2,1,0:T(1,128)S(1)} %copy-done.8, bf16[2,256,128]{2,1,0:T(8,128)(2,1)S(1)} %get-tuple-element.86.refs_4_, ...), custom_call_target="tpu_custom_call" | custom-call | flops 1 | bytes 1 | tf_op jit(solution)/shard_map/last_sum/pallas_call | solution.py:732
  (47 shorter events, 0.3 us)
Async XLA Ops:
  10.5 15.5 %copy-start.3 = (bf16[5,256,128]{2,1,0:T(8,128)(2,1)S(1)}, bf16[5,256,128]{2,1,0:T(8,128)(2,1)}, u32[]{:S(2)}) copy-start(bf16[5,256,128]{2,1,0:T(8,128)(2,1)} %get-tuple-element.60.interps) | copy-start | bytes 983044
  10.5 15.5 %copy-start.7 = (s32[5,1,128]{2,1,0:T(1,128)S(1)}, s32[5,1,128]{2,1,0:T(1,128)}, u32[]{:S(2)}) copy-start(s32[5,1,128]{2,1,0:T(1,128)} %get-tuple-element.59.skels) | copy-start | bytes 7684
  10.5 15.5 %collective-permute-start = (bf16[17,80,256]{2,1,0:T(8,128)(2,1)}, bf16[17,80,256]{2,1,0:T(8,128)(2,1)S(1)}, u32[]{:S(2)}, u32[]{:S(2)}) collective-permute-start(bf16[17,80,256]{2,1,0:T(8,128)(2,1)} %get-tuple-element.58.own), channel_id=1, source_target_pairs={{0,1},{1,0},{2,3},{3,2},{4,5},{5,4},{6,7},{7,6},{8,9},{9,8},{10,11... | collective-permute-start | bytes 2088968 | tf_op jit(solution)/shard_map/ppermute | solution.py:745
  11.1 24.8 %collective-permute-start.3 = (bf16[2064,128]{1,0:T(8,128)(2,1)}, bf16[2064,128]{1,0:T(8,128)(2,1)S(1)}, u32[]{:S(2)}, u32[]{:S(2)}) collective-permute-start(bf16[2064,128]{1,0:T(8,128)(2,1)} %get-tuple-element.63.refs_2_.refs_3_.refs_4_), channel_id=1, source_target_pairs={{0,2},{1,3},{2,0},{3,1},{4,6},{5,7},{6,4},{7,5},{8,10},{9,11},{10,... | collective-permute-start | bytes 1585160 | tf_op jit(solution)/shard_map/ppermute | solution.py:745
  13.6 22.3 %collective-permute-start.4 = (bf16[16,80,256]{2,1,0:T(8,128)(2,1)}, bf16[16,80,256]{2,1,0:T(8,128)(2,1)S(1)}, u32[]{:S(2)}, u32[]{:S(2)}) collective-permute-start(bf16[16,80,256]{2,1,0:T(8,128)(2,1)} %get-tuple-element.66.refs_4_.refs_6_.refs_2_), channel_id=1, source_target_pairs={{0,4},{1,5},{2,6},{3,7},{4,0},{5,1},{6,2},{7,3},{8,12},{9,13},{10,... | collective-permute-start | bytes 1966088 | tf_op jit(solution)/shard_map/ppermute | solution.py:745
  15.1 31.7 %collective-permute-start.6 = (bf16[16,80,256]{2,1,0:T(8,128)(2,1)}, bf16[16,80,256]{2,1,0:T(8,128)(2,1)S(1)}, u32[]{:S(2)}, u32[]{:S(2)}) collective-permute-start(bf16[16,80,256]{2,1,0:T(8,128)(2,1)} %get-tuple-element.66.refs_4_.refs_6_.refs_2_), channel_id=1, source_target_pairs={{0,16},{1,17},{2,18},{3,19},{4,20},{5,21},{6,22},{7,23},{8,24},{9,... | collective-permute-start | bytes 1966088 | tf_op jit(solution)/shard_map/ppermute | solution.py:745
  17.7 29.1 %collective-permute-start.2 = (bf16[2064,128]{1,0:T(8,128)(2,1)}, bf16[2064,128]{1,0:T(8,128)(2,1)S(1)}, u32[]{:S(2)}, u32[]{:S(2)}) collective-permute-start(bf16[2064,128]{1,0:T(8,128)(2,1)} %get-tuple-element.63.refs_2_.refs_3_.refs_4_), channel_id=1, source_target_pairs={{0,8},{1,9},{2,10},{3,11},{4,12},{5,13},{6,14},{7,15},{8,0},{9,1},... | collective-permute-start | bytes 1585160 | tf_op jit(solution)/shard_map/ppermute | solution.py:745
  26.1 1.1 %copy-start.4 = (bf16[17,80,256]{2,1,0:T(8,128)(2,1)S(1)}, bf16[17,80,256]{2,1,0:T(8,128)(2,1)}, u32[]{:S(2)}) copy-start(bf16[17,80,256]{2,1,0:T(8,128)(2,1)} %get-tuple-element.58.own) | copy-start | bytes 2088964
  27.3 8.6 %copy-start.1 = (bf16[16,80,256]{2,1,0:T(8,128)(2,1)S(1)}, bf16[16,80,256]{2,1,0:T(8,128)(2,1)}, u32[]{:S(2)}) copy-start(bf16[16,80,256]{2,1,0:T(8,128)(2,1)} %get-tuple-element.66.refs_4_.refs_6_.refs_2_) | copy-start | bytes 1966084
  27.3 8.6 %copy-start.2 = (bf16[2064,128]{1,0:T(8,128)(2,1)S(1)}, bf16[2064,128]{1,0:T(8,128)(2,1)}, u32[]{:S(2)}) copy-start(bf16[2064,128]{1,0:T(8,128)(2,1)} %get-tuple-element.63.refs_2_.refs_3_.refs_4_) | copy-start | bytes 1585156
  27.3 8.6 %copy-start.10 = (s32[2,128]{1,0:T(2,128)S(1)}, s32[2,128]{1,0:T(2,128)}, u32[]{:S(2)}) copy-start(s32[2,128]{1,0:T(2,128)} %get-tuple-element.65.refs_1_) | copy-start | bytes 3076
  27.4 8.4 %collective-permute-start.1 = (bf16[80,128]{1,0:T(8,128)(2,1)S(1)}, bf16[80,128]{1,0:T(8,128)(2,1)S(1)}, u32[]{:S(2)}, u32[]{:S(2)}) collective-permute-start(bf16[80,128]{1,0:T(8,128)(2,1)S(1)} %climb0.1.own), channel_id=1, source_target_pairs={{0,2},{1,3},{2,0},{3,1},{4,6},{5,7},{6,4},{7,5},{8,10},{9,11},{10,... | collective-permute-start | bytes 61448 | tf_op jit(solution)/shard_map/ppermute | solution.py:745
  35.7 13.2 %copy-start.11 = (s32[2,128]{1,0:T(2,128)S(1)}, s32[2,128]{1,0:T(2,128)}, u32[]{:S(2)}) copy-start(s32[2,128]{1,0:T(2,128)} %get-tuple-element.69.refs_1_) | copy-start | bytes 3076
  42.5 5.4 %collective-permute-start.5 = (bf16[16,80,256]{2,1,0:T(8,128)(2,1)S(1)}, bf16[16,80,256]{2,1,0:T(8,128)(2,1)S(1)}, u32[]{:S(2)}, u32[]{:S(2)}) collective-permute-start(bf16[16,80,256]{2,1,0:T(8,128)(2,1)S(1)} %collective-permute-done.4.refs_6_.refs_8_.refs_4_), channel_id=1, source_target_pairs={{0,1},{1,0},{2,3},{3,2},{4,5},{5,4},{6,7},{7,6},{8,9},{9,8},{10,11... | collective-permute-start | bytes 1966088 | tf_op jit(solution)/shard_map/ppermute | solution.py:745
  46.8 2.1 %collective-permute-start.7 = (bf16[16,80,256]{2,1,0:T(8,128)(2,1)S(1)}, bf16[16,80,256]{2,1,0:T(8,128)(2,1)S(1)}, u32[]{:S(2)}, u32[]{:S(2)}) collective-permute-start(bf16[16,80,256]{2,1,0:T(8,128)(2,1)S(1)} %collective-permute-done.6.refs_10_.refs_6_), channel_id=1, source_target_pairs={{0,1},{1,0},{2,3},{3,2},{4,5},{5,4},{6,7},{7,6},{8,9},{9,8},{10,11... | collective-permute-start | bytes 1966088 | tf_op jit(solution)/shard_map/ppermute | solution.py:745
  46.8 15.5 %collective-permute-start.9 = (bf16[2064,128]{1,0:T(8,128)(2,1)S(1)}, bf16[2064,128]{1,0:T(8,128)(2,1)S(1)}, u32[]{:S(2)}, u32[]{:S(2)}) collective-permute-start(bf16[2064,128]{1,0:T(8,128)(2,1)S(1)} %collective-permute-done.2.refs_5_.refs_6_), channel_id=1, source_target_pairs={{0,2},{1,3},{2,0},{3,1},{4,6},{5,7},{6,4},{7,5},{8,10},{9,11},{10,... | collective-permute-start | bytes 1585160 | tf_op jit(solution)/shard_map/ppermute | solution.py:745
  47.4 21.4 %collective-permute-start.13 = (bf16[16,80,256]{2,1,0:T(8,128)(2,1)S(1)}, bf16[16,80,256]{2,1,0:T(8,128)(2,1)S(1)}, u32[]{:S(2)}, u32[]{:S(2)}) collective-permute-start(bf16[16,80,256]{2,1,0:T(8,128)(2,1)S(1)} %collective-permute-done.6.refs_10_.refs_6_), channel_id=1, source_target_pairs={{0,4},{1,5},{2,6},{3,7},{4,0},{5,1},{6,2},{7,3},{8,12},{9,13},{10,... | collective-permute-start | bytes 1966088 | tf_op jit(solution)/shard_map/ppermute | solution.py:745
  58.8 9.7 %collective-permute-start.8 = (bf16[80,128]{1,0:T(8,128)(2,1)S(1)}, bf16[80,128]{1,0:T(8,128)(2,1)S(1)}, u32[]{:S(2)}, u32[]{:S(2)}) collective-permute-start(bf16[80,128]{1,0:T(8,128)(2,1)S(1)} %climb1.1.own), channel_id=1, source_target_pairs={{0,4},{1,5},{2,6},{3,7},{4,0},{5,1},{6,2},{7,3},{8,12},{9,13},{10,... | collective-permute-start | bytes 61448 | tf_op jit(solution)/shard_map/ppermute | solution.py:745
  59.5 9.0 %collective-permute-start.10 = (bf16[80,128]{1,0:T(8,128)(2,1)S(1)}, bf16[80,128]{1,0:T(8,128)(2,1)S(1)}, u32[]{:S(2)}, u32[]{:S(2)}) collective-permute-start(bf16[80,128]{1,0:T(8,128)(2,1)S(1)} %climb1.1.own), channel_id=1, source_target_pairs={{0,8},{1,9},{2,10},{3,11},{4,12},{5,13},{6,14},{7,15},{8,0},{9,1},... | collective-permute-start | bytes 61448 | tf_op jit(solution)/shard_map/ppermute | solution.py:745
  61.3 7.2 %collective-permute-start.11 = (bf16[80,128]{1,0:T(8,128)(2,1)S(1)}, bf16[80,128]{1,0:T(8,128)(2,1)S(1)}, u32[]{:S(2)}, u32[]{:S(2)}) collective-permute-start(bf16[80,128]{1,0:T(8,128)(2,1)S(1)} %climb1.1.own), channel_id=1, source_target_pairs={{0,12},{1,13},{2,14},{3,15},{4,8},{5,9},{6,10},{7,11},{8,4},{9,5},... | collective-permute-start | bytes 61448 | tf_op jit(solution)/shard_map/ppermute | solution.py:745
  62.4 9.0 %copy-start.9 = (s32[2,128]{1,0:T(2,128)S(1)}, s32[2,128]{1,0:T(2,128)}, u32[]{:S(2)}) copy-start(s32[2,128]{1,0:T(2,128)} %get-tuple-element.81.refs_0_) | copy-start | bytes 3076
  68.8 2.6 %collective-permute-start.14 = (bf16[16,80,256]{2,1,0:T(8,128)(2,1)S(1)}, bf16[16,80,256]{2,1,0:T(8,128)(2,1)S(1)}, u32[]{:S(2)}, u32[]{:S(2)}) collective-permute-start(bf16[16,80,256]{2,1,0:T(8,128)(2,1)S(1)} %collective-permute-done.13.refs_8_), channel_id=1, source_target_pairs={{0,1},{1,0},{2,3},{3,2},{4,5},{5,4},{6,7},{7,6},{8,9},{9,8},{10,11... | collective-permute-start | bytes 1966088 | tf_op jit(solution)/shard_map/ppermute | solution.py:745
  68.9 9.3 %collective-permute-start.12 = (bf16[80,128]{1,0:T(8,128)(2,1)S(1)}, bf16[80,128]{1,0:T(8,128)(2,1)S(1)}, u32[]{:S(2)}, u32[]{:S(2)}) collective-permute-start(bf16[80,128]{1,0:T(8,128)(2,1)S(1)} %get-tuple-element.80), channel_id=1, source_target_pairs={{0,16},{1,17},{2,18},{3,19},{4,20},{5,21},{6,22},{7,23},{8,24},{9,... | collective-permute-start | bytes 61448 | tf_op jit(solution)/shard_map/ppermute | solution.py:745
  71.4 10.4 %copy-start = (bf16[16,256,128]{2,1,0:T(8,128)(2,1)S(1)}, bf16[16,256,128]{2,1,0:T(8,128)(2,1)}, u32[]{:S(2)}) copy-start(bf16[16,256,128]{2,1,0:T(8,128)(2,1)} %get-tuple-element.88.refs_5_.refs_4_) | copy-start | bytes 3145732
  78.2 9.3 %copy-start.5 = (f32[256,128]{1,0:T(8,128)S(1)}, f32[256,128]{1,0:T(8,128)}, u32[]{:S(2)}) copy-start(f32[256,128]{1,0:T(8,128)} %self_and_far1.1.refs_1_) | copy-start | bytes 393220
  78.2 9.3 %copy-start.6 = (f32[256,128]{1,0:T(8,128)S(1)}, f32[256,128]{1,0:T(8,128)}, u32[]{:S(2)}) copy-start(f32[256,128]{1,0:T(8,128)} %get-tuple-element.56.refs_0_) | copy-start | bytes 393220
  78.3 9.3 %copy-start.8 = (f32[16,1,256]{2,1,0:T(1,128)S(1)}, f32[16,1,256]{2,1,0:T(1,128)}, u32[]{:S(2)}) copy-start(f32[16,1,256]{2,1,0:T(1,128)} %get-tuple-element.51.refs_3_) | copy-start | bytes 49156
  78.3 7.4 %collective-permute-start.15 = (bf16[2,256,128]{2,1,0:T(8,128)(2,1)S(1)}, bf16[2,256,128]{2,1,0:T(8,128)(2,1)S(1)}, u32[]{:S(2)}, u32[]{:S(2)}) collective-permute-start(bf16[2,256,128]{2,1,0:T(8,128)(2,1)S(1)} %get-tuple-element.90), channel_id=1, source_target_pairs={{0,2},{1,3},{2,0},{3,1},{4,6},{5,7},{6,4},{7,5},{8,10},{9,11},{10,... | collective-permute-start | bytes 393224 | tf_op jit(solution)/shard_map/ppermute | solution.py:745
  78.3 7.4 %collective-permute-start.16 = (bf16[2,256,128]{2,1,0:T(8,128)(2,1)S(1)}, bf16[2,256,128]{2,1,0:T(8,128)(2,1)S(1)}, u32[]{:S(2)}, u32[]{:S(2)}) collective-permute-start(bf16[2,256,128]{2,1,0:T(8,128)(2,1)S(1)} %get-tuple-element.92), channel_id=1, source_target_pairs={{0,8},{1,9},{2,10},{3,11},{4,12},{5,13},{6,14},{7,15},{8,0},{9,1},... | collective-permute-start | bytes 393224 | tf_op jit(solution)/shard_map/ppermute | solution.py:745
  79.7 7.9 %collective-permute-start.17 = (bf16[2,256,128]{2,1,0:T(8,128)(2,1)S(1)}, bf16[2,256,128]{2,1,0:T(8,128)(2,1)S(1)}, u32[]{:S(2)}, u32[]{:S(2)}) collective-permute-start(bf16[2,256,128]{2,1,0:T(8,128)(2,1)S(1)} %get-tuple-element.94), channel_id=1, source_target_pairs={{0,10},{1,11},{2,8},{3,9},{4,14},{5,15},{6,12},{7,13},{8,2},{9,3},... | collective-permute-start | bytes 393224 | tf_op jit(solution)/shard_map/ppermute | solution.py:745
